TPU v7x, 32 devices: a whole 2x2x4 slice. The times are simulated.
32 devices in a mesh: groups: 2 (over x), adapter: 4 (over y, core), tensor: 4 (over z).
Axes of the slice: x: 2, y: 2, z: 4, core: 2. Of those that a mesh axis runs over, the one named last changes fastest.
Arguments:
- tokens: bfloat16 [4096, 8192], P(('groups', 'adapter'), 'tensor'), parts along dimension 0, may hold values from -6 to 6
- queries: bfloat16 [4096, 8192], P(('groups', 'adapter'), 'tensor'), parts along dimension 0, may hold values from -24 to 24
- kv_cache: bfloat16 [4096, 16, 2048], P(('groups', 'adapter'), None, 'tensor'), parts along dimension 0, may hold values from -24 to 24
- kv_lengths: int32 [4096], P(('groups', 'adapter')), parts along dimension 0, may hold values from 2 to 16, as said below
- variant_ids: int32 [4096, 1], P(('groups', 'adapter')), parts along dimension 0, may hold values from 0 to 7; in each aligned block of 512 rows (0 to 511, 512 to 1023, ...) at most 160 rows name the same one
- base_weight: bfloat16 [8192, 2048], P('tensor'), may hold values from -0.0625 to 0.0625
- delta_down: bfloat16 [8, 8192, 256], P('adapter', 'tensor'), may hold values from -0.0625 to 0.0625
- delta_up: bfloat16 [8, 256, 2048], P('adapter', None, 'tensor'), may hold values from -0.375 to 0.375
Outputs:
- fresh_kv: bfloat16 [4096, 2048], P(('groups', 'adapter'), 'tensor'), parts along dimension 0
- attended: bfloat16 [4096, 8192], P(('groups', 'adapter'), 'tensor'), parts along dimension 0
There are 2 independent parts, one for each index of `groups`. A program takes and returns all parts, laid end to end along the dimension named above; an argument that names none is the same for every part. Nothing has to cross between parts.
Inputs may be any that keep to these rules, and one draw needn't show every extreme that they name: `variant_ids`: in each aligned block of 512 requests (the requests of one index of adapter) no variant appears more than 160 times, and some variant appears exactly 160 times in some block. `kv_lengths`: every request has at least two cached positions; the first request has 16.
All inputs are finite; a program needn't handle non-finite values.
Results may differ from a plain program's by a relative error of at most 0.006.
Values may be sent and summed in bfloat16 or wider, within the bound.
No kernel may reach another device: no remote copies, remote signals or barrier semaphores. Data moves between devices by JAX's collectives and lax.ppermute only.
A program may use at most 192 MiB of HBM per device.

v0:
```python
import jax
import jax.numpy as jnp
from jax import lax
from jax.sharding import PartitionSpec as P

HEAD = 128


def slot_table(variant_list, variant_count, capacity):
    row_count = variant_list.shape[0]
    one_hot = (variant_list[:, None] == jnp.arange(variant_count, dtype=jnp.int32)[None, :]).astype(
        jnp.int32
    )
    ranking = jnp.cumsum(one_hot, axis=0)
    slot_in = jnp.sum(ranking * one_hot, axis=1) - 1
    flat_slot = variant_list * capacity + slot_in
    row_of = jnp.full((variant_count * capacity,), row_count, jnp.int32)
    row_of = row_of.at[flat_slot].set(jnp.arange(row_count, dtype=jnp.int32))
    return (flat_slot, row_of)


def attend(queries, kv_cache, kv_lengths, fresh_rows):
    row_count = queries.shape[0]
    positions = kv_cache.shape[1]
    heads_local = queries.shape[1] // HEAD
    kv_local = fresh_rows.shape[1] // (2 * HEAD)
    group = heads_local // kv_local
    query_four = queries.reshape(row_count, kv_local, group, HEAD)
    cache_five = kv_cache.reshape(row_count, positions, kv_local, 2, HEAD)
    fresh_four = fresh_rows.reshape(row_count, kv_local, 2, HEAD)
    score_scale = HEAD ** (-0.5)
    scores = (
        jnp.einsum(
            "rgqd,rpgd->rgqp",
            query_four,
            cache_five[:, :, :, 0],
            preferred_element_type=jnp.float32,
        )
        * score_scale
    )
    own_score = (
        jnp.einsum(
            "rgqd,rgd->rgq", query_four, fresh_four[:, :, 0], preferred_element_type=jnp.float32
        )
        * score_scale
    )
    visible = (jnp.arange(positions, dtype=jnp.int32)[None, :] < kv_lengths[:, None])[
        :, None, None, :
    ]
    scores = jnp.where(visible, scores, jnp.float32(-1e30))
    largest = jnp.maximum(jnp.max(scores, axis=-1), own_score)
    weights = jnp.where(visible, jnp.exp(scores - largest[..., None]), jnp.float32(0.0))
    own_weight = jnp.exp(own_score - largest)
    denominator = jnp.sum(weights, axis=-1) + own_weight
    probs = (weights / denominator[..., None]).astype(jnp.bfloat16)
    own_prob = (own_weight / denominator).astype(jnp.bfloat16)
    mixed = jnp.einsum(
        "rgqp,rpgd->rgqd", probs, cache_five[:, :, :, 1], preferred_element_type=jnp.float32
    )
    mixed = mixed + own_prob.astype(jnp.float32)[..., None] * fresh_four[:, :, None, 1].astype(
        jnp.float32
    )
    return mixed.astype(jnp.bfloat16).reshape(row_count, heads_local * HEAD)


def local(tokens, queries, kv_cache, kv_lengths, variant_ids, base_weight, delta_down, delta_up):
    row_count = tokens.shape[0]
    local_width = tokens.shape[1]
    owners = lax.axis_size("adapter")
    var_local = delta_down.shape[0]
    variants = var_local * owners
    capacity = row_count * 5 // (2 * variants)
    partial_value = jnp.dot(tokens, base_weight, preferred_element_type=jnp.float32)
    base_part = lax.psum_scatter(partial_value, "tensor", scatter_dimension=1, tiled=True)
    column_width = base_part.shape[1]
    flat_slot, row_of = slot_table(variant_ids[:, 0], variants, capacity)
    padded = jnp.concatenate([tokens, jnp.zeros((1, local_width), jnp.bfloat16)], axis=0)
    slotted = padded[row_of].reshape(variants, capacity, local_width)
    product_term = jnp.einsum(
        "vmd,vdr->vmr",
        slotted,
        lax.all_gather(delta_down, "adapter", axis=0, tiled=True),
        preferred_element_type=jnp.float32,
    )
    partial_rank = product_term
    lowrank = lax.psum(partial_rank, "tensor").astype(jnp.bfloat16)
    product_term = jnp.einsum(
        "vmr,vrc->vmc",
        lowrank,
        lax.all_gather(delta_up, "adapter", axis=0, tiled=True),
        preferred_element_type=jnp.float32,
    )
    change = product_term.astype(jnp.bfloat16).reshape(variants * capacity, column_width)
    delta_rows = change[flat_slot]
    fresh_rows = (base_part + delta_rows.astype(jnp.float32)).astype(jnp.bfloat16)
    attended = attend(queries, kv_cache, kv_lengths, fresh_rows)
    return (fresh_rows, attended)


def solution(mesh):
    return jax.shard_map(
        local,
        mesh=mesh,
        in_specs=(
            P(("groups", "adapter"), "tensor"),
            P(("groups", "adapter"), "tensor"),
            P(("groups", "adapter"), None, "tensor"),
            P(("groups", "adapter")),
            P(("groups", "adapter"), None),
            P("tensor", None),
            P("adapter", "tensor", None),
            P("adapter", None, "tensor"),
        ),
        out_specs=(P(("groups", "adapter"), "tensor"), P(("groups", "adapter"), "tensor")),
        check_vma=False,
    )
```

profile of v0, /device:TPU:0, one launch (start us, length us, event | category | flops | bytes accessed | tf_op | source)
XLA Modules:
  0.0 185.7 jit_solution(14659028501090028253)
XLA Ops:
  8.0 0.7 all-gather.3.cloned.1.call-update
  8.8 0.7 all-gather.5.cloned.1.call-update
  9.5 10.5 %fusion.29 = f32[512,2048]{1,0:T(8,128)} fusion(bf16[512,2048]{1,0:T(8,128)(2,1)} %param.8, bf16[2048,2048]{1,0:T(8,128)(2,1)} %param.13), kind=kOutput, calls=%fused_computation.52 | convolution fusion | flops 4294967296 | bytes 14680064 | tf_op jit(solution)/shard_map/dot_general | solution.py:73
  20.1 2.0 %concatenate.3 = bf16[513,2048]{1,0:T(8,128)(2,1)S(1)} pad(bf16[512,2048]{1,0:T(8,128)(2,1)} %param.8, bf16[]{:T(256)} %constant.11.clone.1), padding=0_1x0_0 | pad | bytes 4198402 | tf_op jit(solution)/shard_map/concatenate | solution.py:77
  22.1 1.1 reduce-window.6
  23.3 0.2 slice_reduce_fusion
  23.5 14.2 %copy.25 = bf16[512,16,512]{0,2,1:T(8,128)(2,1)} copy(bf16[512,16,512]{2,1,0:T(8,128)(2,1)} %param.10) | data formatting | bytes 16777216 | tf_op args[2]
  37.8 6.0 %fusion.27 = (bf16[512,16,2,1,128]{0,4,3,2,1:T(8,128)(2,1)}, bf16[512,16,2,1,128]{0,4,3,2,1:T(8,128)(2,1)}) fusion(bf16[512,16,2,2,128]{0,4,3,2,1:T(8,128)(2,1)} %bitcast.60), kind=kLoop, calls=%fused_computation.50 | loop fusion | bytes 16777216 | tf_op jit(solution)/shard_map/slice | solution.py:36
  43.8 8.1 %copy.38 = bf16[512,16,2,1,128]{4,1,2,0,3:T(8,128)(2,1)} copy(bf16[512,16,2,1,128]{0,4,3,2,1:T(8,128)(2,1)} %get-tuple-element.3) | data formatting | bytes 8388608
  52.0 3.5 %copy.39 = bf16[64,8,16,128]{3,2,1,0:T(8,128)(2,1)} copy(bf16[64,8,16,128]{3,1,2,0:T(8,128)(2,1)} %bitcast.65) | data formatting | bytes 4194304
  55.5 8.2 %copy.36 = bf16[512,16,2,1,128]{4,1,2,0,3:T(8,128)(2,1)} copy(bf16[512,16,2,1,128]{0,4,3,2,1:T(8,128)(2,1)} %get-tuple-element.2) | data formatting | bytes 8388608
  63.7 0.1 iota_compare_fusion
  63.9 7.5 %fusion.4 = (f32[512,2,8]{2,1,0:T(2,128)S(1)}, f32[512,2,8,16]{3,2,1,0:T(8,128)}) fusion(pred[512,16]{1,0:T(8,128)(4,1)S(1)} %iota_compare_fusion, bf16[512,2,8,128]{3,2,1,0:T(8,128)(2,1)} %bitcast.63, bf16[512,16,2,1,128]{4,1,2,0,3:T(8,128)(2,1)} %copy.36), kind=kOutput, calls=%fused_computation.11 | convolution fusion | flops 33939456 | bytes 6856704 | tf_op jit(solution)/shard_map/rgqd,rpgd->rgqp/dot_general | solution.py:33
  71.3 0.2 copy.28
  71.6 2.6 %scatter_custom_fusion = s32[1280]{0:T(1024)S(1)} fusion(s32[512]{0:T(512)S(1)} %bitcast.72, s32[512]{0:T(512)S(1)} %iota.18, s32[]{:T(128)} %constant.12.clone.1), kind=kCustom, calls=%fused_computation.44 | custom fusion | bytes 5124 | tf_op jit(solution)/shard_map/scatter | solution.py:18
  74.3 6.3 %gather_fusion = bf16[1280,2048]{1,0:T(8,128)(2,1)} fusion(bf16[513,2048]{1,0:T(8,128)(2,1)S(1)} %concatenate.3, s32[2048]{0:T(1024)S(1)} %pad_clamp_fusion), kind=kCustom, calls=%fused_computation | custom fusion | bytes 10490880 | tf_op jit(solution)/shard_map/gather | solution.py:78
  80.6 6.7 %fusion.30 = f32[8,160,256]{2,1,0:T(8,128)S(1)} fusion(bf16[8,160,2048]{2,1,0:T(8,128)(2,1)} %bitcast.61, bf16[8,2048,256]{2,1,0:T(8,128)(2,1)} %all-gather.3.cloned.1.call-done), kind=kOutput, calls=%fused_computation.53 | convolution fusion | flops 1342177280 | bytes 14942208 | tf_op jit(solution)/shard_map/vmd,vdr->vmr/dot_general | solution.py:79
  87.3 56.8 %all-reduce.2 = bf16[8,160,256]{2,1,0:T(8,128)(2,1)S(1)} all-reduce(f32[8,160,256]{2,1,0:T(8,128)S(1)} %fusion.30), channel_id=1, replica_groups=mesh['groups'=2,'adapter'=4,'tensor'=4] {'tensor'}, use_global_device_ids=true, to_apply=%region_5.6 | all-reduce | flops 327680 | bytes 1966080 | tf_op jit(solution)/shard_map/psum | solution.py:86
  144.2 2.1 %convolution_convert_fusion = bf16[8,160,512]{2,1,0:T(8,128)(2,1)S(1)} fusion(bf16[8,256,512]{2,1,0:T(8,128)(2,1)} %all-gather.5.cloned.1.call-done, bf16[8,160,256]{2,1,0:T(8,128)(2,1)S(1)} %all-reduce.2), kind=kOutput, calls=%fused_computation.20 | convolution fusion | flops 336199680 | bytes 4063232 | tf_op jit(solution)/shard_map/vmr,vrc->vmc/dot_general | solution.py:87
  146.3 2.0 %gather_fusion.1 = bf16[512,512]{1,0:T(8,128)(2,1)S(1)} fusion(bf16[1280,512]{1,0:T(8,128)(2,1)S(1)} %bitcast.62, s32[1024]{0:T(1024)S(1)} %pad_clamp_fusion.1), kind=kCustom, calls=%fused_computation.1 | custom fusion | bytes 1050624 | tf_op jit(solution)/shard_map/gather | solution.py:94
  148.3 1.5 add_convert_fusion.1
  149.8 0.1 reshape.72
  150.0 1.5 fusion.28
  151.5 1.2 fusion.15
  152.8 0.6 copy.35
  153.4 0.2 copy.29
  153.6 15.7 %fusion.5 = f32[512,2,8]{2,1,0:T(2,128)S(1)} fusion(f32[512,2,8,16]{3,2,1,0:T(8,128)} %get-tuple-element.9, f32[512,2,8]{2,1,0:T(2,128)S(1)} %copy.29, pred[512,16]{1,0:T(8,128)(4,1)S(1)} %iota_compare_fusion), kind=kLoop, calls=%fused_computation.12 | loop fusion | flops 647168 | bytes 598016 | tf_op jit(solution)/shard_map/reduce_sum | solution.py:54
  169.3 0.2 copy.30
  169.5 0.2 copy.33
  169.8 0.2 copy.31
  170.0 6.4 %add_convert_fusion = bf16[512,2,8,128]{3,2,1,0:T(8,128)(2,1)S(1)} fusion(bf16[512,16,2,1,128]{4,1,2,0,3:T(8,128)(2,1)} %copy.38, f32[512,2,8,16]{3,2,1,0:T(8,128)} %get-tuple-element.9, f32[512,2,128]{2,1,0:T(2,128)S(1)} %bitcast.68, f32[512,2,8]{2,1,0:T(2,128)S(1)} %copy.33, f32[512,2,8]{2,1,0:T(2,128)S(1)} %copy.31, f32[512,2,8]{2,1,0:T(2,128)S(1)} %copy.29, ...), kind=kOutput, calls=%fused_computation.7 | convolution fusion | flops 37486592 | bytes 7446528 | tf_op jit(solution)/shard_map/rgqp,rpgd->rgqd/dot_general | solution.py:57
  176.4 1.9 %copy.45 = bf16[64,8,16,128]{3,1,2,0:T(8,128)(2,1)} copy(bf16[64,8,16,128]{3,2,1,0:T(8,128)(2,1)S(1)} %bitcast.67) | data formatting | bytes 4194304
  (33 shorter events, 0.5 us)
Async XLA Ops:
  8.0 72.6 %all-gather.3.cloned.1.call-start = ((), (), s32[]{:S(2)}) async-start(), calls=%async_computation.2 | async-start | bytes 10485760 | tf_op jit(solution)/shard_map/all_gather | solution.py:82
  8.7 135.4 %all-gather.5.cloned.1.call-start = ((), (), s32[]{:S(2)}) async-start(), calls=%async_computation.3 | async-start | bytes 2621440 | tf_op jit(solution)/shard_map/all_gather | solution.py:90
  9.5 138.8 %reduce-scatter.2.cloned.1.call-start = ((), (), s32[]{:S(2)}) async-start(), calls=%async_computation.1 | async-start | bytes 5242880 | tf_op jit(solution)/shard_map/reduce_scatter | solution.py:74
  20.0 2.1 %copy-start.3 = (s32[512,1]{0,1:T(1,128)S(1)}, s32[512,1]{0,1:T(1,128)}, u32[]{:S(2)}) copy-start(s32[512,1]{0,1:T(1,128)} %param.12) | copy-start | bytes 6148
  23.5 14.2 %copy-start.4 = (s32[8,5]{0,1:T(8,128)}, s32[8,5]{0,1:T(8,128)S(1)}, u32[]{:S(2)}) copy-start(s32[8,5]{0,1:T(8,128)S(1)} %reduce-window.9) | copy-start | bytes 484
  55.5 8.2 %copy-start.5 = (s32[512]{0:T(512)S(1)}, s32[512]{0:T(512)}, u32[]{:S(2)}) copy-start(s32[512]{0:T(512)} %param.11) | copy-start | bytes 6148
  63.8 7.7 %slice-start = ((s32[8,5]{0,1:T(8,128)}), s32[8,4]{0,1:T(4,128)S(1)}, s32[]{:S(2)}) async-start(s32[8,5]{0,1:T(8,128)} %copy-done.4), calls=%async_computation.4 | async-start | bytes 4096 | tf_op jit(solution)/shard_map/slice.1
  148.3 3.3 %copy-start = (bf16[64,8,16,128]{3,2,1,0:T(8,128)(2,1)S(1)}, bf16[64,8,16,128]{3,2,1,0:T(8,128)(2,1)}, u32[]{:S(2)}) copy-start(bf16[64,8,16,128]{3,2,1,0:T(8,128)(2,1)} %copy.39) | copy-start | bytes 6291460
  149.8 3.5 %copy-start.1 = (bf16[512,512]{1,0:T(8,128)(2,1)}, bf16[512,512]{1,0:T(8,128)(2,1)S(1)}, u32[]{:S(2)}) copy-start(bf16[512,512]{1,0:T(8,128)(2,1)S(1)} %add_convert_fusion.1) | copy-start | bytes 1572868
  152.8 17.2 %copy-start.2 = (f32[512,2,1,128]{3,2,1,0:T(1,128)S(1)}, f32[512,2,1,128]{3,2,1,0:T(1,128)}, u32[]{:S(2)}) copy-start(f32[512,2,1,128]{3,2,1,0:T(1,128)} %get-tuple-element.5) | copy-start | bytes 1572868
Sparse Core Ops, SparseCore 0:
  10.5 60.9 all-gather.2
  73.1 22.6 all-gather.4
Sparse Core Ops, SparseCore 1:
  20.1 82.9 reduce-scatter.1
where the time goes:
time: 187 us; the launch traced here: 186 us
  local copies, waits for them, and re-layouts  57 us (30%)
  blocking collectives  56.8 us (30%)
  matrix products  34.4 us (18%)
  other arithmetic  20.2 us (11%)
  between operations  15.7 us (8%)
    psum x1, blocking collectives, local(): lowrank = lax.psum(partial_rank, 'tensor').astype(jnp.bfloat16)  56.8 us
    unnamed x18, local copies, waits for them, and re-layouts  36.1 us
    reduce_sum x1, other arithmetic, attend(): denominator = jnp.sum(weights, axis=-1) + own_weight  15.7 us
    dot_general x1, matrix products, local(): jnp.dot(tokens, base_weight, preferred_element_type=jnp.float32)  10.5 us
    dot_general x1, matrix products, attend(): jnp.einsum('rgqd,rpgd->rgqp', query_four, cache_five[:, :, :, 0], preferr...  7.49 us
    dot_general x1, matrix products, local(): jnp.einsum('vmd,vdr->vmr', slotted, lax.all_gather(delta_down, 'adapter',...  6.71 us
    dot_general x1, matrix products, attend(): jnp.einsum('rgqp,rpgd->rgqd', probs, cache_five[:, :, :, 1], preferred_el...  6.37 us
    gather x1, local copies, waits for them, and re-layouts, local(): slotted = padded[row_of].reshape(variants, capacity, local_width)  6.26 us
  transfers between devices with their start and end apart: 3, of which 0 were waited for; matrix products, arithmetic and copies ran while one was open for 44% of the time, Pallas kernels for 0%

commit v1 on v0

v1 whole, which is shorter than its diff:
```python
import functools

import jax
import jax.numpy as jnp
from jax import lax
from jax.experimental import pallas as pl
from jax.experimental.pallas import tpu as pltpu
from jax.sharding import PartitionSpec as P

HEAD = 128
BF16 = jnp.bfloat16
F32 = jnp.float32


def params(mib):
    return pltpu.CompilerParams(vmem_limit_bytes=mib << 20)


def cost(flops, bytes_accessed):
    return pl.CostEstimate(flops=flops, bytes_accessed=bytes_accessed, transcendentals=0)


def swap(value, axis, bit):
    return lax.ppermute(value, axis, [(i, i ^ bit) for i in range(lax.axis_size(axis))])


def project_kernel(count, steps, shards_ref, x_ref, w_ref, *outs):
    del shards_ref
    step = pl.program_id(0)
    result = jnp.dot(x_ref[...], w_ref[...], preferred_element_type=F32).astype(BF16)
    for i in range(count):

        @pl.when(step // steps == i)
        def _(i=i):
            outs[i][...] = result


def project(tokens, weight, shards, width):
    rows, depth = tokens.shape
    count = len(shards)
    block = min(width, 256)
    steps = width // block

    def out_map(i, step, shards_ref):
        return (0, jnp.clip(step - i * steps, 0, steps - 1))

    return pl.pallas_call(
        functools.partial(project_kernel, count, steps),
        out_shape=[jax.ShapeDtypeStruct((rows, width), BF16)] * count,
        grid_spec=pltpu.PrefetchScalarGridSpec(
            num_scalar_prefetch=1,
            grid=(count * steps,),
            in_specs=[
                pl.BlockSpec((rows, depth), lambda step, shards_ref: (0, 0)),
                pl.BlockSpec(
                    (depth, block),
                    lambda step, shards_ref: (0, shards_ref[step // steps] * steps + step % steps),
                ),
            ],
            out_specs=[
                pl.BlockSpec((rows, block), functools.partial(out_map, i)) for i in range(count)
            ],
        ),
        compiler_params=params(40),
        cost_estimate=cost(
            2 * rows * depth * width * count, 2 * (rows * depth + (rows + depth) * width * count)
        ),
        name="project",
    )(jnp.stack(shards).astype(jnp.int32), tokens, weight)


def codes_kernel(sizes, steps, has_start, ids_ref, variant_ref, x_ref, *refs):
    weights = refs[: len(sizes)]
    start_ref = refs[len(sizes)] if has_start else None
    out_ref, total = refs[-2:]
    step = pl.program_id(0)
    width = out_ref.shape[1]
    x = x_ref[...]

    @pl.when(step == 0)
    def _():
        total[...] = jnp.zeros_like(total)

    flat = [w.at[j] for w, size in zip(weights, sizes) for j in range(size)]
    pair = max(1, 256 // width)
    for first in range(0, len(flat), pair):
        group = flat[first : first + pair]
        w = jnp.concatenate([g[...] for g in group], axis=1)
        columns = pl.ds(first * width, len(group) * width)
        total[:, columns] += jnp.dot(x, w, preferred_element_type=F32)

    @pl.when(step == steps - 1)
    def _():
        kept = start_ref[...] if has_start else jnp.zeros(out_ref.shape, F32)
        for i in range(len(flat)):
            mine = variant_ref[...] == ids_ref[i]
            kept = jnp.where(mine, total[:, i * width : (i + 1) * width], kept)
        out_ref[...] = kept.astype(out_ref.dtype)


def codes(tokens, variant_ids, weights, ids, start, start_at, dtype):
    rows, depth = tokens.shape
    width = weights[0].shape[2]
    sizes = [w.shape[0] for w in weights]
    block = min(depth, 512)
    steps = depth // block
    operands = [variant_ids, tokens] + list(weights)
    in_specs = [
        pl.BlockSpec((rows, 1), lambda k, ids_ref: (0, 0)),
        pl.BlockSpec((rows, block), lambda k, ids_ref: (0, k)),
    ] + [pl.BlockSpec((m, block, width), lambda k, ids_ref: (0, k, 0)) for m in sizes]
    if start is not None:
        operands.append(start)
        in_specs.append(pl.BlockSpec((rows, width), lambda k, ids_ref: (0, start_at)))
    return pl.pallas_call(
        functools.partial(codes_kernel, sizes, steps, start is not None),
        out_shape=jax.ShapeDtypeStruct((rows, width), dtype),
        grid_spec=pltpu.PrefetchScalarGridSpec(
            num_scalar_prefetch=1,
            grid=(steps,),
            in_specs=in_specs,
            out_specs=pl.BlockSpec((rows, width), lambda k, ids_ref: (0, 0)),
            scratch_shapes=[pltpu.VMEM((rows, sum(sizes) * width), F32)],
        ),
        compiler_params=params(48),
        cost_estimate=cost(
            2 * rows * depth * width * sum(sizes), 2 * depth * (rows + width * sum(sizes))
        ),
        name="codes",
    )(ids, *operands)


def cached_kernel(positions, group, len_ref, q_ref, kv_ref, out_ref, lse_ref):
    rows = q_ref.shape[0]
    kv_local = kv_ref.shape[2] // (2 * HEAD)
    scale = HEAD ** (-0.5)
    near = 128 // positions
    lane = lax.broadcasted_iota(jnp.int32, (near, 128), 1)
    sublane = lax.broadcasted_iota(jnp.int32, (near, 128), 0)
    same = lane // positions == sublane
    at = lane % positions
    ones = jnp.ones((128, HEAD), BF16)

    for base in range(0, rows, 2 * near):
        here = pl.ds(base, 2 * near)
        seen = [same & (at < len_ref[pl.ds(base + half * near, near), :]) for half in range(2)]
        table = [jnp.zeros((near, 128), F32) for _ in range(2)]
        for g in range(kv_local):
            at_key, at_value = 2 * g * HEAD, (2 * g + 1) * HEAD
            keys = kv_ref[here, :, at_key : at_key + HEAD].reshape(256, HEAD)
            values = kv_ref[here, :, at_value : at_value + HEAD].reshape(256, HEAD)
            query = jnp.concatenate(
                [
                    q_ref[here, (g * group + h) * HEAD : (g * group + h + 1) * HEAD]
                    for h in range(group)
                ],
                axis=0,
            )
            scores = lax.dot_general(
                query, keys, (((1,), (1,)), ((), ())), preferred_element_type=F32
            ).reshape(group, 2, near, 256)
            results = []
            for half in range(2):
                own = scores[:, half, :, half * 128 : (half + 1) * 128] * scale
                own = jnp.where(seen[half][None], own, jnp.float32(-1e30))
                largest = jnp.max(own, axis=-1, keepdims=True)
                weight = jnp.exp(own - largest).astype(BF16).reshape(group * near, 128)
                value = jnp.concatenate([values[half * 128 : (half + 1) * 128], ones], axis=1)
                mixed = jnp.dot(weight, value, preferred_element_type=F32)
                total = mixed[:, HEAD:]
                results.append((mixed[:, :HEAD] / total).reshape(group, near, HEAD))
                lse = largest + jnp.log(total).reshape(group, near, 128)
                for h in range(group):
                    table[half] = jnp.where(lane == g * group + h, lse[h], table[half])
            both = jnp.stack(results, axis=1).reshape(group, 2 * near, HEAD).astype(BF16)
            for h in range(group):
                out_ref[here, (g * group + h) * HEAD : (g * group + h + 1) * HEAD] = both[h]
        for half in range(2):
            lse_ref[pl.ds(base + half * near, near), :] = table[half]


def cached(queries, kv_cache, lengths):
    rows, features = queries.shape
    positions, width = kv_cache.shape[1:]
    group = features * 2 // width
    block = 64
    return pl.pallas_call(
        functools.partial(cached_kernel, positions, group),
        out_shape=[
            jax.ShapeDtypeStruct((rows, features), BF16),
            jax.ShapeDtypeStruct((rows, 128), F32),
        ],
        grid=(rows // block,),
        in_specs=[
            pl.BlockSpec((block, 1), lambda i: (i, 0)),
            pl.BlockSpec((block, features), lambda i: (i, 0)),
            pl.BlockSpec((block, positions, width), lambda i: (i, 0, 0)),
        ],
        out_specs=[
            pl.BlockSpec((block, features), lambda i: (i, 0)),
            pl.BlockSpec((block, 128), lambda i: (i, 0)),
        ],
        compiler_params=params(40),
        cost_estimate=cost(
            2 * rows * features * 1024, 2 * rows * (2 * features + positions * width)
        ),
        name="cached",
    )(lengths, queries, kv_cache)


def finish_kernel(counts, group, ids_ref, variant_ref, q_ref, out1_ref, lse_ref, *refs):
    terms, codes_a, codes_b, ups = counts
    refs = list(refs)
    take = lambda n: [refs.pop(0) for _ in range(n)]
    base_refs, a_refs, b_refs, up_refs = take(terms), take(codes_a), take(codes_b), take(len(ups))
    fresh_ref, attended_ref = refs
    variant = variant_ref[...]

    def total(parts):
        result = parts[0][...].astype(F32)
        for part in parts[1:]:
            result = result + part[...].astype(F32)
        return result

    code = jnp.concatenate([total(a_refs).astype(BF16), total(b_refs).astype(BF16)], axis=1)
    change = jnp.zeros(fresh_ref.shape, F32)
    at = 0
    for up_ref, size in zip(up_refs, ups):
        for j in range(size):
            mine = jnp.where(variant == ids_ref[at], code, jnp.zeros_like(code))
            change = change + jnp.dot(mine, up_ref[j], preferred_element_type=F32)
            at += 1
    fresh = (total(base_refs) + change.astype(BF16).astype(F32)).astype(BF16)
    fresh_ref[...] = fresh
    ones = jnp.ones((2 * HEAD, HEAD), BF16)
    scale = HEAD ** (-0.5)
    for g in range(fresh.shape[1] // (2 * HEAD)):
        key = fresh[:, 2 * g * HEAD : (2 * g + 1) * HEAD].astype(F32)
        value = fresh[:, (2 * g + 1) * HEAD : (2 * g + 2) * HEAD].astype(F32)
        for h in range(g * group, (g + 1) * group):
            columns = slice(h * HEAD, (h + 1) * HEAD)
            product = q_ref[:, columns].astype(F32) * key
            high = product.astype(BF16)
            low = (product - high.astype(F32)).astype(BF16)
            score = jnp.dot(
                jnp.concatenate([high, low], axis=1), ones, preferred_element_type=F32
            )
            weight = 1.0 / (1.0 + jnp.exp(lse_ref[:, h : h + 1] - score * scale))
            old = out1_ref[:, columns].astype(F32)
            attended_ref[:, columns] = (old + weight * (value - old)).astype(BF16)


def finish(variant_ids, queries, out1, lse, base_terms, codes_a, codes_b, ups, ids):
    rows, features = queries.shape
    width = base_terms[0].shape[1]
    rank_part = codes_a[0].shape[1]
    group = features * 2 // width
    block = 128
    by_row = lambda columns: pl.BlockSpec((block, columns), lambda i, ids_ref: (i, 0))
    counts = (len(base_terms), len(codes_a), len(codes_b), [u.shape[0] for u in ups])
    return pl.pallas_call(
        functools.partial(finish_kernel, counts, group),
        out_shape=[
            jax.ShapeDtypeStruct((rows, width), BF16),
            jax.ShapeDtypeStruct((rows, features), BF16),
        ],
        grid_spec=pltpu.PrefetchScalarGridSpec(
            num_scalar_prefetch=1,
            grid=(rows // block,),
            in_specs=[by_row(1), by_row(features), by_row(features), by_row(128)]
            + [by_row(width)] * len(base_terms)
            + [by_row(rank_part)] * (len(codes_a) + len(codes_b))
            + [pl.BlockSpec(u.shape, lambda i, ids_ref: (0, 0, 0)) for u in ups],
            out_specs=[by_row(width), by_row(features)],
        ),
        compiler_params=params(40),
        cost_estimate=cost(
            2 * rows * width * 256 * sum(counts[3]), 2 * rows * (3 * features + 4 * width)
        ),
        name="finish",
    )(ids, variant_ids, queries, out1, lse, *base_terms, *codes_a, *codes_b, *ups)


def reduce_base(tokens, weight, width):
    size = lax.axis_size("tensor")
    me = lax.axis_index("tensor")
    last = size - 1
    parts = {last: [project(tokens, weight, [me ^ last], width)[0]]}
    others = [t for t in range(last - 1, -1, -1)]
    others.sort(key=lambda t: -(t & 1))
    for t, part in zip(others, project(tokens, weight, [me ^ t for t in others], width)):
        parts[t] = [part]
    bit = 1
    while bit < size:
        for t in range(last, 0, -1):
            if t & bit and t & (bit - 1) == 0:
                total = parts[t][0]
                if len(parts[t]) > 1:
                    total = sum(part.astype(F32) for part in parts[t]).astype(BF16)
                parts[t ^ bit].append(swap(total, "tensor", bit))
        bit *= 2
    return parts[0]


def all_reduce(value):
    size = lax.axis_size("tensor")
    bit = 1
    terms = [value]
    while bit < size:
        if len(terms) > 1:
            terms = [sum(term.astype(F32) for term in terms).astype(BF16)]
        terms.append(swap(terms[0], "tensor", bit))
        bit *= 2
    return terms


def low_rank(tokens, variant_ids, delta_down, delta_up):
    owners = lax.axis_size("adapter")
    mine = lax.axis_index("adapter")
    local, depth, rank = delta_down.shape
    half = rank // 2
    down = [delta_down[:, :, :half], delta_down[:, :, half:]]
    if owners != 4 or lax.axis_size("groups") != 2 or local != 2:
        ids = jnp.arange(owners * local, dtype=jnp.int32)
        every = lax.all_gather(delta_down, "adapter", axis=0, tiled=True)
        up = lax.all_gather(delta_up, "adapter", axis=0, tiled=True)
        both = [
            codes(tokens, variant_ids, [every[:, :, at : at + half]], ids, None, 0, BF16)
            for at in (0, half)
        ]
        return both, [up], ids
    group = lax.axis_index("groups")
    first = lax.dynamic_slice_in_dim(down[0], group, 1, axis=0)
    from_y = swap(first, "adapter", 2)
    near = swap(delta_down, "adapter", 1)
    from_x = swap(from_y, "groups", 1)
    far = swap(down[1], "adapter", 2)
    up_y = swap(delta_up, "adapter", 2)

    ids_near = [2 * mine, 2 * mine + 1, 2 * (mine ^ 1), 2 * (mine ^ 1) + 1]
    start = codes(
        tokens, variant_ids, [delta_down, near], jnp.stack(ids_near), None, 0, F32
    )
    pair_a = jnp.concatenate([from_y, from_x], axis=0)
    pair_a_near = swap(pair_a, "adapter", 1)
    lane, lane_near = 2 * (mine ^ 2), 2 * (mine ^ 3)
    ids_a = [lane + group, lane + 1 - group, lane_near + group, lane_near + 1 - group]
    part_a = codes(
        tokens, variant_ids, [pair_a, pair_a_near], jnp.stack(ids_a), start, 0, BF16
    )
    far_near = swap(far, "adapter", 1)
    ids_b = [lane, lane + 1, lane_near, lane_near + 1]
    part_b = codes(
        tokens, variant_ids, [far, far_near], jnp.stack(ids_b), start, 1, BF16
    )
    up_two = jnp.concatenate([delta_up, up_y], axis=0)
    up_near = swap(up_two, "adapter", 1)
    ids_up = [2 * (mine ^ k) + j for k in (0, 2, 1, 3) for j in (0, 1)]
    return [part_a, part_b], [up_two, up_near], jnp.stack(ids_up).astype(jnp.int32)


def local(tokens, queries, kv_cache, kv_lengths, variant_ids, base_weight, delta_down, delta_up):
    width = base_weight.shape[1] // lax.axis_size("tensor")
    parts, ups, ids = low_rank(tokens, variant_ids, delta_down, delta_up)
    base_terms = reduce_base(tokens, base_weight, width)
    codes_a, codes_b = [all_reduce(part) for part in parts]
    out1, lse = cached(queries, kv_cache, kv_lengths[:, None])
    fresh, attended = finish(
        variant_ids, queries, out1, lse, base_terms, codes_a, codes_b, ups, ids
    )
    return (fresh, attended)


def solution(mesh):
    return jax.shard_map(
        local,
        mesh=mesh,
        in_specs=(
            P(("groups", "adapter"), "tensor"),
            P(("groups", "adapter"), "tensor"),
            P(("groups", "adapter"), None, "tensor"),
            P(("groups", "adapter")),
            P(("groups", "adapter"), None),
            P("tensor", None),
            P("adapter", "tensor", None),
            P("adapter", None, "tensor"),
        ),
        out_specs=(P(("groups", "adapter"), "tensor"), P(("groups", "adapter"), "tensor")),
        check_vma=False,
    )
```

time: 187 us -> 128 us (0.68)
  blocking collectives: 56.8 us -> 0 us
  waiting for transfers between devices: 1.45 us -> 46.9 us
  Pallas kernels: 0 us -> 36.6 us
  local copies, waits for them, and re-layouts: 57 us -> 22.2 us
  matrix products: 34.4 us -> 0 us
  starting transfers between devices: 0.12 us -> 19.5 us
  other arithmetic: 20.2 us -> 1.56 us
  between operations: 15.7 us -> 0.82 us
    psum x1 -> x0, blocking collectives: 56.8 us -> none  [local(): lowrank = lax.psum(partial_rank, 'tensor').astype(jnp.bfloat16)]
    ppermute x0 -> x15, waiting for transfers between devices: none -> 46.9 us  [swap(): lax.ppermute(value, axis, [(i, i ^ bit) for i in range(lax.axis_size(axis...]
    pallas_call x0 -> x7, Pallas kernels: none -> 36.6 us  [the longest x3 14.7 us: codes(): pl.pallas_call(functools.partial(codes_kernel, sizes, steps, start is not...]
    dot_general x6 -> x0, matrix products: 34.4 us -> none  [the longest x1 10.5 us: local(): jnp.dot(tokens, base_weight, preferred_element_type=jnp.float32)]
    unnamed x18 -> x25, local copies, waits for them, and re-layouts: 36.1 us -> 14.1 us
    ppermute x0 -> x15, starting transfers between devices: none -> 19.5 us  [swap(): lax.ppermute(value, axis, [(i, i ^ bit) for i in range(lax.axis_size(axis...]
    reduce_sum x2 -> x0, other arithmetic: 15.8 us -> none  [the longest x1 15.7 us: attend(): denominator = jnp.sum(weights, axis=-1) + own_weight]
    gather x2 -> x0, local copies, waits for them, and re-layouts: 8.24 us -> none  [the longest x1 6.26 us: local(): slotted = padded[row_of].reshape(variants, capacity, local_width)]
  transfers between devices with their start and end apart: 3 -> 15, of which waited for: 0 -> 6; matrix products, arithmetic and copies ran while one was open for 44% -> 9% of each run, Pallas kernels for 0% -> 24%
where the time goes in v1:
time: 128 us
  waiting for transfers between devices  46.9 us (37%)
  Pallas kernels  36.6 us (29%)
  local copies, waits for them, and re-layouts  22.2 us (17%)
  starting transfers between devices  19.5 us (15%)
  other arithmetic  1.56 us (1%)
    ppermute x15, waiting for transfers between devices, swap(): lax.ppermute(value, axis, [(i, i ^ bit) for i in range(lax.axis_size(axis...  46.9 us
    ppermute x15, starting transfers between devices, swap(): lax.ppermute(value, axis, [(i, i ^ bit) for i in range(lax.axis_size(axis...  19.5 us
    pallas_call x3, Pallas kernels, codes(): pl.pallas_call(functools.partial(codes_kernel, sizes, steps, start is not...  14.7 us
    unnamed x25, local copies, waits for them, and re-layouts  14.1 us
    pallas_call x2, Pallas kernels, project(): pl.pallas_call(functools.partial(project_kernel, count, steps), out_shape...  9.54 us
    pallas_call x1, Pallas kernels, cached(): pl.pallas_call(functools.partial(cached_kernel, positions, group), out_sh...  6.29 us
    pallas_call x1, Pallas kernels, finish(): pl.pallas_call(functools.partial(finish_kernel, counts, group), out_shape...  6.06 us
    slice x1, local copies, waits for them, and re-layouts, low_rank(): down = [delta_down[:, :, :half], delta_down[:, :, half:]]  3.11 us
  transfers between devices with their start and end apart: 15, of which 6 were waited for; matrix products, arithmetic and copies ran while one was open for 9% of the time, Pallas kernels for 24%

profile of v1, /device:TPU:0, one launch (start us, length us, event | category | flops | bytes accessed | tf_op | source)
XLA Modules:
  0.0 127.5 jit_solution(16527506354799914030)
XLA Ops:
  1.2 3.1 %fusion = (bf16[2,2048,128]{2,1,0:T(8,128)(2,1)}, bf16[2,2048,128]{2,1,0:T(8,128)(2,1)}) fusion(bf16[2,2048,256]{2,1,0:T(8,128)(2,1)} %refs_0_.1), kind=kLoop, calls=%fused_computation.12 | loop fusion | bytes 4194304 | tf_op jit(solution)/shard_map/slice | solution.py:322
  4.3 2.6 %collective-permute-start.9 = (bf16[2,2048,128]{2,1,0:T(8,128)(2,1)}, bf16[2,2048,128]{2,1,0:T(8,128)(2,1)S(1)}, u32[]{:S(2)}, u32[]{:S(2)}) collective-permute-start(bf16[2,2048,128]{2,1,0:T(8,128)(2,1)} %get-tuple-element.12), channel_id=1, source_target_pairs={{0,8},{4,12},{8,0},{12,4},{1,9},{5,13},{9,1},{13,5},{2,10},{6,14},... | collective-permute-start | bytes 3145736 | tf_op jit(solution)/shard_map/ppermute | solution.py:24
  6.8 1.9 %constant_dynamic-slice_fusion = bf16[1,2048,128]{2,1,0:T(8,128)(2,1)} fusion(bf16[2,2048,128]{2,1,0:T(8,128)(2,1)} %get-tuple-element.13, s32[]{:T(128)S(6)} %select_n.3), kind=kLoop, calls=%fused_computation.11 | loop fusion | bytes 1048580 | tf_op jit(solution)/shard_map/dynamic_slice | solution.py:333
  8.7 3.4 %copy-done.1 = bf16[2048,2048]{1,0:T(8,128)(2,1)S(1)} copy-done((bf16[2048,2048]{1,0:T(8,128)(2,1)S(1)}, bf16[2048,2048]{1,0:T(8,128)(2,1)}, u32[]{:S(2)}) %copy-start.1) | copy-done | bytes 8388632
  12.1 2.6 %project.3 = bf16[512,512]{1,0:T(8,128)(2,1)} custom-call(s32[1]{0:T(128)} %bitcast.12.shards_ref, bf16[512,2048]{1,0:T(8,128)(2,1)S(1)} %copy-done, bf16[2048,2048]{1,0:T(8,128)(2,1)S(1)} %copy-done.1), custom_call_target="tpu_custom_call" | custom-call | flops 1073741824 | bytes 4718592 | tf_op jit(solution)/shard_map/project/pallas_call | solution.py:47
  14.7 2.1 %collective-permute-start.1 = (bf16[512,512]{1,0:T(8,128)(2,1)}, bf16[512,512]{1,0:T(8,128)(2,1)}, u32[]{:S(2)}, u32[]{:S(2)}) collective-permute-start(bf16[512,512]{1,0:T(8,128)(2,1)} %project.3), channel_id=1, source_target_pairs={{0,1},{1,0},{2,3},{3,2},{4,5},{5,4},{6,7},{7,6},{8,9},{9,8},{10,11... | collective-permute-start | bytes 1572872 | tf_op jit(solution)/shard_map/ppermute | solution.py:24
  16.7 1.5 %collective-permute-start.13 = (bf16[2,256,512]{2,1,0:T(8,128)(2,1)}, bf16[2,256,512]{2,1,0:T(8,128)(2,1)}, u32[]{:S(2)}, u32[]{:S(2)}) collective-permute-start(bf16[2,256,512]{2,1,0:T(8,128)(2,1)} %param.15), channel_id=1, source_target_pairs={{0,8},{4,12},{8,0},{12,4},{1,9},{5,13},{9,1},{13,5},{2,10},{6,14},... | collective-permute-start | bytes 1572872 | tf_op jit(solution)/shard_map/ppermute | solution.py:24
  18.3 24.0 %collective-permute-done.3 = bf16[1,2048,128]{2,1,0:T(8,128)(2,1)} collective-permute-done((bf16[1,2048,128]{2,1,0:T(8,128)(2,1)}, bf16[1,2048,128]{2,1,0:T(8,128)(2,1)}, u32[]{:S(2)}, u32[]{:S(2)}) %collective-permute-start.3) | collective-permute-done | bytes 524320 | tf_op jit(solution)/shard_map/ppermute | solution.py:24
  42.4 2.0 %collective-permute-start.4 = (bf16[1,2048,128]{2,1,0:T(8,128)(2,1)}, bf16[1,2048,128]{2,1,0:T(8,128)(2,1)}, u32[]{:S(2)}, u32[]{:S(2)}) collective-permute-start(bf16[1,2048,128]{2,1,0:T(8,128)(2,1)} %collective-permute-done.3), channel_id=1, source_target_pairs={{0,16},{16,0},{1,17},{17,1},{2,18},{18,2},{3,19},{19,3},{4,20},{20... | collective-permute-start | bytes 1572872 | tf_op jit(solution)/shard_map/ppermute | solution.py:24
  45.6 1.1 constant_dynamic-update-slice_fusion.3
  46.8 1.1 constant_dynamic-update-slice_fusion.1
  47.9 8.1 %collective-permute-done.4 = bf16[1,2048,128]{2,1,0:T(8,128)(2,1)} collective-permute-done((bf16[1,2048,128]{2,1,0:T(8,128)(2,1)}, bf16[1,2048,128]{2,1,0:T(8,128)(2,1)}, u32[]{:S(2)}, u32[]{:S(2)}) %collective-permute-start.4) | collective-permute-done | bytes 524320 | tf_op jit(solution)/shard_map/ppermute | solution.py:24
  56.0 1.1 constant_dynamic-update-slice_fusion.refs_0_
  57.2 3.4 %copy-done.2 = bf16[2048,2048]{1,0:T(8,128)(2,1)S(1)} copy-done((bf16[2048,2048]{1,0:T(8,128)(2,1)S(1)}, bf16[2048,2048]{1,0:T(8,128)(2,1)}, u32[]{:S(2)}) %copy-start.2) | copy-done | bytes 8388632
  60.6 7.0 %project.2 = (bf16[512,512]{1,0:T(8,128)(2,1)}, bf16[512,512]{1,0:T(8,128)(2,1)S(1)}, bf16[512,512]{1,0:T(8,128)(2,1)S(1)}) custom-call(s32[3]{0:T(128)S(1)} %pad_add_fusion.shards_ref, bf16[512,2048]{1,0:T(8,128)(2,1)S(1)} %copy-done, bf16[2048,2048]{1,0:T(8,128)(2,1)S(1)} %copy-done.2), custom_call_target="tpu_custom_call" | custom-call | flops 3221225472 | bytes 9961472 | tf_op jit(solution)/shard_map/project/pallas_call | solution.py:47
  67.6 1.6 %collective-permute-start = (bf16[512,512]{1,0:T(8,128)(2,1)}, bf16[512,512]{1,0:T(8,128)(2,1)S(1)}, u32[]{:S(2)}, u32[]{:S(2)}) collective-permute-start(bf16[512,512]{1,0:T(8,128)(2,1)} %get-tuple-element.10), channel_id=1, source_target_pairs={{0,1},{1,0},{2,3},{3,2},{4,5},{5,4},{6,7},{7,6},{8,9},{9,8},{10,11... | collective-permute-start | bytes 1572872 | tf_op jit(solution)/shard_map/ppermute | solution.py:24
  69.2 1.1 constant_dynamic-update-slice_fusion.2.refs_7_
  70.6 1.6 %copy-done.5 = bf16[2,2048,256]{2,1,0:T(8,128)(2,1)S(1)} copy-done((bf16[2,2048,256]{2,1,0:T(8,128)(2,1)S(1)}, bf16[2,2048,256]{2,1,0:T(8,128)(2,1)}, u32[]{:S(2)}) %copy-start.5) | copy-done | bytes 2097176
  72.2 5.7 %codes.3.refs_2_ = f32[512,256]{1,0:T(8,128)S(1)} custom-call(s32[4]{0:T(128)S(1)} %pad_add_fusion.2.ids_ref, s32[512,1]{1,0:T(8,128)S(1)} %copy.18.variant_ref, bf16[512,2048]{1,0:T(8,128)(2,1)S(1)} %copy-done, bf16[2,2048,256]{2,1,0:T(8,128)(2,1)S(1)} %copy-done.5, bf16[2,2048,256]{2,1,0:T(8,128)(2,1)} %collective-permute-done.6.refs_1_), custom_call_target="tpu_custom_call" | custom-call | flops 2147483648 | bytes 6291456 | tf_op jit(solution)/shard_map/codes/pallas_call | solution.py:115
  77.9 4.5 %codes.5 = bf16[512,128]{1,0:T(8,128)(2,1)S(1)} custom-call(s32[4]{0:T(128)S(1)} %pad_add_fusion.3.ids_ref, s32[512,1]{1,0:T(8,128)S(1)} %copy.18.variant_ref, bf16[512,2048]{1,0:T(8,128)(2,1)S(1)} %copy-done, bf16[2,2048,128]{2,1,0:T(8,128)(2,1)S(1)} %collective-permute-done.9.refs_0_, bf16[2,2048,128]{2,1,0:T(8,128)(2,1)} %collective-permute-done.10.refs_1_, ...), custom_call_target="tpu_custom_call" | custom-call | flops 1073741824 | bytes 4194304 | tf_op jit(solution)/shard_map/codes/pallas_call | solution.py:115
  82.9 1.2 add_convert_fusion
  84.1 2.6 %collective-permute-start.2 = (bf16[512,512]{1,0:T(8,128)(2,1)S(1)}, bf16[512,512]{1,0:T(8,128)(2,1)S(1)}, u32[]{:S(2)}, u32[]{:S(2)}) collective-permute-start(bf16[512,512]{1,0:T(8,128)(2,1)S(1)} %add_convert_fusion), channel_id=1, source_target_pairs={{0,2},{1,3},{2,0},{3,1},{4,6},{5,7},{6,4},{7,5},{8,10},{9,11},{10,... | collective-permute-start | bytes 1572872 | tf_op jit(solution)/shard_map/ppermute | solution.py:24
  86.8 4.5 %codes.4 = bf16[512,128]{1,0:T(8,128)(2,1)S(1)} custom-call(s32[4]{0:T(128)S(1)} %pad_add_fusion.1.ids_ref, s32[512,1]{1,0:T(8,128)S(1)} %copy.18.variant_ref, bf16[512,2048]{1,0:T(8,128)(2,1)S(1)} %copy-done, bf16[2,2048,128]{2,1,0:T(8,128)(2,1)S(1)} %constant_dynamic-update-slice_fusion.refs_0_, bf16[2,2048,128]{2,1,0:T(8,128)(2,1)} %collective-permute-done.5.refs_1_, ...), custom_call_target="tpu_custom_call" | custom-call | flops 1073741824 | bytes 4194304 | tf_op jit(solution)/shard_map/codes/pallas_call | solution.py:115
  91.3 1.6 %collective-permute-start.7 = (bf16[512,128]{1,0:T(8,128)(2,1)S(1)}, bf16[512,128]{1,0:T(8,128)(2,1)S(1)}, u32[]{:S(2)}, u32[]{:S(2)}) collective-permute-start(bf16[512,128]{1,0:T(8,128)(2,1)S(1)} %codes.4), channel_id=1, source_target_pairs={{0,1},{1,0},{2,3},{3,2},{4,5},{5,4},{6,7},{7,6},{8,9},{9,8},{10,11... | collective-permute-start | bytes 393224 | tf_op jit(solution)/shard_map/ppermute | solution.py:24
  93.4 8.5 %collective-permute-done.7 = bf16[512,128]{1,0:T(8,128)(2,1)S(1)} collective-permute-done((bf16[512,128]{1,0:T(8,128)(2,1)S(1)}, bf16[512,128]{1,0:T(8,128)(2,1)S(1)}, u32[]{:S(2)}, u32[]{:S(2)}) %collective-permute-start.7) | collective-permute-done | bytes 131104 | tf_op jit(solution)/shard_map/ppermute | solution.py:24
  102.0 3.6 %collective-permute-start.8 = (bf16[512,128]{1,0:T(8,128)(2,1)S(1)}, bf16[512,128]{1,0:T(8,128)(2,1)S(1)}, u32[]{:S(2)}, u32[]{:S(2)}) collective-permute-start(bf16[512,128]{1,0:T(8,128)(2,1)S(1)} %add_convert_fusion.2.refs_3_), channel_id=1, source_target_pairs={{0,2},{1,3},{2,0},{3,1},{4,6},{5,7},{6,4},{7,5},{8,10},{9,11},{10,... | collective-permute-start | bytes 393224 | tf_op jit(solution)/shard_map/ppermute | solution.py:24
  105.6 3.4 %copy-done.3 = bf16[512,16,512]{2,1,0:T(8,128)(2,1)S(1)} copy-done((bf16[512,16,512]{2,1,0:T(8,128)(2,1)S(1)}, bf16[512,16,512]{2,1,0:T(8,128)(2,1)}, u32[]{:S(2)}) %copy-start.3) | copy-done | bytes 8388632
  109.0 6.3 %cached.1 = (bf16[512,2048]{1,0:T(8,128)(2,1)S(1)}, f32[512,128]{1,0:T(8,128)S(1)}) custom-call(s32[512,1]{1,0:T(8,128)S(1)} %copy-done.6, bf16[512,2048]{1,0:T(8,128)(2,1)S(1)} %copy-done.4, bf16[512,16,512]{2,1,0:T(8,128)(2,1)S(1)} %copy-done.3), custom_call_target="tpu_custom_call" | custom-call | flops 2147483648 | bytes 12582912 | tf_op jit(solution)/shard_map/cached/pallas_call | solution.py:187
  115.3 1.5 %collective-permute-done.2.refs_2_ = bf16[512,512]{1,0:T(8,128)(2,1)S(1)} collective-permute-done((bf16[512,512]{1,0:T(8,128)(2,1)S(1)}, bf16[512,512]{1,0:T(8,128)(2,1)S(1)}, u32[]{:S(2)}, u32[]{:S(2)}) %collective-permute-start.2) | collective-permute-done | bytes 524320 | tf_op jit(solution)/shard_map/ppermute | solution.py:24
  116.8 2.8 %collective-permute-done.12.refs_6_ = bf16[512,128]{1,0:T(8,128)(2,1)S(1)} collective-permute-done((bf16[512,128]{1,0:T(8,128)(2,1)S(1)}, bf16[512,128]{1,0:T(8,128)(2,1)S(1)}, u32[]{:S(2)}, u32[]{:S(2)}) %collective-permute-start.12) | collective-permute-done | bytes 131104 | tf_op jit(solution)/shard_map/ppermute | solution.py:24
  119.6 1.9 %collective-permute-done.8.refs_4_ = bf16[512,128]{1,0:T(8,128)(2,1)S(1)} collective-permute-done((bf16[512,128]{1,0:T(8,128)(2,1)S(1)}, bf16[512,128]{1,0:T(8,128)(2,1)S(1)}, u32[]{:S(2)}, u32[]{:S(2)}) %collective-permute-start.8) | collective-permute-done | bytes 131104 | tf_op jit(solution)/shard_map/ppermute | solution.py:24
  121.5 6.1 %finish.1 = (bf16[512,512]{1,0:T(8,128)(2,1)}, bf16[512,2048]{1,0:T(8,128)(2,1)}) custom-call(s32[8]{0:T(128)S(1)} %stack.79.ids_ref, s32[512,1]{1,0:T(8,128)S(1)} %copy.18.variant_ref, bf16[512,2048]{1,0:T(8,128)(2,1)S(1)} %copy-done.4, bf16[512,2048]{1,0:T(8,128)(2,1)S(1)} %get-tuple-element.7.out1_ref, f32[512,128]{1,0:T(8,128)S(1)} %get-tuple-element.8.lse_ref, ...), custom_call_target="tpu_custom_call" | custom-call | flops 1073741824 | bytes 8388608 | tf_op jit(solution)/shard_map/finish/pallas_call | solution.py:261
  (43 shorter events, 3.4 us)
Async XLA Ops:
  0.6 8.1 %copy-start = (bf16[512,2048]{1,0:T(8,128)(2,1)S(1)}, bf16[512,2048]{1,0:T(8,128)(2,1)}, u32[]{:S(2)}) copy-start(bf16[512,2048]{1,0:T(8,128)(2,1)} %x_ref.9) | copy-start | bytes 6291460
  0.6 69.6 %collective-permute-start.6 = (bf16[2,2048,256]{2,1,0:T(8,128)(2,1)}, bf16[2,2048,256]{2,1,0:T(8,128)(2,1)}, u32[]{:S(2)}, u32[]{:S(2)}) collective-permute-start(bf16[2,2048,256]{2,1,0:T(8,128)(2,1)} %refs_0_.1), channel_id=1, source_target_pairs={{0,4},{4,0},{8,12},{12,8},{1,5},{5,1},{9,13},{13,9},{2,6},{6,2},{1... | collective-permute-start | bytes 6291464 | tf_op jit(solution)/shard_map/ppermute | solution.py:24
  4.3 42.4 %collective-permute-start.9 = (bf16[2,2048,128]{2,1,0:T(8,128)(2,1)}, bf16[2,2048,128]{2,1,0:T(8,128)(2,1)S(1)}, u32[]{:S(2)}, u32[]{:S(2)}) collective-permute-start(bf16[2,2048,128]{2,1,0:T(8,128)(2,1)} %get-tuple-element.12), channel_id=1, source_target_pairs={{0,8},{4,12},{8,0},{12,4},{1,9},{5,13},{9,1},{13,5},{2,10},{6,14},... | collective-permute-start | bytes 3145736 | tf_op jit(solution)/shard_map/ppermute | solution.py:24
  8.7 33.7 %collective-permute-start.3 = (bf16[1,2048,128]{2,1,0:T(8,128)(2,1)}, bf16[1,2048,128]{2,1,0:T(8,128)(2,1)}, u32[]{:S(2)}, u32[]{:S(2)}) collective-permute-start(bf16[1,2048,128]{2,1,0:T(8,128)(2,1)} %constant_dynamic-slice_fusion), channel_id=1, source_target_pairs={{0,8},{4,12},{8,0},{12,4},{1,9},{5,13},{9,1},{13,5},{2,10},{6,14},... | collective-permute-start | bytes 1572872 | tf_op jit(solution)/shard_map/ppermute | solution.py:24
  8.7 3.4 %copy-start.1 = (bf16[2048,2048]{1,0:T(8,128)(2,1)S(1)}, bf16[2048,2048]{1,0:T(8,128)(2,1)}, u32[]{:S(2)}) copy-start(bf16[2048,2048]{1,0:T(8,128)(2,1)} %w_ref.3) | copy-start | bytes 25165828
  12.1 32.4 %copy-start.9 = (s32[512,1]{0,1:T(1,128)S(1)}, s32[512,1]{0,1:T(1,128)}, u32[]{:S(2)}) copy-start(s32[512,1]{0,1:T(1,128)} %param.12) | copy-start | bytes 6148
  12.1 32.6 %copy-start.10 = (s32[512]{0:T(512)S(1)}, s32[512]{0:T(512)}, u32[]{:S(2)}) copy-start(s32[512]{0:T(512)} %param.11) | copy-start | bytes 6148
  14.7 68.3 %collective-permute-start.1 = (bf16[512,512]{1,0:T(8,128)(2,1)}, bf16[512,512]{1,0:T(8,128)(2,1)}, u32[]{:S(2)}, u32[]{:S(2)}) collective-permute-start(bf16[512,512]{1,0:T(8,128)(2,1)} %project.3), channel_id=1, source_target_pairs={{0,1},{1,0},{2,3},{3,2},{4,5},{5,4},{6,7},{7,6},{8,9},{9,8},{10,11... | collective-permute-start | bytes 1572872 | tf_op jit(solution)/shard_map/ppermute | solution.py:24
  16.7 50.9 %collective-permute-start.13 = (bf16[2,256,512]{2,1,0:T(8,128)(2,1)}, bf16[2,256,512]{2,1,0:T(8,128)(2,1)}, u32[]{:S(2)}, u32[]{:S(2)}) collective-permute-start(bf16[2,256,512]{2,1,0:T(8,128)(2,1)} %param.15), channel_id=1, source_target_pairs={{0,8},{4,12},{8,0},{12,4},{1,9},{5,13},{9,1},{13,5},{2,10},{6,14},... | collective-permute-start | bytes 1572872 | tf_op jit(solution)/shard_map/ppermute | solution.py:24
  42.4 13.6 %collective-permute-start.4 = (bf16[1,2048,128]{2,1,0:T(8,128)(2,1)}, bf16[1,2048,128]{2,1,0:T(8,128)(2,1)}, u32[]{:S(2)}, u32[]{:S(2)}) collective-permute-start(bf16[1,2048,128]{2,1,0:T(8,128)(2,1)} %collective-permute-done.3), channel_id=1, source_target_pairs={{0,16},{16,0},{1,17},{17,1},{2,18},{18,2},{3,19},{19,3},{4,20},{20... | collective-permute-start | bytes 1572872 | tf_op jit(solution)/shard_map/ppermute | solution.py:24
  46.7 31.2 %collective-permute-start.10 = (bf16[2,2048,128]{2,1,0:T(8,128)(2,1)S(1)}, bf16[2,2048,128]{2,1,0:T(8,128)(2,1)}, u32[]{:S(2)}, u32[]{:S(2)}) collective-permute-start(bf16[2,2048,128]{2,1,0:T(8,128)(2,1)S(1)} %collective-permute-done.9.refs_0_), channel_id=1, source_target_pairs={{0,4},{4,0},{8,12},{12,8},{1,5},{5,1},{9,13},{13,9},{2,6},{6,2},{1... | collective-permute-start | bytes 3145736 | tf_op jit(solution)/shard_map/ppermute | solution.py:24
  57.1 29.7 %collective-permute-start.5 = (bf16[2,2048,128]{2,1,0:T(8,128)(2,1)S(1)}, bf16[2,2048,128]{2,1,0:T(8,128)(2,1)}, u32[]{:S(2)}, u32[]{:S(2)}) collective-permute-start(bf16[2,2048,128]{2,1,0:T(8,128)(2,1)S(1)} %constant_dynamic-update-slice_fusion.refs_0_), channel_id=1, source_target_pairs={{0,4},{4,0},{8,12},{12,8},{1,5},{5,1},{9,13},{13,9},{2,6},{6,2},{1... | collective-permute-start | bytes 3145736 | tf_op jit(solution)/shard_map/ppermute | solution.py:24
  57.2 3.4 %copy-start.2 = (bf16[2048,2048]{1,0:T(8,128)(2,1)S(1)}, bf16[2048,2048]{1,0:T(8,128)(2,1)}, u32[]{:S(2)}) copy-start(bf16[2048,2048]{1,0:T(8,128)(2,1)} %w_ref.3) | copy-start | bytes 25165828
  67.5 2.7 %copy-start.7 = (bf16[512,512]{1,0:T(8,128)(2,1)}, bf16[512,512]{1,0:T(8,128)(2,1)S(1)}, u32[]{:S(2)}) copy-start(bf16[512,512]{1,0:T(8,128)(2,1)S(1)} %get-tuple-element.9.refs_0_) | copy-start | bytes 1572868
  67.6 47.6 %collective-permute-start = (bf16[512,512]{1,0:T(8,128)(2,1)}, bf16[512,512]{1,0:T(8,128)(2,1)S(1)}, u32[]{:S(2)}, u32[]{:S(2)}) collective-permute-start(bf16[512,512]{1,0:T(8,128)(2,1)} %get-tuple-element.10), channel_id=1, source_target_pairs={{0,1},{1,0},{2,3},{3,2},{4,5},{5,4},{6,7},{7,6},{8,9},{9,8},{10,11... | collective-permute-start | bytes 1572872 | tf_op jit(solution)/shard_map/ppermute | solution.py:24
  70.3 46.5 %collective-permute-start.14 = (bf16[4,256,512]{2,1,0:T(8,128)(2,1)S(1)}, bf16[4,256,512]{2,1,0:T(8,128)(2,1)S(1)}, u32[]{:S(2)}, u32[]{:S(2)}) collective-permute-start(bf16[4,256,512]{2,1,0:T(8,128)(2,1)S(1)} %constant_dynamic-update-slice_fusion.2.refs_7_), channel_id=1, source_target_pairs={{0,4},{4,0},{8,12},{12,8},{1,5},{5,1},{9,13},{13,9},{2,6},{6,2},{1... | collective-permute-start | bytes 3145736 | tf_op jit(solution)/shard_map/ppermute | solution.py:24
  70.6 1.6 %copy-start.5 = (bf16[2,2048,256]{2,1,0:T(8,128)(2,1)S(1)}, bf16[2,2048,256]{2,1,0:T(8,128)(2,1)}, u32[]{:S(2)}) copy-start(bf16[2,2048,256]{2,1,0:T(8,128)(2,1)} %refs_0_.1) | copy-start | bytes 6291460
  82.4 10.6 %collective-permute-start.11 = (bf16[512,128]{1,0:T(8,128)(2,1)S(1)}, bf16[512,128]{1,0:T(8,128)(2,1)S(1)}, u32[]{:S(2)}, u32[]{:S(2)}) collective-permute-start(bf16[512,128]{1,0:T(8,128)(2,1)S(1)} %codes.5), channel_id=1, source_target_pairs={{0,1},{1,0},{2,3},{3,2},{4,5},{5,4},{6,7},{7,6},{8,9},{9,8},{10,11... | collective-permute-start | bytes 393224 | tf_op jit(solution)/shard_map/ppermute | solution.py:24
  84.1 21.5 %copy-start.4 = (bf16[512,2048]{1,0:T(8,128)(2,1)S(1)}, bf16[512,2048]{1,0:T(8,128)(2,1)}, u32[]{:S(2)}) copy-start(bf16[512,2048]{1,0:T(8,128)(2,1)} %q_ref.3) | copy-start | bytes 6291460
  84.1 21.4 %copy-start.6 = (s32[512,1]{1,0:T(8,128)S(1)}, s32[512,1]{1,0:T(8,128)}, u32[]{:S(2)}) copy-start(s32[512,1]{1,0:T(8,128)} %copy.14.len_ref) | copy-start | bytes 6148
  84.1 32.6 %collective-permute-start.2 = (bf16[512,512]{1,0:T(8,128)(2,1)S(1)}, bf16[512,512]{1,0:T(8,128)(2,1)S(1)}, u32[]{:S(2)}, u32[]{:S(2)}) collective-permute-start(bf16[512,512]{1,0:T(8,128)(2,1)S(1)} %add_convert_fusion), channel_id=1, source_target_pairs={{0,2},{1,3},{2,0},{3,1},{4,6},{5,7},{6,4},{7,5},{8,10},{9,11},{10,... | collective-permute-start | bytes 1572872 | tf_op jit(solution)/shard_map/ppermute | solution.py:24
  91.3 10.6 %collective-permute-start.7 = (bf16[512,128]{1,0:T(8,128)(2,1)S(1)}, bf16[512,128]{1,0:T(8,128)(2,1)S(1)}, u32[]{:S(2)}, u32[]{:S(2)}) collective-permute-start(bf16[512,128]{1,0:T(8,128)(2,1)S(1)} %codes.4), channel_id=1, source_target_pairs={{0,1},{1,0},{2,3},{3,2},{4,5},{5,4},{6,7},{7,6},{8,9},{9,8},{10,11... | collective-permute-start | bytes 393224 | tf_op jit(solution)/shard_map/ppermute | solution.py:24
  93.0 26.6 %collective-permute-start.12 = (bf16[512,128]{1,0:T(8,128)(2,1)S(1)}, bf16[512,128]{1,0:T(8,128)(2,1)S(1)}, u32[]{:S(2)}, u32[]{:S(2)}) collective-permute-start(bf16[512,128]{1,0:T(8,128)(2,1)S(1)} %add_convert_fusion.1.refs_5_), channel_id=1, source_target_pairs={{0,2},{1,3},{2,0},{3,1},{4,6},{5,7},{6,4},{7,5},{8,10},{9,11},{10,... | collective-permute-start | bytes 393224 | tf_op jit(solution)/shard_map/ppermute | solution.py:24
  102.0 19.5 %collective-permute-start.8 = (bf16[512,128]{1,0:T(8,128)(2,1)S(1)}, bf16[512,128]{1,0:T(8,128)(2,1)S(1)}, u32[]{:S(2)}, u32[]{:S(2)}) collective-permute-start(bf16[512,128]{1,0:T(8,128)(2,1)S(1)} %add_convert_fusion.2.refs_3_), channel_id=1, source_target_pairs={{0,2},{1,3},{2,0},{3,1},{4,6},{5,7},{6,4},{7,5},{8,10},{9,11},{10,... | collective-permute-start | bytes 393224 | tf_op jit(solution)/shard_map/ppermute | solution.py:24
  105.6 3.4 %copy-start.3 = (bf16[512,16,512]{2,1,0:T(8,128)(2,1)S(1)}, bf16[512,16,512]{2,1,0:T(8,128)(2,1)}, u32[]{:S(2)}) copy-start(bf16[512,16,512]{2,1,0:T(8,128)(2,1)} %kv_ref.1) | copy-start | bytes 25165828
  109.0 12.5 %copy-start.8 = (bf16[512,512]{1,0:T(8,128)(2,1)S(1)}, bf16[512,512]{1,0:T(8,128)(2,1)}, u32[]{:S(2)}) copy-start(bf16[512,512]{1,0:T(8,128)(2,1)} %copy-done.7) | copy-start | bytes 1572868

commit v2 on v0

v2 whole, which is shorter than its diff:
```python
import functools

import jax
import jax.numpy as jnp
from jax import lax
from jax.experimental import pallas as pl
from jax.experimental.pallas import tpu as pltpu
from jax.sharding import PartitionSpec as P

HEAD = 128
BF16 = jnp.bfloat16
F32 = jnp.float32
ANY = pl.BlockSpec(memory_space=pl.ANY)
WHOLE = pl.BlockSpec(memory_space=pltpu.VMEM)
SCALARS = pl.BlockSpec(memory_space=pltpu.SMEM)


def params(mib):
    return pltpu.CompilerParams(vmem_limit_bytes=mib << 20)


def brief():
    return pl.CostEstimate(flops=1, bytes_accessed=1, transcendentals=0)


def gate(value, after):
    def body(*refs):
        del refs

    return pl.pallas_call(
        body,
        out_shape=jax.ShapeDtypeStruct(value.shape, value.dtype),
        in_specs=[ANY] * (1 + len(after)),
        out_specs=ANY,
        input_output_aliases={0: 0},
        compiler_params=params(16),
        cost_estimate=brief(),
        name="gate",
    )(value, *after)


def cut(value, first, count, column, width, after):
    depth = value.shape[1]
    pieces = 2
    block = depth // pieces

    def body(first_ref, value_ref, *refs):
        out_ref, held, sems = refs[-3:]
        where = [(i, pl.ds(k * block, block), k) for i in range(count) for k in range(pieces)]
        loads = [
            pltpu.make_async_copy(
                value_ref.at[first_ref[0] + i, rows, pl.ds(column * width, width)],
                held.at[i, rows],
                sems.at[0, i, k],
            )
            for i, rows, k in where
        ]
        stores = [
            pltpu.make_async_copy(held.at[i, rows], out_ref.at[i, rows], sems.at[1, i, k])
            for i, rows, k in where
        ]
        for load in loads:
            load.start()
        for load, store in zip(loads, stores):
            load.wait()
            store.start()
        for store in stores:
            store.wait()

    return pl.pallas_call(
        body,
        out_shape=jax.ShapeDtypeStruct((count, depth, width), value.dtype),
        in_specs=[SCALARS] + [ANY] * (1 + len(after)),
        out_specs=ANY,
        scratch_shapes=[
            pltpu.VMEM((count, depth, width), value.dtype),
            pltpu.SemaphoreType.DMA((2, count, pieces)),
        ],
        compiler_params=params(16),
        cost_estimate=brief(),
        name="cut",
    )(jnp.full((1,), first, jnp.int32), value, *after)


def permute(value, axis, pairs):
    return lax.ppermute(value, axis, pairs)


def swap(value, axis, bit):
    return lax.ppermute(value, axis, [(i, i ^ bit) for i in range(lax.axis_size(axis))])


def added(terms):
    return sum(term.astype(F32) for term in terms).astype(BF16)


def project(tokens, weight, shards, width, after):
    rows, depth = tokens.shape
    count = len(shards)
    pieces = 4
    block = depth // pieces

    def body(shards_ref, x_ref, w_ref, *refs):
        outs = refs[len(after) : len(after) + count]
        held, made, load_sems, store_sems = refs[len(after) + count :]
        loads = [
            [
                pltpu.make_async_copy(
                    w_ref.at[
                        pl.ds(k * block, block),
                        pl.ds(pl.multiple_of(shards_ref[i] * width, width), width),
                    ],
                    held.at[i, pl.ds(k * block, block)],
                    load_sems.at[i, k],
                )
                for k in range(pieces)
            ]
            for i in range(count)
        ]
        stores = [
            pltpu.make_async_copy(made.at[i], outs[i], store_sems.at[i]) for i in range(count)
        ]
        for group in loads:
            for load in group:
                load.start()
        for i in range(count):
            if i == 0:
                total = jnp.zeros((rows, width), F32)
                for k in range(pieces):
                    loads[0][k].wait()
                    part = slice(k * block, (k + 1) * block)
                    total = total + jnp.dot(
                        x_ref[:, part], held[0, part], preferred_element_type=F32
                    )
                made[0] = total.astype(BF16)
            else:
                for k in range(pieces):
                    loads[i][k].wait()
                made[i] = jnp.dot(x_ref[...], held[i], preferred_element_type=F32).astype(BF16)
            stores[i].start()
        for store in stores:
            store.wait()

    return pl.pallas_call(
        body,
        out_shape=[jax.ShapeDtypeStruct((rows, width), BF16)] * count,
        in_specs=[SCALARS, WHOLE] + [ANY] * (1 + len(after)),
        out_specs=[ANY] * count,
        scratch_shapes=[
            pltpu.VMEM((count, depth, width), BF16),
            pltpu.VMEM((count, rows, width), BF16),
            pltpu.SemaphoreType.DMA((count, pieces)),
            pltpu.SemaphoreType.DMA((count,)),
        ],
        compiler_params=params(48),
        cost_estimate=brief(),
        name="project",
    )(jnp.stack(shards).astype(jnp.int32), tokens, weight, *after)


def codes(sets, weights, ids, column, dtypes, after):
    depth, width = weights[0].shape[1:]
    sizes = [w.shape[0] for w in weights]
    has_start = [start is not None for _, _, start in sets]
    chunk = 256
    pair = max(1, 256 // width)

    def body(ids_ref, *refs):
        refs = list(refs)
        inputs = []
        for started in has_start:
            inputs.append([refs.pop(0) for _ in range(3 if started else 2)])
        flat = [w.at[j] for w, size in zip(refs[: len(sizes)], sizes) for j in range(size)]
        outs = refs[-len(sets) :]
        groups = [flat[at : at + pair] for at in range(0, len(flat), pair)]
        for out_ref, given in zip(outs, inputs):
            for row in range(0, out_ref.shape[0], chunk):
                here = slice(row, row + chunk)
                x, variant = given[0][here], given[1][here]
                if len(given) == 3:
                    kept = given[2][here, column : column + width]
                else:
                    kept = jnp.zeros((x.shape[0], width), F32)
                for g, group in enumerate(groups):
                    w = jnp.concatenate([entry[...] for entry in group], axis=1)
                    product = jnp.dot(x, w, preferred_element_type=F32)
                    for j in range(len(group)):
                        mine = variant == ids_ref[g * pair + j]
                        kept = jnp.where(mine, product[:, j * width : (j + 1) * width], kept)
                out_ref[here] = kept.astype(out_ref.dtype)

    operands = []
    for tokens, variant, start in sets:
        operands += [tokens, variant] + ([start] if start is not None else [])
    return pl.pallas_call(
        body,
        out_shape=[
            jax.ShapeDtypeStruct((tokens.shape[0], width), dtype)
            for (tokens, _, _), dtype in zip(sets, dtypes)
        ],
        in_specs=[SCALARS] + [WHOLE] * (len(operands) + len(weights)) + [ANY] * len(after),
        out_specs=[WHOLE] * len(sets),
        compiler_params=params(30),
        cost_estimate=brief(),
        name="codes",
    )(ids.astype(jnp.int32), *operands, *weights, *after)


def cached_kernel(positions, group, len_ref, q_ref, kv_ref, *refs):
    out_ref, lse_ref = refs[-2:]
    rows = q_ref.shape[0]
    kv_local = kv_ref.shape[2] // (2 * HEAD)
    scale = HEAD ** (-0.5)
    near = 128 // positions
    lane = lax.broadcasted_iota(jnp.int32, (near, 128), 1)
    sublane = lax.broadcasted_iota(jnp.int32, (near, 128), 0)
    same = lane // positions == sublane
    at = lane % positions
    ones = jnp.ones((128, HEAD), BF16)

    for base in range(0, rows, 2 * near):
        here = pl.ds(base, 2 * near)
        seen = [same & (at < len_ref[pl.ds(base + half * near, near), :]) for half in range(2)]
        table = [jnp.zeros((near, 128), F32) for _ in range(2)]
        for g in range(kv_local):
            at_key, at_value = 2 * g * HEAD, (2 * g + 1) * HEAD
            keys = kv_ref[here, :, at_key : at_key + HEAD].reshape(256, HEAD)
            values = kv_ref[here, :, at_value : at_value + HEAD].reshape(256, HEAD)
            query = jnp.concatenate(
                [
                    q_ref[here, (g * group + h) * HEAD : (g * group + h + 1) * HEAD]
                    for h in range(group)
                ],
                axis=0,
            )
            scores = lax.dot_general(
                query, keys, (((1,), (1,)), ((), ())), preferred_element_type=F32
            ).reshape(group, 2, near, 256)
            results = []
            for half in range(2):
                own = scores[:, half, :, half * 128 : (half + 1) * 128] * scale
                own = jnp.where(seen[half][None], own, jnp.float32(-1e30))
                largest = jnp.max(own, axis=-1, keepdims=True)
                weight = jnp.exp(own - largest).astype(BF16).reshape(group * near, 128)
                value = jnp.concatenate([values[half * 128 : (half + 1) * 128], ones], axis=1)
                mixed = jnp.dot(weight, value, preferred_element_type=F32)
                total = mixed[:, HEAD:]
                results.append((mixed[:, :HEAD] / total).reshape(group, near, HEAD))
                lse = largest + jnp.log(total).reshape(group, near, 128)
                for h in range(group):
                    table[half] = jnp.where(lane == g * group + h, lse[h], table[half])
            both = jnp.stack(results, axis=1).reshape(group, 2 * near, HEAD).astype(BF16)
            for h in range(group):
                out_ref[here, (g * group + h) * HEAD : (g * group + h + 1) * HEAD] = both[h]
        for half in range(2):
            lse_ref[pl.ds(base + half * near, near), :] = table[half]


def cached(queries, kv_cache, lengths, first, count, earlier, after):
    rows, features = queries.shape
    positions, width = kv_cache.shape[1:]
    group = features * 2 // width
    block = 64
    base = first // block
    return pl.pallas_call(
        functools.partial(cached_kernel, positions, group),
        out_shape=[
            jax.ShapeDtypeStruct((rows, features), BF16),
            jax.ShapeDtypeStruct((rows, 128), F32),
        ],
        grid=(count // block,),
        in_specs=[
            pl.BlockSpec((block, 1), lambda i: (base + i, 0)),
            pl.BlockSpec((block, features), lambda i: (base + i, 0)),
            pl.BlockSpec((block, positions, width), lambda i: (base + i, 0, 0)),
        ]
        + [ANY] * (len(earlier) + len(after)),
        out_specs=[
            pl.BlockSpec((block, features), lambda i: (base + i, 0)),
            pl.BlockSpec((block, 128), lambda i: (base + i, 0)),
        ],
        input_output_aliases={3 + i: i for i in range(len(earlier))},
        compiler_params=params(30),
        cost_estimate=brief(),
        name="cached",
    )(lengths, queries, kv_cache, *earlier, *after)


def finish(variant_ids, queries, out1, lse, base_terms, choice, codes_a, codes_b, ups, ids):
    rows, features = queries.shape
    width = base_terms[0].shape[1]
    group = features * 2 // width
    chunk = 128
    scale = HEAD ** (-0.5)
    flag, extra = choice
    counts = [len(base_terms), len(extra), len(codes_a), len(codes_b), len(ups)]

    def body(ids_ref, flag_ref, variant_ref, q_ref, out1_ref, lse_ref, *refs):
        refs = list(refs)
        take = lambda n: [refs.pop(0) for _ in range(n)]
        base_refs, extra_refs, a_refs, b_refs, up_refs = [take(n) for n in counts]
        fresh_ref, attended_ref, fresh_made, attended_made, sems = refs
        ones = jnp.ones((2 * HEAD, HEAD), BF16)

        def total(parts, here):
            result = parts[0][here].astype(F32)
            for part in parts[1:]:
                result = result + part[here].astype(F32)
            return result

        stores = []
        for at in range(0, rows, chunk):
            here = slice(at, at + chunk)
            variant = variant_ref[here]
            code = jnp.concatenate(
                [total(a_refs, here).astype(BF16), total(b_refs, here).astype(BF16)], axis=1
            )
            change = jnp.zeros((chunk, width), F32)
            entry = 0
            for up_ref in up_refs:
                for j in range(up_ref.shape[0]):
                    mine = jnp.where(variant == ids_ref[entry], code, jnp.zeros_like(code))
                    change = change + jnp.dot(mine, up_ref[j], preferred_element_type=F32)
                    entry += 1
            base = total(base_refs, here)
            for part in extra_refs:
                base = base + jnp.where(flag_ref[0] == 1, part[here].astype(F32), 0.0)
            fresh = (base + change.astype(BF16).astype(F32)).astype(BF16)
            fresh_made[here] = fresh
            for g in range(width // (2 * HEAD)):
                key = fresh[:, 2 * g * HEAD : (2 * g + 1) * HEAD].astype(F32)
                value = fresh[:, (2 * g + 1) * HEAD : (2 * g + 2) * HEAD].astype(F32)
                for h in range(g * group, (g + 1) * group):
                    columns = slice(h * HEAD, (h + 1) * HEAD)
                    product = q_ref[here, columns].astype(F32) * key
                    high = product.astype(BF16)
                    low = (product - high.astype(F32)).astype(BF16)
                    score = jnp.dot(
                        jnp.concatenate([high, low], axis=1), ones, preferred_element_type=F32
                    )
                    weight = 1.0 / (1.0 + jnp.exp(lse_ref[here, h : h + 1] - score * scale))
                    old = out1_ref[here, columns].astype(F32)
                    attended_made[here, columns] = (old + weight * (value - old)).astype(BF16)
            for k, (made, ref) in enumerate(
                ((fresh_made, fresh_ref), (attended_made, attended_ref))
            ):
                lines = pl.ds(at, chunk)
                stores.append(
                    pltpu.make_async_copy(made.at[lines], ref.at[lines], sems.at[k, at // chunk])
                )
                stores[-1].start()
        for store in stores:
            store.wait()

    operands = [variant_ids, queries, out1, lse, *base_terms, *extra, *codes_a, *codes_b, *ups]
    return pl.pallas_call(
        body,
        out_shape=[
            jax.ShapeDtypeStruct((rows, width), BF16),
            jax.ShapeDtypeStruct((rows, features), BF16),
        ],
        in_specs=[SCALARS, SCALARS] + [WHOLE] * len(operands),
        out_specs=[ANY, ANY],
        scratch_shapes=[
            pltpu.VMEM((rows, width), BF16),
            pltpu.VMEM((rows, features), BF16),
            pltpu.SemaphoreType.DMA((2, rows // chunk)),
        ],
        compiler_params=params(30),
        cost_estimate=brief(),
        name="finish",
    )(ids.astype(jnp.int32), jnp.full((1,), flag, jnp.int32), *operands)


def all_reduce(value):
    size = lax.axis_size("tensor")
    bit = 1
    terms = [value]
    while bit < size:
        if len(terms) > 1:
            terms = [added(terms)]
        terms.append(swap(terms[0], "tensor", bit))
        bit *= 2
    return terms


def reduce_parts(parts):
    size = lax.axis_size("tensor")
    parts = {t: [part] for t, part in parts.items()}
    bit = 1
    while bit < size:
        for t in range(size - 1, 0, -1):
            if t & bit and t & (bit - 1) == 0:
                total = parts[t][0] if len(parts[t]) == 1 else added(parts[t])
                parts[t ^ bit].append(swap(total, "tensor", bit))
        bit *= 2
    return parts[0]


def general(tokens, queries, kv_cache, lengths, variant_ids, base_weight, delta_down, delta_up):
    size, me = lax.axis_size("tensor"), lax.axis_index("tensor")
    rows = tokens.shape[0]
    width = base_weight.shape[1] // size
    owners = lax.axis_size("adapter")
    variants, _, rank = delta_down.shape
    half = rank // 2
    every = lax.all_gather(delta_down, "adapter", axis=0, tiled=True)
    up = lax.all_gather(delta_up, "adapter", axis=0, tiled=True)
    order = sorted(range(size), key=lambda t: (-(t & 1), -t))
    parts = project(tokens, base_weight, [me ^ t for t in order], width, [])
    base_terms = reduce_parts(dict(zip(order, parts)))
    ids = jnp.arange(owners * variants, dtype=jnp.int32)
    rows_of = [(tokens, variant_ids, None)]
    codes_a, codes_b = [
        all_reduce(codes(rows_of, [every[:, :, at : at + half]], ids, 0, [BF16], parts[:1])[0])
        for at in (0, half)
    ]
    out1, lse = cached(queries, kv_cache, lengths, 0, rows, [], parts[:1])
    return finish(
        variant_ids, queries, out1, lse, base_terms, (0, []), codes_a, codes_b, [up], ids
    )


def paired(tokens, queries, kv_cache, lengths, variant_ids, base_weight, delta_down, delta_up):
    me = lax.axis_index("tensor")
    mine = lax.axis_index("adapter")
    group = lax.axis_index("groups")
    rows = tokens.shape[0]
    width = base_weight.shape[1] // 4
    half = delta_down.shape[2] // 2

    first = cut(delta_down, group, 1, 0, half, [])
    from_y = swap(first, "adapter", 2)
    near = swap(tokens, "adapter", 1)
    near_ids = swap(variant_ids, "adapter", 1)
    (part_a,) = project(tokens, base_weight, [me ^ 2], width, [first])
    got_a = permute(part_a, "tensor", [(0, 1), (1, 3), (2, 0), (3, 2)])
    second = cut(delta_down, 0, 2, 1, half, [part_a])
    far = swap(second, "adapter", 2)
    part_b, part_c, own = project(
        tokens, base_weight, [me ^ 3, me ^ 1, me], width, [second]
    )
    got_b1 = permute(part_b, "tensor", [(0, 3), (3, 0)])
    got_c = swap(part_c, "tensor", 1)

    from_y = gate(from_y, [own])
    from_x = swap(from_y, "groups", 1)
    both = [(tokens, variant_ids, None), (near, near_ids, None)]
    start, start_near = codes(
        both, [delta_down], jnp.stack([2 * mine, 2 * mine + 1]), 0, [F32, F32], [own, from_y]
    )
    sum_b = added([part_b, got_a])
    got_b2 = permute(sum_b, "tensor", [(1, 2), (2, 1)])
    early = cached(queries, kv_cache, lengths, 0, rows // 2, [], [start, sum_b])
    lane = 2 * (mine ^ 2)
    both = [(tokens, variant_ids, start), (near, near_ids, start_near)]
    a, a_near = codes(
        both,
        [from_y, from_x],
        jnp.stack([lane + group, lane + 1 - group]),
        0,
        [F32, BF16],
        [early[1]],
    )
    a = added([a, swap(a_near, "adapter", 1)])
    codes_a = all_reduce(a)
    b, b_near = codes(
        both, [far], jnp.stack([lane, lane + 1]), half, [F32, BF16], [a_near]
    )
    b = added([b, swap(b_near, "adapter", 1)])
    b = gate(b, [got_b1, got_c])
    codes_b = all_reduce(b)
    up_y = swap(delta_up, "adapter", 2)
    out1, lse = cached(
        queries, kv_cache, lengths, rows // 2, rows // 2, early, [b, codes_a[0], up_y]
    )
    ups = [delta_up, up_y, swap(delta_up, "adapter", 1), swap(up_y, "adapter", 1)]
    ids = jnp.stack([2 * (mine ^ k) + j for k in (0, 2, 1, 3) for j in (0, 1)])
    ends = (me == 0) | (me == 3)
    got_b = jnp.where(ends, got_b1, got_b2)
    return finish(
        variant_ids,
        queries,
        out1,
        lse,
        [own, got_c, got_b],
        (ends.astype(jnp.int32), [got_a]),
        codes_a,
        codes_b,
        ups,
        ids,
    )


def local(tokens, queries, kv_cache, kv_lengths, variant_ids, base_weight, delta_down, delta_up):
    sizes = [lax.axis_size(axis) for axis in ("groups", "adapter", "tensor")]
    plan = paired if sizes == [2, 4, 4] and delta_down.shape[0] == 2 else general
    return tuple(
        plan(
            tokens,
            queries,
            kv_cache,
            kv_lengths[:, None],
            variant_ids,
            base_weight,
            delta_down,
            delta_up,
        )
    )


def solution(mesh):
    return jax.shard_map(
        local,
        mesh=mesh,
        in_specs=(
            P(("groups", "adapter"), "tensor"),
            P(("groups", "adapter"), "tensor"),
            P(("groups", "adapter"), None, "tensor"),
            P(("groups", "adapter")),
            P(("groups", "adapter"), None),
            P("tensor", None),
            P("adapter", "tensor", None),
            P("adapter", None, "tensor"),
        ),
        out_specs=(P(("groups", "adapter"), "tensor"), P(("groups", "adapter"), "tensor")),
        check_vma=False,
    )
```

time: 187 us -> 92.8 us (0.50)
  blocking collectives: 56.8 us -> 0 us
  local copies, waits for them, and re-layouts: 57 us -> 15.6 us
  Pallas kernels: 0 us -> 36 us
  matrix products: 34.4 us -> 0 us
  starting transfers between devices: 0.12 us -> 23.7 us
  other arithmetic: 20.2 us -> 4.83 us
  between operations: 15.7 us -> 1.15 us
  waiting for transfers between devices: 1.45 us -> 11.1 us
    psum x1 -> x0, blocking collectives: 56.8 us -> none  [local(): lowrank = lax.psum(partial_rank, 'tensor').astype(jnp.bfloat16)]
    pallas_call x0 -> x12, Pallas kernels: none -> 36 us  [the longest x3 11.2 us: codes(): pl.pallas_call(body, out_shape=[jax.ShapeDtypeStruct((tokens.shape[0], wi...]
    dot_general x6 -> x0, matrix products: 34.4 us -> none  [the longest x1 10.5 us: local(): jnp.dot(tokens, base_weight, preferred_element_type=jnp.float32)]
    ppermute x0 -> x18, starting transfers between devices: none -> 23.7 us  [the longest x15 16.3 us: swap(): lax.ppermute(value, axis, [(i, i ^ bit) for i in range(lax.axis_size(axis...]
    unnamed x18 -> x45, local copies, waits for them, and re-layouts: 36.1 us -> 14.6 us
    reduce_sum x2 -> x0, other arithmetic: 15.8 us -> none  [the longest x1 15.7 us: attend(): denominator = jnp.sum(weights, axis=-1) + own_weight]
    ppermute x0 -> x18, waiting for transfers between devices: none -> 11.1 us  [the longest x15 11.1 us: swap(): lax.ppermute(value, axis, [(i, i ^ bit) for i in range(lax.axis_size(axis...]
    gather x2 -> x0, local copies, waits for them, and re-layouts: 8.24 us -> none  [the longest x1 6.26 us: local(): slotted = padded[row_of].reshape(variants, capacity, local_width)]
  transfers between devices with their start and end apart: 3 -> 18, of which waited for: 0 -> 5; matrix products, arithmetic and copies ran while one was open for 44% -> 6% of each run, Pallas kernels for 0% -> 31%
where the time goes in v2:
time: 92.8 us; the launch traced here: 92.3 us
  Pallas kernels  36 us (39%)
  starting transfers between devices  23.7 us (26%)
  local copies, waits for them, and re-layouts  15.6 us (17%)
  waiting for transfers between devices  11.1 us (12%)
  other arithmetic  4.83 us (5%)
  between operations  1.15 us (1%)
    ppermute x15, starting transfers between devices, swap(): lax.ppermute(value, axis, [(i, i ^ bit) for i in range(lax.axis_size(axis...  16.3 us
    unnamed x45, local copies, waits for them, and re-layouts  14.6 us
    pallas_call x3, Pallas kernels, codes(): pl.pallas_call(body, out_shape=[jax.ShapeDtypeStruct((tokens.shape[0], wi...  11.2 us
    ppermute x15, waiting for transfers between devices, swap(): lax.ppermute(value, axis, [(i, i ^ bit) for i in range(lax.axis_size(axis...  11.1 us
    pallas_call x2, Pallas kernels, project(): pl.pallas_call(body, out_shape=[jax.ShapeDtypeStruct((rows, width), BF16)...  9.39 us
    ppermute x3, starting transfers between devices, permute(): return lax.ppermute(value, axis, pairs)  7.42 us
    pallas_call x1, Pallas kernels, finish(): pl.pallas_call(body, out_shape=[jax.ShapeDtypeStruct((rows, width), BF16)...  6.97 us
    pallas_call x2, Pallas kernels, cached(): pl.pallas_call(functools.partial(cached_kernel, positions, group), out_sh...  6.29 us
  transfers between devices with their start and end apart: 18, of which 5 were waited for; matrix products, arithmetic and copies ran while one was open for 6% of the time, Pallas kernels for 31%

profile of v2, /device:TPU:0, one launch (start us, length us, event | category | flops | bytes accessed | tf_op | source)
XLA Modules:
  0.0 92.3 jit_solution(394128836988378411)
XLA Ops:
  1.2 1.7 %copy-done.3 = bf16[2,2048,256]{2,1,0:T(8,128)(2,1)S(1)} copy-done((bf16[2,2048,256]{2,1,0:T(8,128)(2,1)S(1)}, bf16[2,2048,256]{2,1,0:T(8,128)(2,1)}, u32[]{:S(2)}) %copy-start.3) | copy-done | bytes 2097176
  2.9 0.9 cut.2.refs_0_
  3.8 2.6 %collective-permute-start.2 = (bf16[1,2048,128]{2,1,0:T(8,128)(2,1)}, bf16[1,2048,128]{2,1,0:T(8,128)(2,1)S(1)}, u32[]{:S(2)}, u32[]{:S(2)}) collective-permute-start(bf16[1,2048,128]{2,1,0:T(8,128)(2,1)} %cut.2.refs_0_), channel_id=1, source_target_pairs={{0,8},{4,12},{8,0},{12,4},{1,9},{5,13},{9,1},{13,5},{2,10},{6,14},... | collective-permute-start | bytes 1572872 | tf_op jit(solution)/shard_map/ppermute | solution.py:90
  6.4 3.5 %project.2.refs_0_ = bf16[512,512]{1,0:T(8,128)(2,1)} custom-call(s32[1]{0:T(128)} %bitcast.13.shards_ref, bf16[512,2048]{1,0:T(8,128)(2,1)S(1)} %copy-done, bf16[2048,2048]{1,0:T(8,128)(2,1)} %w_ref.3, bf16[1,2048,128]{2,1,0:T(8,128)(2,1)} %cut.2.refs_0_), custom_call_target="tpu_custom_call" | custom-call | flops 1 | bytes 1 | tf_op jit(solution)/shard_map/project/pallas_call | solution.py:144
  10.0 1.2 %cut.3.refs_0_ = bf16[2,2048,128]{2,1,0:T(8,128)(2,1)} custom-call(s32[1]{0:T(128)} %constant.20.clone.1.first_ref, bf16[2,2048,256]{2,1,0:T(8,128)(2,1)S(1)} %copy-done.4, bf16[512,512]{1,0:T(8,128)(2,1)} %project.2.refs_0_), custom_call_target="tpu_custom_call" | custom-call | flops 1 | bytes 1 | tf_op jit(solution)/shard_map/cut/pallas_call | solution.py:70
  11.3 2.0 %collective-permute-start.3 = (bf16[512,512]{1,0:T(8,128)(2,1)}, bf16[512,512]{1,0:T(8,128)(2,1)}, u32[]{:S(2)}, u32[]{:S(2)}) collective-permute-start(bf16[512,512]{1,0:T(8,128)(2,1)} %project.2.refs_0_), channel_id=1, source_target_pairs={{0,1},{1,3},{2,0},{3,2},{4,5},{5,7},{6,4},{7,6},{8,9},{9,11},{10,8... | collective-permute-start | bytes 1572872 | tf_op jit(solution)/shard_map/ppermute | solution.py:86
  13.6 5.8 %project.3 = (bf16[512,512]{1,0:T(8,128)(2,1)S(1)}, bf16[512,512]{1,0:T(8,128)(2,1)S(1)}, bf16[512,512]{1,0:T(8,128)(2,1)S(1)}) custom-call(s32[3]{0:T(128)S(1)} %pad_add_fusion.1.shards_ref, bf16[512,2048]{1,0:T(8,128)(2,1)S(1)} %copy-done, bf16[2048,2048]{1,0:T(8,128)(2,1)} %w_ref.3, bf16[2,2048,128]{2,1,0:T(8,128)(2,1)} %cut.3.refs_0_), custom_call_target="tpu_custom_call" | custom-call | flops 1 | bytes 1 | tf_op jit(solution)/shard_map/project/pallas_call | solution.py:144
  21.1 1.5 %collective-permute-start.5 = (bf16[1,2048,128]{2,1,0:T(8,128)(2,1)S(1)}, bf16[1,2048,128]{2,1,0:T(8,128)(2,1)}, u32[]{:S(2)}, u32[]{:S(2)}) collective-permute-start(bf16[1,2048,128]{2,1,0:T(8,128)(2,1)S(1)} %gate.2.refs_6_), channel_id=1, source_target_pairs={{0,16},{16,0},{1,17},{17,1},{2,18},{18,2},{3,19},{19,3},{4,20},{20... | collective-permute-start | bytes 1572872 | tf_op jit(solution)/shard_map/ppermute | solution.py:90
  23.7 4.4 %collective-permute-start.7 = (bf16[512,512]{1,0:T(8,128)(2,1)}, bf16[512,512]{1,0:T(8,128)(2,1)}, u32[]{:S(2)}, u32[]{:S(2)}) collective-permute-start(bf16[512,512]{1,0:T(8,128)(2,1)} %copy-done.16), channel_id=1, source_target_pairs={{0,3},{3,0},{4,7},{7,4},{8,11},{11,8},{12,15},{15,12},{16,19},{19,... | collective-permute-start | bytes 1572872 | tf_op jit(solution)/shard_map/ppermute | solution.py:86
  28.2 1.6 %collective-permute-start.11 = (bf16[2,256,512]{2,1,0:T(8,128)(2,1)}, bf16[2,256,512]{2,1,0:T(8,128)(2,1)}, u32[]{:S(2)}, u32[]{:S(2)}) collective-permute-start(bf16[2,256,512]{2,1,0:T(8,128)(2,1)} %refs_8_.1), channel_id=1, source_target_pairs={{0,8},{4,12},{8,0},{12,4},{1,9},{5,13},{9,1},{13,5},{2,10},{6,14},... | collective-permute-start | bytes 1572872 | tf_op jit(solution)/shard_map/ppermute | solution.py:90
  29.8 1.3 %add_convert_fusion.refs_1_ = bf16[512,512]{1,0:T(8,128)(2,1)S(1)} fusion(bf16[512,512]{1,0:T(8,128)(2,1)} %collective-permute-done.3.refs_3_, bf16[512,512]{1,0:T(8,128)(2,1)} %copy-done.16), kind=kLoop, calls=%fused_computation | loop fusion | flops 1048576 | bytes 1572864 | tf_op jit(solution)/shard_map/convert_element_type | solution.py:94
  31.2 1.6 %copy-done.5 = bf16[2,2048,256]{2,1,0:T(8,128)(2,1)S(1)} copy-done((bf16[2,2048,256]{2,1,0:T(8,128)(2,1)S(1)}, bf16[2,2048,256]{2,1,0:T(8,128)(2,1)}, u32[]{:S(2)}) %copy-start.5) | copy-done | bytes 2097176
  32.7 4.2 %codes.3 = (f32[512,256]{1,0:T(8,128)S(1)}, f32[512,256]{1,0:T(8,128)S(1)}) custom-call(s32[2]{0:T(128)S(1)} %pad_add_fusion.ids_ref, bf16[512,2048]{1,0:T(8,128)(2,1)S(1)} %copy-done, s32[512,1]{1,0:T(8,128)S(1)} %copy.25.refs_1_.variant_ref, bf16[512,2048]{1,0:T(8,128)(2,1)} %collective-permute-done.refs_2_.refs_3_, ...), custom_call_target="tpu_custom_call" | custom-call | flops 1 | bytes 1 | tf_op jit(solution)/shard_map/codes/pallas_call | solution.py:195
  37.0 3.4 %copy-done.1 = bf16[512,16,512]{2,1,0:T(8,128)(2,1)S(1)} copy-done((bf16[512,16,512]{2,1,0:T(8,128)(2,1)S(1)}, bf16[512,16,512]{2,1,0:T(8,128)(2,1)}, u32[]{:S(2)}) %copy-start.1) | copy-done | bytes 8388632
  40.3 3.1 %cached.2 = (bf16[512,2048]{1,0:T(8,128)(2,1)S(1)}, f32[512,128]{1,0:T(8,128)S(1)}) custom-call(s32[512,1]{1,0:T(8,128)S(1)} %copy-done.12, bf16[512,2048]{1,0:T(8,128)(2,1)S(1)} %copy-done.6, bf16[512,16,512]{2,1,0:T(8,128)(2,1)S(1)} %copy-done.1, f32[512,256]{1,0:T(8,128)S(1)} %get-tuple-element.16.refs_0_.refs_2_, ...), custom_call_target="tpu_custom_call" | custom-call | flops 1 | bytes 1 | tf_op jit(solution)/shard_map/cached/pallas_call | solution.py:265
  43.5 1.3 %copy-done.8 = bf16[512,2048]{1,0:T(8,128)(2,1)} copy-done((bf16[512,2048]{1,0:T(8,128)(2,1)}, bf16[512,2048]{1,0:T(8,128)(2,1)S(1)}, u32[]{:S(2)}) %copy-start.8) | copy-done | bytes 2097176
  44.8 3.1 %codes.4 = (f32[512,128]{1,0:T(8,128)S(1)}, bf16[512,128]{1,0:T(8,128)(2,1)S(1)}) custom-call(s32[2]{0:T(128)S(1)} %pad_add_fusion.3.ids_ref, bf16[512,2048]{1,0:T(8,128)(2,1)S(1)} %copy-done, s32[512,1]{1,0:T(8,128)S(1)} %copy.25.refs_1_.variant_ref, f32[512,256]{1,0:T(8,128)S(1)} %get-tuple-element.16.refs_0_.refs_2_, ...), custom_call_target="tpu_custom_call" | custom-call | flops 1 | bytes 1 | tf_op jit(solution)/shard_map/codes/pallas_call | solution.py:195
  48.6 3.9 %codes.5 = (f32[512,128]{1,0:T(8,128)S(1)}, bf16[512,128]{1,0:T(8,128)(2,1)}) custom-call(s32[2]{0:T(128)S(1)} %pad_add_fusion.2.ids_ref, bf16[512,2048]{1,0:T(8,128)(2,1)S(1)} %copy-done, s32[512,1]{1,0:T(8,128)S(1)} %copy.25.refs_1_.variant_ref, f32[512,256]{1,0:T(8,128)S(1)} %get-tuple-element.16.refs_0_.refs_2_, ...), custom_call_target="tpu_custom_call" | custom-call | flops 1 | bytes 1 | tf_op jit(solution)/shard_map/codes/pallas_call | solution.py:195
  53.8 1.1 %collective-permute-done.6 = bf16[512,128]{1,0:T(8,128)(2,1)S(1)} collective-permute-done((bf16[512,128]{1,0:T(8,128)(2,1)}, bf16[512,128]{1,0:T(8,128)(2,1)S(1)}, u32[]{:S(2)}, u32[]{:S(2)}) %collective-permute-start.6) | collective-permute-done | bytes 131104 | tf_op jit(solution)/shard_map/ppermute | solution.py:90
  55.1 1.0 %add_convert_fusion.4.refs_0_ = bf16[512,128]{1,0:T(8,128)(2,1)S(1)} fusion(f32[512,128]{1,0:T(8,128)} %copy-done.18, bf16[512,128]{1,0:T(8,128)(2,1)S(1)} %collective-permute-done.6), kind=kLoop, calls=%fused_computation.5 | loop fusion | flops 196608 | bytes 524288 | tf_op jit(solution)/shard_map/convert_element_type | solution.py:94
  56.2 1.0 %collective-permute-start.12 = (bf16[512,512]{1,0:T(8,128)(2,1)S(1)}, bf16[512,512]{1,0:T(8,128)(2,1)S(1)}, u32[]{:S(2)}, u32[]{:S(2)}) collective-permute-start(bf16[512,512]{1,0:T(8,128)(2,1)S(1)} %copy-done.15), channel_id=1, source_target_pairs={{1,2},{2,1},{5,6},{6,5},{9,10},{10,9},{13,14},{14,13},{17,18},{18,... | collective-permute-start | bytes 1572872 | tf_op jit(solution)/shard_map/ppermute | solution.py:86
  57.7 4.2 %collective-permute-start.14 = (bf16[512,128]{1,0:T(8,128)(2,1)S(1)}, bf16[512,128]{1,0:T(8,128)(2,1)S(1)}, u32[]{:S(2)}, u32[]{:S(2)}) collective-permute-start(bf16[512,128]{1,0:T(8,128)(2,1)S(1)} %gate.3.refs_2_), channel_id=1, source_target_pairs={{0,1},{1,0},{2,3},{3,2},{4,5},{5,4},{6,7},{7,6},{8,9},{9,8},{10,11... | collective-permute-start | bytes 393224 | tf_op jit(solution)/shard_map/ppermute | solution.py:90
  61.8 1.0 %add_convert_fusion.3 = bf16[512,128]{1,0:T(8,128)(2,1)S(1)} fusion(f32[512,128]{1,0:T(8,128)} %copy-done.17, bf16[512,128]{1,0:T(8,128)(2,1)S(1)} %collective-permute-done.9), kind=kLoop, calls=%fused_computation.4 | loop fusion | flops 196608 | bytes 524288 | tf_op jit(solution)/shard_map/convert_element_type | solution.py:94
  62.9 3.2 %collective-permute-done.14 = bf16[512,128]{1,0:T(8,128)(2,1)S(1)} collective-permute-done((bf16[512,128]{1,0:T(8,128)(2,1)S(1)}, bf16[512,128]{1,0:T(8,128)(2,1)S(1)}, u32[]{:S(2)}, u32[]{:S(2)}) %collective-permute-start.14) | collective-permute-done | bytes 131104 | tf_op jit(solution)/shard_map/ppermute | solution.py:90
  66.1 2.4 %collective-permute-start.15 = (bf16[512,128]{1,0:T(8,128)(2,1)S(1)}, bf16[512,128]{1,0:T(8,128)(2,1)S(1)}, u32[]{:S(2)}, u32[]{:S(2)}) collective-permute-start(bf16[512,128]{1,0:T(8,128)(2,1)S(1)} %add_convert_fusion.1.refs_6_), channel_id=1, source_target_pairs={{0,2},{1,3},{2,0},{3,1},{4,6},{5,7},{6,4},{7,5},{8,10},{9,11},{10,... | collective-permute-start | bytes 393224 | tf_op jit(solution)/shard_map/ppermute | solution.py:90
  68.7 2.1 %collective-permute-start.13 = (bf16[512,128]{1,0:T(8,128)(2,1)S(1)}, bf16[512,128]{1,0:T(8,128)(2,1)S(1)}, u32[]{:S(2)}, u32[]{:S(2)}) collective-permute-start(bf16[512,128]{1,0:T(8,128)(2,1)S(1)} %add_convert_fusion.2.refs_3_.refs_4_), channel_id=1, source_target_pairs={{0,2},{1,3},{2,0},{3,1},{4,6},{5,7},{6,4},{7,5},{8,10},{9,11},{10,... | collective-permute-start | bytes 393224 | tf_op jit(solution)/shard_map/ppermute | solution.py:90
  70.9 1.1 %broadcast_select_fusion.refs_2_ = bf16[512,512]{1,0:T(8,128)(2,1)S(1)} fusion(bf16[512,512]{1,0:T(8,128)(2,1)} %collective-permute-done.7.refs_1_, bf16[512,512]{1,0:T(8,128)(2,1)S(1)} %collective-permute-done.12, pred[]{:T(512)S(6)} %or.3), kind=kLoop, calls=%fused_computation.1 | loop fusion | flops 262144 | bytes 1572865 | tf_op jit(solution)/shard_map/jit(_where)/select_n | solution.py:480
  72.0 3.4 %copy-done.2 = bf16[512,16,512]{2,1,0:T(8,128)(2,1)S(1)} copy-done((bf16[512,16,512]{2,1,0:T(8,128)(2,1)S(1)}, bf16[512,16,512]{2,1,0:T(8,128)(2,1)}, u32[]{:S(2)}) %copy-start.2) | copy-done | bytes 8388632
  75.4 3.1 %cached.3 = (bf16[512,2048]{1,0:T(8,128)(2,1)S(1)}, f32[512,128]{1,0:T(8,128)S(1)}) custom-call(s32[512,1]{1,0:T(8,128)S(1)} %copy-done.13, bf16[512,2048]{1,0:T(8,128)(2,1)S(1)} %copy-done.7, bf16[512,16,512]{2,1,0:T(8,128)(2,1)S(1)} %copy-done.2, bf16[512,2048]{1,0:T(8,128)(2,1)S(1)} %copy-done.9, ...), custom_call_target="tpu_custom_call", output_to_operand_aliasing={{0}: (3, {}), {1}: (4, {})} | custom-call | flops 1 | bytes 1 | tf_op jit(solution)/shard_map/cached/pallas_call | solution.py:265
  78.6 4.3 %collective-permute-done.15.refs_7_ = bf16[512,128]{1,0:T(8,128)(2,1)S(1)} collective-permute-done((bf16[512,128]{1,0:T(8,128)(2,1)S(1)}, bf16[512,128]{1,0:T(8,128)(2,1)S(1)}, u32[]{:S(2)}, u32[]{:S(2)}) %collective-permute-start.15) | collective-permute-done | bytes 131104 | tf_op jit(solution)/shard_map/ppermute | solution.py:90
  82.9 2.3 %collective-permute-done.13.refs_5_ = bf16[512,128]{1,0:T(8,128)(2,1)S(1)} collective-permute-done((bf16[512,128]{1,0:T(8,128)(2,1)S(1)}, bf16[512,128]{1,0:T(8,128)(2,1)S(1)}, u32[]{:S(2)}, u32[]{:S(2)}) %collective-permute-start.13) | collective-permute-done | bytes 131104 | tf_op jit(solution)/shard_map/ppermute | solution.py:90
  85.2 7.0 %finish.1 = (bf16[512,512]{1,0:T(8,128)(2,1)}, bf16[512,2048]{1,0:T(8,128)(2,1)}) custom-call(s32[8]{0:T(128)S(1)} %stack.69.ids_ref, s32[1]{0:T(128)} %bitcast.8.flag_ref, s32[512,1]{1,0:T(8,128)S(1)} %copy.25.refs_1_.variant_ref, bf16[512,2048]{1,0:T(8,128)(2,1)S(1)} %copy-done.7, bf16[512,2048]{1,0:T(8,128)(2,1)S(1)} %get-tuple-element.26.out1_ref, ...), custom_call_target="tpu_custom_call" | custom-call | flops 1 | bytes 1 | tf_op jit(solution)/shard_map/finish/pallas_call | solution.py:356
  (73 shorter events, 6.7 us)
Async XLA Ops:
  0.6 5.8 %copy-start = (bf16[512,2048]{1,0:T(8,128)(2,1)S(1)}, bf16[512,2048]{1,0:T(8,128)(2,1)}, u32[]{:S(2)}) copy-start(bf16[512,2048]{1,0:T(8,128)(2,1)} %refs_0_.5) | copy-start | bytes 6291460
  0.6 27.6 %collective-permute-start = (bf16[512,2048]{1,0:T(8,128)(2,1)}, bf16[512,2048]{1,0:T(8,128)(2,1)}, u32[]{:S(2)}, u32[]{:S(2)}) collective-permute-start(bf16[512,2048]{1,0:T(8,128)(2,1)} %refs_0_.5), channel_id=1, source_target_pairs={{0,4},{4,0},{8,12},{12,8},{1,5},{5,1},{9,13},{13,9},{2,6},{6,2},{1... | collective-permute-start | bytes 6291464 | tf_op jit(solution)/shard_map/ppermute | solution.py:90
  3.8 17.4 %collective-permute-start.2 = (bf16[1,2048,128]{2,1,0:T(8,128)(2,1)}, bf16[1,2048,128]{2,1,0:T(8,128)(2,1)S(1)}, u32[]{:S(2)}, u32[]{:S(2)}) collective-permute-start(bf16[1,2048,128]{2,1,0:T(8,128)(2,1)} %cut.2.refs_0_), channel_id=1, source_target_pairs={{0,8},{4,12},{8,0},{12,4},{1,9},{5,13},{9,1},{13,5},{2,10},{6,14},... | collective-permute-start | bytes 1572872 | tf_op jit(solution)/shard_map/ppermute | solution.py:90
  6.4 3.6 %copy-start.4 = (bf16[2,2048,256]{2,1,0:T(8,128)(2,1)S(1)}, bf16[2,2048,256]{2,1,0:T(8,128)(2,1)}, u32[]{:S(2)}) copy-start(bf16[2,2048,256]{2,1,0:T(8,128)(2,1)} %refs_4_.1) | copy-start | bytes 6291460
  10.0 3.4 %copy-start.20 = (s32[512,1]{0,1:T(1,128)S(1)}, s32[512,1]{0,1:T(1,128)}, u32[]{:S(2)}) copy-start(s32[512,1]{0,1:T(1,128)} %param.12) | copy-start | bytes 6148
  11.2 37.4 %collective-permute-start.4 = (bf16[2,2048,128]{2,1,0:T(8,128)(2,1)}, bf16[2,2048,128]{2,1,0:T(8,128)(2,1)}, u32[]{:S(2)}, u32[]{:S(2)}) collective-permute-start(bf16[2,2048,128]{2,1,0:T(8,128)(2,1)} %cut.3.refs_0_), channel_id=1, source_target_pairs={{0,8},{4,12},{8,0},{12,4},{1,9},{5,13},{9,1},{13,5},{2,10},{6,14},... | collective-permute-start | bytes 3145736 | tf_op jit(solution)/shard_map/ppermute | solution.py:90
  11.3 16.8 %collective-permute-start.3 = (bf16[512,512]{1,0:T(8,128)(2,1)}, bf16[512,512]{1,0:T(8,128)(2,1)}, u32[]{:S(2)}, u32[]{:S(2)}) collective-permute-start(bf16[512,512]{1,0:T(8,128)(2,1)} %project.2.refs_0_), channel_id=1, source_target_pairs={{0,1},{1,3},{2,0},{3,2},{4,5},{5,7},{6,4},{7,6},{8,9},{9,11},{10,8... | collective-permute-start | bytes 1572872 | tf_op jit(solution)/shard_map/ppermute | solution.py:86
  13.6 9.3 %copy-start.21 = (s32[512]{0:T(512)S(1)}, s32[512]{0:T(512)}, u32[]{:S(2)}) copy-start(s32[512]{0:T(512)} %param.11) | copy-start | bytes 6148
  13.6 10.1 %collective-permute-start.1 = (s32[512,1]{1,0:T(8,128)S(1)}, s32[512,1]{1,0:T(8,128)}, u32[]{:S(2)}, u32[]{:S(2)}) collective-permute-start(s32[512,1]{1,0:T(8,128)S(1)} %copy.25.refs_1_.variant_ref), channel_id=1, source_target_pairs={{0,4},{4,0},{8,12},{12,8},{1,5},{5,1},{9,13},{13,9},{2,6},{6,2},{1... | collective-permute-start | bytes 6152 | tf_op jit(solution)/shard_map/ppermute | solution.py:90
  21.1 23.7 %collective-permute-start.5 = (bf16[1,2048,128]{2,1,0:T(8,128)(2,1)S(1)}, bf16[1,2048,128]{2,1,0:T(8,128)(2,1)}, u32[]{:S(2)}, u32[]{:S(2)}) collective-permute-start(bf16[1,2048,128]{2,1,0:T(8,128)(2,1)S(1)} %gate.2.refs_6_), channel_id=1, source_target_pairs={{0,16},{16,0},{1,17},{17,1},{2,18},{18,2},{3,19},{19,3},{4,20},{20... | collective-permute-start | bytes 1572872 | tf_op jit(solution)/shard_map/ppermute | solution.py:90
  23.7 32.4 %collective-permute-start.7 = (bf16[512,512]{1,0:T(8,128)(2,1)}, bf16[512,512]{1,0:T(8,128)(2,1)}, u32[]{:S(2)}, u32[]{:S(2)}) collective-permute-start(bf16[512,512]{1,0:T(8,128)(2,1)} %copy-done.16), channel_id=1, source_target_pairs={{0,3},{3,0},{4,7},{7,4},{8,11},{11,8},{12,15},{15,12},{16,19},{19,... | collective-permute-start | bytes 1572872 | tf_op jit(solution)/shard_map/ppermute | solution.py:86
  28.1 29.5 %collective-permute-start.8 = (bf16[512,512]{1,0:T(8,128)(2,1)}, bf16[512,512]{1,0:T(8,128)(2,1)}, u32[]{:S(2)}, u32[]{:S(2)}) collective-permute-start(bf16[512,512]{1,0:T(8,128)(2,1)} %copy-done.19), channel_id=1, source_target_pairs={{0,1},{1,0},{2,3},{3,2},{4,5},{5,4},{6,7},{7,6},{8,9},{9,8},{10,11... | collective-permute-start | bytes 1572872 | tf_op jit(solution)/shard_map/ppermute | solution.py:90
  28.2 29.0 %collective-permute-start.11 = (bf16[2,256,512]{2,1,0:T(8,128)(2,1)}, bf16[2,256,512]{2,1,0:T(8,128)(2,1)}, u32[]{:S(2)}, u32[]{:S(2)}) collective-permute-start(bf16[2,256,512]{2,1,0:T(8,128)(2,1)} %refs_8_.1), channel_id=1, source_target_pairs={{0,8},{4,12},{8,0},{12,4},{1,9},{5,13},{9,1},{13,5},{2,10},{6,14},... | collective-permute-start | bytes 1572872 | tf_op jit(solution)/shard_map/ppermute | solution.py:90
  32.7 4.2 %copy-start.14 = (bf16[512,512]{1,0:T(8,128)(2,1)}, bf16[512,512]{1,0:T(8,128)(2,1)S(1)}, u32[]{:S(2)}) copy-start(bf16[512,512]{1,0:T(8,128)(2,1)S(1)} %add_convert_fusion.refs_1_) | copy-start | bytes 1572868
  32.7 4.2 %copy-start.6 = (bf16[512,2048]{1,0:T(8,128)(2,1)S(1)}, bf16[512,2048]{1,0:T(8,128)(2,1)}, u32[]{:S(2)}) copy-start(bf16[512,2048]{1,0:T(8,128)(2,1)} %q_ref.5) | copy-start | bytes 6291460
  32.7 4.2 %copy-start.12 = (s32[512,1]{1,0:T(8,128)S(1)}, s32[512,1]{1,0:T(8,128)}, u32[]{:S(2)}) copy-start(s32[512,1]{1,0:T(8,128)} %copy.24.len_ref) | copy-start | bytes 6148
  37.0 3.4 %copy-start.1 = (bf16[512,16,512]{2,1,0:T(8,128)(2,1)S(1)}, bf16[512,16,512]{2,1,0:T(8,128)(2,1)}, u32[]{:S(2)}) copy-start(bf16[512,16,512]{2,1,0:T(8,128)(2,1)} %kv_ref.3) | copy-start | bytes 25165828
  48.6 7.5 %copy-start.15 = (bf16[512,512]{1,0:T(8,128)(2,1)S(1)}, bf16[512,512]{1,0:T(8,128)(2,1)}, u32[]{:S(2)}) copy-start(bf16[512,512]{1,0:T(8,128)(2,1)} %copy-done.14) | copy-start | bytes 1572868
  53.2 1.7 %collective-permute-start.6 = (bf16[512,128]{1,0:T(8,128)(2,1)}, bf16[512,128]{1,0:T(8,128)(2,1)S(1)}, u32[]{:S(2)}, u32[]{:S(2)}) collective-permute-start(bf16[512,128]{1,0:T(8,128)(2,1)} %get-tuple-element.23), channel_id=1, source_target_pairs={{0,4},{4,0},{8,12},{12,8},{1,5},{5,1},{9,13},{13,9},{2,6},{6,2},{1... | collective-permute-start | bytes 393224 | tf_op jit(solution)/shard_map/ppermute | solution.py:90
  53.3 25.3 %collective-permute-start.16 = (bf16[2,256,512]{2,1,0:T(8,128)(2,1)}, bf16[2,256,512]{2,1,0:T(8,128)(2,1)}, u32[]{:S(2)}, u32[]{:S(2)}) collective-permute-start(bf16[2,256,512]{2,1,0:T(8,128)(2,1)} %refs_8_.1), channel_id=1, source_target_pairs={{0,4},{4,0},{8,12},{12,8},{1,5},{5,1},{9,13},{13,9},{2,6},{6,2},{1... | collective-permute-start | bytes 1572872 | tf_op jit(solution)/shard_map/ppermute | solution.py:90
  55.0 6.9 %collective-permute-start.9 = (bf16[512,128]{1,0:T(8,128)(2,1)S(1)}, bf16[512,128]{1,0:T(8,128)(2,1)S(1)}, u32[]{:S(2)}, u32[]{:S(2)}) collective-permute-start(bf16[512,128]{1,0:T(8,128)(2,1)S(1)} %get-tuple-element.21.refs_7_), channel_id=1, source_target_pairs={{0,4},{4,0},{8,12},{12,8},{1,5},{5,1},{9,13},{13,9},{2,6},{6,2},{1... | collective-permute-start | bytes 393224 | tf_op jit(solution)/shard_map/ppermute | solution.py:90
  55.1 16.9 %copy-start.11 = (f32[512,128]{1,0:T(8,128)S(1)}, f32[512,128]{1,0:T(8,128)}, u32[]{:S(2)}) copy-start(f32[512,128]{1,0:T(8,128)} %copy-done.10) | copy-start | bytes 786436
  55.1 16.9 %copy-start.13 = (s32[512,1]{1,0:T(8,128)S(1)}, s32[512,1]{1,0:T(8,128)}, u32[]{:S(2)}) copy-start(s32[512,1]{1,0:T(8,128)} %copy.24.len_ref) | copy-start | bytes 6148
  56.1 15.9 %copy-start.7 = (bf16[512,2048]{1,0:T(8,128)(2,1)S(1)}, bf16[512,2048]{1,0:T(8,128)(2,1)}, u32[]{:S(2)}) copy-start(bf16[512,2048]{1,0:T(8,128)(2,1)} %q_ref.5) | copy-start | bytes 6291460
  56.2 15.9 %copy-start.9 = (bf16[512,2048]{1,0:T(8,128)(2,1)S(1)}, bf16[512,2048]{1,0:T(8,128)(2,1)}, u32[]{:S(2)}) copy-start(bf16[512,2048]{1,0:T(8,128)(2,1)} %copy-done.8) | copy-start | bytes 6291460
  56.2 14.7 %collective-permute-start.12 = (bf16[512,512]{1,0:T(8,128)(2,1)S(1)}, bf16[512,512]{1,0:T(8,128)(2,1)S(1)}, u32[]{:S(2)}, u32[]{:S(2)}) collective-permute-start(bf16[512,512]{1,0:T(8,128)(2,1)S(1)} %copy-done.15), channel_id=1, source_target_pairs={{1,2},{2,1},{5,6},{6,5},{9,10},{10,9},{13,14},{14,13},{17,18},{18,... | collective-permute-start | bytes 1572872 | tf_op jit(solution)/shard_map/ppermute | solution.py:86
  57.2 21.4 %collective-permute-start.17 = (bf16[2,256,512]{2,1,0:T(8,128)(2,1)}, bf16[2,256,512]{2,1,0:T(8,128)(2,1)S(1)}, u32[]{:S(2)}, u32[]{:S(2)}) collective-permute-start(bf16[2,256,512]{2,1,0:T(8,128)(2,1)} %collective-permute-done.11.refs_4_.refs_9_), channel_id=1, source_target_pairs={{0,4},{4,0},{8,12},{12,8},{1,5},{5,1},{9,13},{13,9},{2,6},{6,2},{1... | collective-permute-start | bytes 1572872 | tf_op jit(solution)/shard_map/ppermute | solution.py:90
  57.7 8.4 %collective-permute-start.14 = (bf16[512,128]{1,0:T(8,128)(2,1)S(1)}, bf16[512,128]{1,0:T(8,128)(2,1)S(1)}, u32[]{:S(2)}, u32[]{:S(2)}) collective-permute-start(bf16[512,128]{1,0:T(8,128)(2,1)S(1)} %gate.3.refs_2_), channel_id=1, source_target_pairs={{0,1},{1,0},{2,3},{3,2},{4,5},{5,4},{6,7},{7,6},{8,9},{9,8},{10,11... | collective-permute-start | bytes 393224 | tf_op jit(solution)/shard_map/ppermute | solution.py:90
  62.8 5.9 %collective-permute-start.10 = (bf16[512,128]{1,0:T(8,128)(2,1)S(1)}, bf16[512,128]{1,0:T(8,128)(2,1)S(1)}, u32[]{:S(2)}, u32[]{:S(2)}) collective-permute-start(bf16[512,128]{1,0:T(8,128)(2,1)S(1)} %add_convert_fusion.3), channel_id=1, source_target_pairs={{0,1},{1,0},{2,3},{3,2},{4,5},{5,4},{6,7},{7,6},{8,9},{9,8},{10,11... | collective-permute-start | bytes 393224 | tf_op jit(solution)/shard_map/ppermute | solution.py:90
  66.1 16.8 %collective-permute-start.15 = (bf16[512,128]{1,0:T(8,128)(2,1)S(1)}, bf16[512,128]{1,0:T(8,128)(2,1)S(1)}, u32[]{:S(2)}, u32[]{:S(2)}) collective-permute-start(bf16[512,128]{1,0:T(8,128)(2,1)S(1)} %add_convert_fusion.1.refs_6_), channel_id=1, source_target_pairs={{0,2},{1,3},{2,0},{3,1},{4,6},{5,7},{6,4},{7,5},{8,10},{9,11},{10,... | collective-permute-start | bytes 393224 | tf_op jit(solution)/shard_map/ppermute | solution.py:90
  68.7 16.4 %collective-permute-start.13 = (bf16[512,128]{1,0:T(8,128)(2,1)S(1)}, bf16[512,128]{1,0:T(8,128)(2,1)S(1)}, u32[]{:S(2)}, u32[]{:S(2)}) collective-permute-start(bf16[512,128]{1,0:T(8,128)(2,1)S(1)} %add_convert_fusion.2.refs_3_.refs_4_), channel_id=1, source_target_pairs={{0,2},{1,3},{2,0},{3,1},{4,6},{5,7},{6,4},{7,5},{8,10},{9,11},{10,... | collective-permute-start | bytes 393224 | tf_op jit(solution)/shard_map/ppermute | solution.py:90
  72.0 3.4 %copy-start.2 = (bf16[512,16,512]{2,1,0:T(8,128)(2,1)S(1)}, bf16[512,16,512]{2,1,0:T(8,128)(2,1)}, u32[]{:S(2)}) copy-start(bf16[512,16,512]{2,1,0:T(8,128)(2,1)} %kv_ref.3) | copy-start | bytes 25165828
  (8 other events, 10.8 us)

commit v3 on v2

v3 whole, which is shorter than its diff:
```python
import functools

import jax
import jax.numpy as jnp
from jax import lax
from jax.experimental import pallas as pl
from jax.experimental.pallas import tpu as pltpu
from jax.sharding import PartitionSpec as P

HEAD = 128
BF16 = jnp.bfloat16
F32 = jnp.float32
ANY = pl.BlockSpec(memory_space=pl.ANY)
WHOLE = pl.BlockSpec(memory_space=pltpu.VMEM)
SCALARS = pl.BlockSpec(memory_space=pltpu.SMEM)


def params(mib):
    return pltpu.CompilerParams(vmem_limit_bytes=mib << 20)


def brief():
    return pl.CostEstimate(flops=1, bytes_accessed=1, transcendentals=0)


def gate(value, after):
    def body(*refs):
        del refs

    return pl.pallas_call(
        body,
        out_shape=jax.ShapeDtypeStruct(value.shape, value.dtype),
        in_specs=[ANY] * (1 + len(after)),
        out_specs=ANY,
        input_output_aliases={0: 0},
        compiler_params=params(16),
        cost_estimate=brief(),
        name="gate",
    )(value, *after)


def in_vmem(shape, dtype):
    return pltpu.VMEM(shape, dtype)


def in_hbm(value):
    return pltpu.with_memory_space_constraint(value, pltpu.HBM)


def cut(value, takes, after):
    depth, rank = value.shape[1:]
    half = rank // 2
    pieces = 2
    block = depth // pieces

    def body(first_ref, value_ref, *refs):
        outs, sems = refs[len(after) : -1], refs[-1]
        loads = []
        for n, (out_ref, (_, count, column)) in enumerate(zip(outs, takes)):
            for i in range(count):
                for k in range(pieces):
                    lines = pl.ds(k * block, block)
                    loads.append(
                        pltpu.make_async_copy(
                            value_ref.at[first_ref[n] + i, lines, pl.ds(column * half, half)],
                            out_ref.at[i, lines],
                            sems.at[n, i, k],
                        )
                    )
        for load in loads:
            load.start()
        for load in loads:
            load.wait()

    return pl.pallas_call(
        body,
        out_shape=[in_vmem((count, depth, half), value.dtype) for _, count, _ in takes],
        in_specs=[SCALARS] + [ANY] * (1 + len(after)),
        out_specs=[WHOLE] * len(takes),
        scratch_shapes=[
            pltpu.SemaphoreType.DMA((len(takes), max(count for _, count, _ in takes), pieces))
        ],
        compiler_params=params(16),
        cost_estimate=brief(),
        name="cut",
    )(jnp.stack([jnp.int32(first) for first, _, _ in takes]), in_hbm(value), *after)


def swap(value, axis, bit):
    return lax.ppermute(value, axis, [(i, i ^ bit) for i in range(lax.axis_size(axis))])


def added(terms):
    return sum(term.astype(F32) for term in terms).astype(BF16)


def project(tokens, weight, shards, width, after, down=None, takes=(), near_adds=()):
    rows, depth = tokens.shape
    count = len(shards)
    pieces = 4
    block = depth // pieces
    extra = 1 if takes else 0

    def body(scalars_ref, x_ref, w_ref, *refs):
        down_ref = refs[0] if extra else None
        refs = refs[extra + len(after) :]
        outs, cuts = refs[:count], refs[count : count + len(takes)]
        held, made, load_sems, store_sems = refs[count + len(takes) :][:4]
        scratch = refs[count + len(takes) + 4 :]
        loads = [
            [
                pltpu.make_async_copy(
                    w_ref.at[
                        pl.ds(k * block, block),
                        pl.ds(pl.multiple_of(scalars_ref[i] * width, width), width),
                    ],
                    held.at[i, pl.ds(k * block, block)],
                    load_sems.at[i, k],
                )
                for k in range(pieces)
            ]
            for i in range(count)
        ]
        stores = [
            pltpu.make_async_copy(made.at[i], outs[i], store_sems.at[i])
            for i in range(count)
            if i not in near_adds
        ]
        cut_in, cut_out = [], []
        for n, (_, size, column) in enumerate(takes):
            spot, sems = scratch[n], scratch[len(takes)]
            half = spot.shape[2]
            start = scalars_ref[count + n]
            cut_in.append(
                pltpu.make_async_copy(
                    down_ref.at[pl.ds(start, size), :, pl.ds(column * half, half)],
                    spot,
                    sems.at[n, 0],
                )
            )
            cut_out.append(pltpu.make_async_copy(spot, cuts[n], sems.at[n, 1]))
        for copy in cut_in[:1]:
            copy.start()
        for group in loads:
            for load in group:
                load.start()
        for copy in cut_in[1:]:
            copy.start()
        for i in range(count):
            if i == 0:
                total = jnp.zeros((rows, width), F32)
                for k in range(pieces):
                    loads[0][k].wait()
                    part = slice(k * block, (k + 1) * block)
                    total = total + jnp.dot(
                        x_ref[:, part], held[0, part], preferred_element_type=F32
                    )
                result = total.astype(BF16)
            else:
                for k in range(pieces):
                    loads[i][k].wait()
                result = jnp.dot(x_ref[...], held[i], preferred_element_type=F32).astype(BF16)
            if i in near_adds:
                outs[i][...] = result
            else:
                made[i] = result
                stores[sum(1 for n in range(i) if n not in near_adds)].start()
            if i == 0:
                for copy, out in zip(cut_in, cut_out):
                    copy.wait()
                    out.start()
        for store in stores + cut_out:
            store.wait()

    shapes = [
        (in_vmem if i in near_adds else pltpu.HBM)((rows, width), BF16) for i in range(count)
    ]
    scratch = [
        pltpu.VMEM((count, depth, width), BF16),
        pltpu.VMEM((count, rows, width), BF16),
        pltpu.SemaphoreType.DMA((count, pieces)),
        pltpu.SemaphoreType.DMA((count,)),
    ]
    operands = [tokens, in_hbm(weight)]
    scalars = list(shards)
    if extra:
        operands.append(in_hbm(down))
        for first, size, _ in takes:
            piece = (size, depth, down.shape[2] // 2)
            shapes.append(pltpu.HBM(piece, BF16))
            scratch.append(pltpu.VMEM(piece, BF16))
            scalars.append(first)
        scratch.append(pltpu.SemaphoreType.DMA((len(takes), 2)))
    return pl.pallas_call(
        body,
        out_shape=shapes,
        in_specs=[SCALARS, WHOLE] + [ANY] * (1 + extra + len(after)),
        out_specs=[WHOLE if i in near_adds else ANY for i in range(len(shapes))],
        scratch_shapes=scratch,
        compiler_params=params(20),
        cost_estimate=brief(),
        name="project",
    )(jnp.stack([jnp.int32(n) for n in scalars]), *operands, *after)


def near_codes(tokens, variant, near, near_variant, down, ids, after):
    rows, depth = tokens.shape
    count, _, rank = down.shape
    chunk = 256

    def body(ids_ref, x_ref, variant_ref, near_ref, near_variant_ref, down_ref, *refs):
        out_ref, near_out_ref, kept_ref, held, sems = refs[-5:]
        loads = [
            pltpu.make_async_copy(down_ref.at[j], held.at[j], sems.at[j]) for j in range(count)
        ]
        copy = pltpu.make_async_copy(near_ref, kept_ref, sems.at[count])
        loads[0].start()
        copy.start()
        for load in loads[1:]:
            load.start()
        for j in range(count):
            loads[j].wait()
            for source, named, result in (
                (x_ref, variant_ref, out_ref),
                (kept_ref, near_variant_ref, near_out_ref),
            ):
                if j == 0 and source is kept_ref:
                    copy.wait()
                for row in range(0, rows, chunk):
                    here = slice(row, row + chunk)
                    product = jnp.dot(source[here], held[j], preferred_element_type=F32)
                    other = result[here] if j > 0 else jnp.zeros_like(product)
                    result[here] = jnp.where(named[here] == ids_ref[j], product, other)

    return pl.pallas_call(
        body,
        out_shape=[
            in_vmem((rows, rank), F32),
            in_vmem((rows, rank), F32),
            in_vmem((rows, depth), BF16),
        ],
        in_specs=[SCALARS, WHOLE, WHOLE, ANY, WHOLE, ANY] + [ANY] * len(after),
        out_specs=[WHOLE] * 3,
        scratch_shapes=[
            pltpu.VMEM(down.shape, BF16),
            pltpu.SemaphoreType.DMA((count + 1,)),
        ],
        compiler_params=params(20),
        cost_estimate=brief(),
        name="near_codes",
    )(ids.astype(jnp.int32), tokens, variant, in_hbm(near), near_variant, in_hbm(down), *after)


def codes(sets, weights, ids, column, dtypes, after, fetch=False):
    depth, width = weights[0].shape[1:]
    sizes = [w.shape[0] for w in weights]
    has_start = [start is not None for _, _, start in sets]
    pair = max(1, 256 // width)
    chunk = 256

    def body(ids_ref, *refs):
        refs = list(refs)
        inputs = []
        for started in has_start:
            inputs.append([refs.pop(0) for _ in range(3 if started else 2)])
        flat = [w.at[j] for w, size in zip(refs[: len(sizes)], sizes) for j in range(size)]
        if fetch:
            kept_ref, sem = refs[-2:]
            copy = pltpu.make_async_copy(inputs[-1][0], kept_ref, sem)
            copy.start()
            inputs[-1][0] = kept_ref
            refs = refs[:-2]
        outs = refs[-len(sets) :]
        groups = [flat[at : at + pair] for at in range(0, len(flat), pair)]
        for n, (out_ref, given) in enumerate(zip(outs, inputs)):
            if fetch and n == len(sets) - 1:
                copy.wait()
            for row in range(0, out_ref.shape[0], chunk):
                here = slice(row, row + chunk)
                x, variant = given[0][here], given[1][here]
                if len(given) == 3:
                    kept = given[2][here, column : column + width]
                else:
                    kept = jnp.zeros((x.shape[0], width), F32)
                for g, group in enumerate(groups):
                    w = jnp.concatenate([entry[...] for entry in group], axis=1)
                    product = jnp.dot(x, w, preferred_element_type=F32)
                    for j in range(len(group)):
                        mine = variant == ids_ref[g * pair + j]
                        kept = jnp.where(mine, product[:, j * width : (j + 1) * width], kept)
                out_ref[here] = kept.astype(out_ref.dtype)

    operands, specs = [], []
    for n, (tokens, variant, start) in enumerate(sets):
        last = fetch and n == len(sets) - 1
        operands += [in_hbm(tokens) if last else tokens, variant]
        specs += [ANY if last else WHOLE, WHOLE]
        if start is not None:
            operands.append(start)
            specs.append(WHOLE)
    shapes = [
        in_vmem((tokens.shape[0], width), dtype) for (tokens, _, _), dtype in zip(sets, dtypes)
    ]
    if fetch:
        shapes.append(in_vmem(sets[-1][0].shape, BF16))
    return pl.pallas_call(
        body,
        out_shape=shapes,
        in_specs=[SCALARS] + specs + [WHOLE] * len(weights) + [ANY] * len(after),
        out_specs=[WHOLE] * len(shapes),
        scratch_shapes=[pltpu.SemaphoreType.DMA(())] if fetch else [],
        compiler_params=params(20),
        cost_estimate=brief(),
        name="codes",
    )(ids.astype(jnp.int32), *operands, *weights, *after)


def cached(queries, kv_cache, lengths, first, rows, after):
    features = queries.shape[1]
    positions, width = kv_cache.shape[1:]
    kv_local = width // (2 * HEAD)
    group = features // HEAD // kv_local
    scale = HEAD ** (-0.5)
    near = 128 // positions
    block = 64
    blocks = rows // block

    def body(len_ref, q_ref, kv_ref, *refs):
        out_ref, lse_ref, held, sems = refs[-4:]
        loads = []
        for b in range(blocks):
            lines = pl.ds(b * block, block)
            source = kv_ref.at[pl.ds(first + b * block, block)]
            loads.append(pltpu.make_async_copy(source, held.at[lines], sems.at[b]))
            loads[-1].start()
        lane = lax.broadcasted_iota(jnp.int32, (near, 128), 1)
        sublane = lax.broadcasted_iota(jnp.int32, (near, 128), 0)
        same = lane // positions == sublane
        at = lane % positions
        ones = jnp.ones((128, HEAD), BF16)

        def part(base):
            here = pl.ds(base, 2 * near)
            there = pl.ds(first + base, 2 * near)
            lines = [pl.ds(base + half * near, near) for half in range(2)]
            seen = [
                same & (at < len_ref[pl.ds((first + base) // near + half, 1), :])
                for half in range(2)
            ]
            table = [jnp.zeros((near, 128), F32) for _ in range(2)]
            for g in range(kv_local):
                at_key, at_value = 2 * g * HEAD, (2 * g + 1) * HEAD
                keys = held[here, :, at_key : at_key + HEAD].reshape(256, HEAD)
                values = held[here, :, at_value : at_value + HEAD].reshape(256, HEAD)
                heads = [slice((g * group + h) * HEAD, (g * group + h + 1) * HEAD) for h in range(group)]
                query = jnp.concatenate([q_ref[there, columns] for columns in heads], axis=0)
                scores = lax.dot_general(
                    query, keys, (((1,), (1,)), ((), ())), preferred_element_type=F32
                ).reshape(group, 2, near, 256)
                results = []
                for half in range(2):
                    own = scores[:, half, :, half * 128 : (half + 1) * 128] * scale
                    own = jnp.where(seen[half][None], own, jnp.float32(-1e30))
                    largest = jnp.max(own, axis=-1, keepdims=True)
                    weight = jnp.exp(own - largest).astype(BF16).reshape(group * near, 128)
                    value = jnp.concatenate([values[half * 128 : (half + 1) * 128], ones], axis=1)
                    mixed = jnp.dot(weight, value, preferred_element_type=F32)
                    total = mixed[:, HEAD:]
                    results.append((mixed[:, :HEAD] / total).reshape(group, near, HEAD))
                    lse = largest + jnp.log(total).reshape(group, near, 128)
                    for h in range(group):
                        table[half] = jnp.where(lane == g * group + h, lse[h], table[half])
                both = jnp.stack(results, axis=1).reshape(group, 2 * near, HEAD).astype(BF16)
                for h, columns in enumerate(heads):
                    out_ref[here, columns] = both[h]
            for half in range(2):
                lse_ref[lines[half], :] = table[half]

        def step(b, carry):
            lines = pl.ds(pl.multiple_of(b * block, block), block)
            pltpu.make_async_copy(kv_ref.at[lines], held.at[lines], sems.at[b]).wait()
            for base in range(0, block, 2 * near):
                part(pl.multiple_of(b * block + base, 2 * near))
            return carry

        lax.fori_loop(0, blocks, step, 0)

    return pl.pallas_call(
        body,
        out_shape=[in_vmem((rows, features), BF16), in_vmem((rows, 128), F32)],
        in_specs=[WHOLE, WHOLE, ANY] + [ANY] * len(after),
        out_specs=[WHOLE, WHOLE],
        scratch_shapes=[
            pltpu.VMEM((rows,) + kv_cache.shape[1:], BF16),
            pltpu.SemaphoreType.DMA((blocks,)),
        ],
        compiler_params=params(20),
        cost_estimate=brief(),
        name="cached",
    )(lengths, queries, in_hbm(kv_cache), *after)


def gather_up(terms, flags, ups, after):
    sizes = [up.shape[0] for up in ups]

    def body(flags_ref, *refs):
        term_refs, up_refs = refs[: len(terms)], refs[len(terms) : len(terms) + len(ups)]
        base_ref, up_ref, sems = refs[-3:]
        copies, at = [], 0
        for n, size in enumerate(sizes):
            copies.append(
                pltpu.make_async_copy(up_refs[n], up_ref.at[pl.ds(at, size)], sems.at[n])
            )
            copies[-1].start()
            at += size
        total = jnp.zeros(base_ref.shape, F32)
        for n, term_ref in enumerate(term_refs):
            total = total + jnp.where(flags_ref[n] == 1, term_ref[...].astype(F32), 0.0)
        base_ref[...] = total
        for copy in copies:
            copy.wait()

    return pl.pallas_call(
        body,
        out_shape=[
            in_vmem(terms[0].shape, F32),
            in_vmem((sum(sizes),) + ups[0].shape[1:], BF16),
        ],
        in_specs=[SCALARS] + [WHOLE] * len(terms) + [ANY] * (len(ups) + len(after)),
        out_specs=[WHOLE, WHOLE],
        scratch_shapes=[pltpu.SemaphoreType.DMA((len(ups),))],
        compiler_params=params(20),
        cost_estimate=brief(),
        name="gather_up",
    )(jnp.stack([jnp.int32(flag) for flag in flags]), *terms, *ups, *after)


def finish(variant_ids, queries, ranges, base, codes_a, codes_b, up, ids):
    rows, features = queries.shape
    width = base.shape[1]
    heads = features // HEAD
    group = features * 2 // width
    chunk = 128
    scale = HEAD ** (-0.5)
    counts = [len(codes_a), len(codes_b)]
    firsts = [0]
    for out1, _ in ranges:
        firsts.append(firsts[-1] + out1.shape[0])

    def body(ids_ref, variant_ref, q_ref, base_ref, up_ref, *refs):
        refs = list(refs)
        done = [(refs.pop(0), refs.pop(0)) for _ in ranges]
        a_refs, b_refs = refs[: counts[0]], refs[counts[0] : counts[0] + counts[1]]
        fresh_ref, attended_ref, fresh_made, attended_made, sems = refs[-5:]
        ones = jnp.ones((2 * HEAD, HEAD), BF16)

        def total(parts, here):
            result = parts[0][here].astype(F32)
            for part in parts[1:]:
                result = result + part[here].astype(F32)
            return result

        stores = []
        for at in range(0, rows, chunk):
            here = slice(at, at + chunk)
            which = max(n for n in range(len(ranges)) if firsts[n] <= at)
            out1_ref, lse_ref = done[which]
            inner = slice(at - firsts[which], at - firsts[which] + chunk)
            variant = variant_ref[here]
            code = jnp.concatenate(
                [total(a_refs, here).astype(BF16), total(b_refs, here).astype(BF16)], axis=1
            )
            masked = [
                jnp.where(variant == ids_ref[entry], code, jnp.zeros_like(code))
                for entry in range(up_ref.shape[0])
            ]
            change = jnp.dot(
                jnp.concatenate(masked, axis=1),
                up_ref[...].reshape(-1, width),
                preferred_element_type=F32,
            )
            fresh = (base_ref[here] + change.astype(BF16).astype(F32)).astype(BF16)
            fresh_made[here] = fresh
            keys, values = [], []
            for g in range(width // (2 * HEAD)):
                keys.append(fresh[:, 2 * g * HEAD : (2 * g + 1) * HEAD].astype(F32))
                values.append(fresh[:, (2 * g + 1) * HEAD : (2 * g + 2) * HEAD].astype(F32))
            for h in range(heads):
                columns = slice(h * HEAD, (h + 1) * HEAD)
                product = q_ref[here, columns].astype(F32) * keys[h // group]
                high = product.astype(BF16)
                low = (product - high.astype(F32)).astype(BF16)
                score = jnp.dot(
                    jnp.concatenate([high, low], axis=1), ones, preferred_element_type=F32
                )
                weight = 1.0 / (1.0 + jnp.exp(lse_ref[inner, h : h + 1] - score * scale))
                old = out1_ref[inner, columns].astype(F32)
                moved = old + weight * (values[h // group] - old)
                attended_made[here, columns] = moved.astype(BF16)
            for k, (made, ref) in enumerate(
                ((fresh_made, fresh_ref), (attended_made, attended_ref))
            ):
                lines = pl.ds(at, chunk)
                stores.append(
                    pltpu.make_async_copy(made.at[lines], ref.at[lines], sems.at[k, at // chunk])
                )
                stores[-1].start()
        for store in stores:
            store.wait()

    operands = [variant_ids, queries, base, up]
    for pieces in ranges:
        operands += pieces
    operands += [*codes_a, *codes_b]
    return pl.pallas_call(
        body,
        out_shape=[
            jax.ShapeDtypeStruct((rows, width), BF16),
            jax.ShapeDtypeStruct((rows, features), BF16),
        ],
        in_specs=[SCALARS] + [WHOLE] * len(operands),
        out_specs=[ANY, ANY],
        scratch_shapes=[
            pltpu.VMEM((rows, width), BF16),
            pltpu.VMEM((rows, features), BF16),
            pltpu.SemaphoreType.DMA((2, rows // chunk)),
        ],
        compiler_params=params(20),
        cost_estimate=brief(),
        name="finish",
    )(ids.astype(jnp.int32), *operands)


def all_reduce(value, after=()):
    size = lax.axis_size("tensor")
    bit = 1
    terms = [value]
    while bit < size:
        if len(terms) > 1:
            terms = [added(terms)]
            if after:
                terms = [gate(terms[0], after)]
        terms.append(swap(terms[0], "tensor", bit))
        bit *= 2
    return terms


def reduce_parts(parts):
    size = lax.axis_size("tensor")
    parts = {t: [part] for t, part in parts.items()}
    bit = 1
    while bit < size:
        for t in range(size - 1, 0, -1):
            if t & bit and t & (bit - 1) == 0:
                total = parts[t][0] if len(parts[t]) == 1 else added(parts[t])
                parts[t ^ bit].append(swap(total, "tensor", bit))
        bit *= 2
    return parts[0]


def general(tokens, queries, kv_cache, lengths, variant_ids, base_weight, delta_down, delta_up):
    size, me = lax.axis_size("tensor"), lax.axis_index("tensor")
    width = base_weight.shape[1] // size
    owners = lax.axis_size("adapter")
    variants, _, rank = delta_down.shape
    half = rank // 2
    every = lax.all_gather(delta_down, "adapter", axis=0, tiled=True)
    up = lax.all_gather(delta_up, "adapter", axis=0, tiled=True)
    order = sorted(range(size), key=lambda t: (-(t & 1), -t))
    parts = project(tokens, base_weight, [me ^ t for t in order], width, [])
    base_terms = reduce_parts(dict(zip(order, parts)))
    ids = jnp.arange(owners * variants, dtype=jnp.int32)
    rows_of = [(tokens, variant_ids, None)]
    codes_a, codes_b = [
        all_reduce(codes(rows_of, [every[:, :, at : at + half]], ids, 0, [BF16], parts[:1])[0])
        for at in (0, half)
    ]
    ranges = [cached(queries, kv_cache, lengths, 0, tokens.shape[0], parts[:1])]
    base, up = gather_up(base_terms, [1] * len(base_terms), [up], [])
    return finish(variant_ids, queries, ranges, base, codes_a, codes_b, up, ids)


def paired(tokens, queries, kv_cache, lengths, variant_ids, base_weight, delta_down, delta_up):
    me = lax.axis_index("tensor")
    mine = lax.axis_index("adapter")
    group = lax.axis_index("groups")
    width = base_weight.shape[1] // 4

    rows = tokens.shape[0]
    half = delta_down.shape[2] // 2
    near = swap(tokens, "adapter", 1)
    near_ids = swap(variant_ids, "adapter", 1)
    (first,) = cut(delta_down, [(group, 1, 0)], [])
    from_y = swap(first, "adapter", 2)
    part_3, second = project(
        tokens, base_weight, [me ^ 3], width, [first], delta_down, [(0, 2, 1)]
    )
    got_3 = swap(part_3, "tensor", 1)
    far = swap(second, "adapter", 2)
    part_1, part_2, own = project(
        tokens, base_weight, [me ^ 1, me ^ 2, me], width, [part_3]
    )
    got_1 = swap(part_1, "tensor", 1)
    from_y = gate(from_y, [own])
    from_x = swap(from_y, "groups", 1)
    start, start_near, near = near_codes(
        tokens,
        variant_ids,
        near,
        near_ids,
        delta_down,
        jnp.stack([2 * mine, 2 * mine + 1]),
        [own, from_y, lengths],
    )
    sum_2 = added([part_2, got_3])
    got_2 = swap(sum_2, "tensor", 2)
    lane = 2 * (mine ^ 2)
    both = [(tokens, variant_ids, start), (near, near_ids, start_near)]
    a, a_near = codes(
        both, [from_y, from_x], jnp.stack([lane + group, lane + 1 - group]), 0, [F32, BF16], [start]
    )
    b, b_near = codes(
        both, [far], jnp.stack([lane, lane + 1]), half, [F32, BF16], [a_near]
    )
    a = added([a, swap(a_near, "adapter", 1)])
    b = added([b, swap(b_near, "adapter", 1)])
    b = gate(b, [got_1, got_2])
    codes_a = all_reduce(a)
    early = cached(queries, kv_cache, lengths, 0, 128, [b])
    codes_b = all_reduce(b, [early[1]])
    late = cached(
        queries, kv_cache, lengths, 128, rows - 128, [early[1], codes_a[0], codes_b[0]]
    )
    ups = [delta_up] + [swap(delta_up, "adapter", bit) for bit in (2, 1, 3)]
    ids = jnp.stack([2 * (mine ^ bit) + j for bit in (0, 2, 1, 3) for j in (0, 1)])
    base, up = gather_up([own, got_1, got_2], [1, 1, 1], ups, [late[1], codes_b[0]])
    return finish(variant_ids, queries, [early, late], base, codes_a, codes_b, up, ids)


def local(tokens, queries, kv_cache, kv_lengths, variant_ids, base_weight, delta_down, delta_up):
    sizes = [lax.axis_size(axis) for axis in ("groups", "adapter", "tensor")]
    plan = paired if sizes == [2, 4, 4] and delta_down.shape[0] == 2 else general
    return tuple(
        plan(
            tokens,
            queries,
            kv_cache,
            jnp.repeat(kv_lengths, kv_cache.shape[1]).reshape(-1, 128),
            variant_ids,
            base_weight,
            delta_down,
            delta_up,
        )
    )


def solution(mesh):
    return jax.shard_map(
        local,
        mesh=mesh,
        in_specs=(
            P(("groups", "adapter"), "tensor"),
            P(("groups", "adapter"), "tensor"),
            P(("groups", "adapter"), None, "tensor"),
            P(("groups", "adapter")),
            P(("groups", "adapter"), None),
            P("tensor", None),
            P("adapter", "tensor", None),
            P("adapter", None, "tensor"),
        ),
        out_specs=(P(("groups", "adapter"), "tensor"), P(("groups", "adapter"), "tensor")),
        check_vma=False,
    )
```

time: 92.8 us -> 77.4 us (0.83)
  local copies, waits for them, and re-layouts: 15.6 us -> 2.56 us
  starting transfers between devices: 23.7 us -> 18.5 us
  waiting for transfers between devices: 11.1 us -> 13.9 us
  Pallas kernels: 36 us -> 38.2 us
  other arithmetic: 4.83 us -> 2.67 us
    unnamed x45 -> x19, local copies, waits for them, and re-layouts: 14.6 us -> 2.25 us
    ppermute x3 -> x0, starting transfers between devices: 7.42 us -> none  [permute(): return lax.ppermute(value, axis, pairs)]
    pallas_call x9, Pallas kernels: 29 us -> 32.4 us  [the longest x2 10.8 us: project(): pl.pallas_call(body, out_shape=shapes, in_specs=[SCALARS, WHOLE] + [ANY]...]
    ppermute x15 -> x17, waiting for transfers between devices: 11.1 us -> 13.9 us  [swap(): lax.ppermute(value, axis, [(i, i ^ bit) for i in range(lax.axis_size(axis...]
    ppermute x15 -> x17, starting transfers between devices: 16.3 us -> 18.5 us  [swap(): lax.ppermute(value, axis, [(i, i ^ bit) for i in range(lax.axis_size(axis...]
    convert_element_type x5, other arithmetic: 3.43 us -> 2.27 us  [added(): return sum((term.astype(F32) for term in terms)).astype(BF16)]
    select_n x1 -> x0, other arithmetic: 1.1 us -> none  [paired(): got_b = jnp.where(ends, got_b1, got_b2)]
    pallas_call x1, Pallas kernels: 6.97 us -> 5.88 us  [finish(): pl.pallas_call(body, out_shape=[jax.ShapeDtypeStruct((rows, width), BF16)...]
  transfers between devices with their start and end apart: 18 -> 17, of which waited for: 5 -> 7; matrix products, arithmetic and copies ran while one was open for 6% -> 4% of each run, Pallas kernels for 31% -> 42%
where the time goes in v3:
time: 77.4 us; the launch traced here: 76.9 us
  Pallas kernels  38.2 us (49%)
  starting transfers between devices  18.5 us (24%)
  waiting for transfers between devices  13.9 us (18%)
  other arithmetic  2.67 us (3%)
  local copies, waits for them, and re-layouts  2.56 us (3%)
  between operations  1.06 us (1%)
    ppermute x17, starting transfers between devices, swap(): lax.ppermute(value, axis, [(i, i ^ bit) for i in range(lax.axis_size(axis...  18.5 us
    ppermute x17, waiting for transfers between devices, swap(): lax.ppermute(value, axis, [(i, i ^ bit) for i in range(lax.axis_size(axis...  13.9 us
    pallas_call x2, Pallas kernels, project(): pl.pallas_call(body, out_shape=shapes, in_specs=[SCALARS, WHOLE] + [ANY]...  10.8 us
    pallas_call x2, Pallas kernels, cached(): pl.pallas_call(body, out_shape=[in_vmem((rows, features), BF16), in_vmem(...  7.71 us
    pallas_call x1, Pallas kernels, finish(): pl.pallas_call(body, out_shape=[jax.ShapeDtypeStruct((rows, width), BF16)...  5.88 us
    pallas_call x2, Pallas kernels, codes(): pl.pallas_call(body, out_shape=shapes, in_specs=[SCALARS] + specs + [WHOL...  4.99 us
    pallas_call x1, Pallas kernels, near_codes(): pl.pallas_call(body, out_shape=[in_vmem((rows, rank), F32), in_vmem((rows...  4.91 us
    pallas_call x1, Pallas kernels, gather_up(): pl.pallas_call(body, out_shape=[in_vmem(terms[0].shape, F32), in_vmem((su...  2.76 us
  transfers between devices with their start and end apart: 17, of which 7 were waited for; matrix products, arithmetic and copies ran while one was open for 4% of the time, Pallas kernels for 42%

profile of v3, /device:TPU:0, one launch (start us, length us, event | category | flops | bytes accessed | tf_op | source)
XLA Modules:
  0.0 76.9 jit_solution(12629313975126377190)
XLA Ops:
  0.6 0.5 collective-permute-start.6
  1.2 1.1 %cut.1.refs_1_ = bf16[1,2048,128]{2,1,0:T(8,128)(2,1)S(1)} custom-call(s32[1]{0:T(128)} %bitcast.12.first_ref, bf16[2,2048,256]{2,1,0:T(8,128)(2,1)} %down_ref.1), custom_call_target="tpu_custom_call" | custom-call | flops 1 | bytes 1 | tf_op jit(solution)/shard_map/cut/pallas_call | solution.py:75
  2.3 2.6 %collective-permute-start.8 = (bf16[1,2048,128]{2,1,0:T(8,128)(2,1)S(1)}, bf16[1,2048,128]{2,1,0:T(8,128)(2,1)S(1)}, u32[]{:S(2)}, u32[]{:S(2)}) collective-permute-start(bf16[1,2048,128]{2,1,0:T(8,128)(2,1)S(1)} %cut.1.refs_1_), channel_id=1, source_target_pairs={{0,8},{4,12},{8,0},{12,4},{1,9},{5,13},{9,1},{13,5},{2,10},{6,14},... | collective-permute-start | bytes 1572872 | tf_op jit(solution)/shard_map/ppermute | solution.py:90
  5.0 4.3 %project.2 = (bf16[512,512]{1,0:T(8,128)(2,1)}, bf16[2,2048,128]{2,1,0:T(8,128)(2,1)}) custom-call(s32[2]{0:T(128)S(1)} %pad_add_fusion.1.scalars_ref, bf16[512,2048]{1,0:T(8,128)(2,1)S(1)} %copy-done, bf16[2048,2048]{1,0:T(8,128)(2,1)} %w_ref.3, bf16[2,2048,256]{2,1,0:T(8,128)(2,1)} %down_ref.1, bf16[1,2048,128]{2,1,0:T(8,128)(2,1)S(1)} %cut.1.refs_1_), custom_call_target="tpu_custom_call" | custom-call | flops 1 | bytes 1 | tf_op jit(solution)/shard_map/project/pallas_call | solution.py:194
  9.3 0.4 collective-permute-start.9
  9.7 1.8 %collective-permute-start.1 = (bf16[512,512]{1,0:T(8,128)(2,1)}, bf16[512,512]{1,0:T(8,128)(2,1)}, u32[]{:S(2)}, u32[]{:S(2)}) collective-permute-start(bf16[512,512]{1,0:T(8,128)(2,1)} %get-tuple-element.20.refs_0_), channel_id=1, source_target_pairs={{0,1},{1,0},{2,3},{3,2},{4,5},{5,4},{6,7},{7,6},{8,9},{9,8},{10,11... | collective-permute-start | bytes 1572872 | tf_op jit(solution)/shard_map/ppermute | solution.py:90
  11.7 1.0 %copy-done.6 = bf16[512,512]{1,0:T(8,128)(2,1)S(1)} copy-done((bf16[512,512]{1,0:T(8,128)(2,1)S(1)}, bf16[512,512]{1,0:T(8,128)(2,1)}, u32[]{:S(2)}) %copy-start.6) | copy-done | bytes 524312
  12.8 6.5 %project.3 = (bf16[512,512]{1,0:T(8,128)(2,1)}, bf16[512,512]{1,0:T(8,128)(2,1)}, bf16[512,512]{1,0:T(8,128)(2,1)}) custom-call(s32[3]{0:T(128)S(1)} %pad_add_fusion.scalars_ref, bf16[512,2048]{1,0:T(8,128)(2,1)S(1)} %copy-done, bf16[2048,2048]{1,0:T(8,128)(2,1)} %w_ref.3, bf16[512,512]{1,0:T(8,128)(2,1)S(1)} %copy-done.6), custom_call_target="tpu_custom_call" | custom-call | flops 1 | bytes 1 | tf_op jit(solution)/shard_map/project/pallas_call | solution.py:194
  19.4 1.0 %copy-done.2 = bf16[512,512]{1,0:T(8,128)(2,1)S(1)} copy-done((bf16[512,512]{1,0:T(8,128)(2,1)S(1)}, bf16[512,512]{1,0:T(8,128)(2,1)}, u32[]{:S(2)}) %copy-start.2) | copy-done | bytes 524312
  20.4 1.5 %collective-permute-start.10 = (bf16[1,2048,128]{2,1,0:T(8,128)(2,1)S(1)}, bf16[1,2048,128]{2,1,0:T(8,128)(2,1)}, u32[]{:S(2)}, u32[]{:S(2)}) collective-permute-start(bf16[1,2048,128]{2,1,0:T(8,128)(2,1)S(1)} %gate.3.refs_1_.refs_6_), channel_id=1, source_target_pairs={{0,16},{16,0},{1,17},{17,1},{2,18},{18,2},{3,19},{19,3},{4,20},{20... | collective-permute-start | bytes 1572872 | tf_op jit(solution)/shard_map/ppermute | solution.py:90
  22.0 1.7 %collective-permute-done.1 = bf16[512,512]{1,0:T(8,128)(2,1)} collective-permute-done((bf16[512,512]{1,0:T(8,128)(2,1)}, bf16[512,512]{1,0:T(8,128)(2,1)}, u32[]{:S(2)}, u32[]{:S(2)}) %collective-permute-start.1) | collective-permute-done | bytes 524320 | tf_op jit(solution)/shard_map/ppermute | solution.py:90
  23.7 1.7 %collective-permute-start = (bf16[512,512]{1,0:T(8,128)(2,1)}, bf16[512,512]{1,0:T(8,128)(2,1)}, u32[]{:S(2)}, u32[]{:S(2)}) collective-permute-start(bf16[512,512]{1,0:T(8,128)(2,1)} %get-tuple-element.22), channel_id=1, source_target_pairs={{0,1},{1,0},{2,3},{3,2},{4,5},{5,4},{6,7},{7,6},{8,9},{9,8},{10,11... | collective-permute-start | bytes 1572872 | tf_op jit(solution)/shard_map/ppermute | solution.py:90
  25.4 2.1 %add_convert_fusion = bf16[512,512]{1,0:T(8,128)(2,1)} fusion(bf16[512,512]{1,0:T(8,128)(2,1)} %collective-permute-done.1, bf16[512,512]{1,0:T(8,128)(2,1)} %get-tuple-element.23), kind=kLoop, calls=%fused_computation | loop fusion | flops 1048576 | bytes 1572864 | tf_op jit(solution)/shard_map/convert_element_type | solution.py:94
  27.5 2.6 %collective-permute-start.2 = (bf16[512,512]{1,0:T(8,128)(2,1)}, bf16[512,512]{1,0:T(8,128)(2,1)}, u32[]{:S(2)}, u32[]{:S(2)}) collective-permute-start(bf16[512,512]{1,0:T(8,128)(2,1)} %add_convert_fusion), channel_id=1, source_target_pairs={{0,2},{1,3},{2,0},{3,1},{4,6},{5,7},{6,4},{7,5},{8,10},{9,11},{10,... | collective-permute-start | bytes 1572872 | tf_op jit(solution)/shard_map/ppermute | solution.py:90
  30.5 4.9 %near_codes.1 = (f32[512,256]{1,0:T(8,128)S(1)}, f32[512,256]{1,0:T(8,128)S(1)}, bf16[512,2048]{1,0:T(8,128)(2,1)S(1)}) custom-call(s32[2]{0:T(128)S(1)} %pad_add_fusion.3.ids_ref, bf16[512,2048]{1,0:T(8,128)(2,1)S(1)} %copy-done, s32[512,1]{1,0:T(8,128)S(1)} %copy.26.variant_ref.refs_1_, bf16[512,2048]{1,0:T(8,128)(2,1)} %collective-permute-done.6.near_ref, ...), custom_call_target="tpu_custom_call" | custom-call | flops 1 | bytes 1 | tf_op jit(solution)/shard_map/near_codes/pallas_call | solution.py:235
  35.5 2.4 %codes.2 = (f32[512,128]{1,0:T(8,128)S(1)}, bf16[512,128]{1,0:T(8,128)(2,1)S(1)}) custom-call(s32[2]{0:T(128)S(1)} %pad_add_fusion.4.ids_ref, bf16[512,2048]{1,0:T(8,128)(2,1)S(1)} %copy-done, s32[512,1]{1,0:T(8,128)S(1)} %copy.26.variant_ref.refs_1_, f32[512,256]{1,0:T(8,128)S(1)} %get-tuple-element.24.refs_2_.refs_8_, ...), custom_call_target="tpu_custom_call" | custom-call | flops 1 | bytes 1 | tf_op jit(solution)/shard_map/codes/pallas_call | solution.py:306
  37.9 2.1 %collective-permute-done.9.refs_6_ = bf16[2,2048,128]{2,1,0:T(8,128)(2,1)} collective-permute-done((bf16[2,2048,128]{2,1,0:T(8,128)(2,1)}, bf16[2,2048,128]{2,1,0:T(8,128)(2,1)}, u32[]{:S(2)}, u32[]{:S(2)}) %collective-permute-start.9) | collective-permute-done | bytes 1048608 | tf_op jit(solution)/shard_map/ppermute | solution.py:90
  40.0 2.6 %codes.3 = (f32[512,128]{1,0:T(8,128)S(1)}, bf16[512,128]{1,0:T(8,128)(2,1)S(1)}) custom-call(s32[2]{0:T(128)S(1)} %pad_add_fusion.2.ids_ref, bf16[512,2048]{1,0:T(8,128)(2,1)S(1)} %copy-done, s32[512,1]{1,0:T(8,128)S(1)} %copy.26.variant_ref.refs_1_, f32[512,256]{1,0:T(8,128)S(1)} %get-tuple-element.24.refs_2_.refs_8_, ...), custom_call_target="tpu_custom_call" | custom-call | flops 1 | bytes 1 | tf_op jit(solution)/shard_map/codes/pallas_call | solution.py:306
  42.7 1.8 %collective-permute-start.3 = (bf16[2,256,512]{2,1,0:T(8,128)(2,1)}, bf16[2,256,512]{2,1,0:T(8,128)(2,1)}, u32[]{:S(2)}, u32[]{:S(2)}) collective-permute-start(bf16[2,256,512]{2,1,0:T(8,128)(2,1)} %refs_3_.1), channel_id=1, source_target_pairs={{0,8},{4,12},{8,0},{12,4},{1,9},{5,13},{9,1},{13,5},{2,10},{6,14},... | collective-permute-start | bytes 1572872 | tf_op jit(solution)/shard_map/ppermute | solution.py:90
  44.6 0.3 collective-permute-start.12
  45.0 0.8 collective-permute-done.refs_1_
  46.0 6.7 %collective-permute-done.2.refs_2_ = bf16[512,512]{1,0:T(8,128)(2,1)} collective-permute-done((bf16[512,512]{1,0:T(8,128)(2,1)}, bf16[512,512]{1,0:T(8,128)(2,1)}, u32[]{:S(2)}, u32[]{:S(2)}) %collective-permute-start.2) | collective-permute-done | bytes 524320 | tf_op jit(solution)/shard_map/ppermute | solution.py:90
  52.7 2.1 %collective-permute-start.13 = (bf16[512,128]{1,0:T(8,128)(2,1)S(1)}, bf16[512,128]{1,0:T(8,128)(2,1)S(1)}, u32[]{:S(2)}, u32[]{:S(2)}) collective-permute-start(bf16[512,128]{1,0:T(8,128)(2,1)S(1)} %add_convert_fusion.3), channel_id=1, source_target_pairs={{0,1},{1,0},{2,3},{3,2},{4,5},{5,4},{6,7},{7,6},{8,9},{9,8},{10,11... | collective-permute-start | bytes 393224 | tf_op jit(solution)/shard_map/ppermute | solution.py:90
  54.7 2.5 %cached.2 = (bf16[128,2048]{1,0:T(8,128)(2,1)S(1)}, f32[128,128]{1,0:T(8,128)S(1)}) custom-call(s32[64,128]{1,0:T(8,128)S(1)} %copy.25.refs_2_.len_ref, bf16[512,2048]{1,0:T(8,128)(2,1)S(1)} %copy-done.1, bf16[512,16,512]{2,1,0:T(8,128)(2,1)} %kv_ref.3, bf16[512,128]{1,0:T(8,128)(2,1)S(1)} %gate.4.refs_0_), custom_call_target="tpu_custom_call" | custom-call | flops 1 | bytes 1 | tf_op jit(solution)/shard_map/cached/pallas_call | solution.py:388
  57.3 0.3 collective-permute-done.14
  57.6 1.0 %collective-permute-start.16 = (bf16[512,128]{1,0:T(8,128)(2,1)S(1)}, bf16[512,128]{1,0:T(8,128)(2,1)S(1)}, u32[]{:S(2)}, u32[]{:S(2)}) collective-permute-start(bf16[512,128]{1,0:T(8,128)(2,1)S(1)} %gate.5.refs_2_.refs_8_.refs_6_), channel_id=1, source_target_pairs={{0,2},{1,3},{2,0},{3,1},{4,6},{5,7},{6,4},{7,5},{8,10},{9,11},{10,... | collective-permute-start | bytes 393224 | tf_op jit(solution)/shard_map/ppermute | solution.py:90
  58.6 1.4 %collective-permute-done.13 = bf16[512,128]{1,0:T(8,128)(2,1)S(1)} collective-permute-done((bf16[512,128]{1,0:T(8,128)(2,1)S(1)}, bf16[512,128]{1,0:T(8,128)(2,1)S(1)}, u32[]{:S(2)}, u32[]{:S(2)}) %collective-permute-start.13) | collective-permute-done | bytes 131104 | tf_op jit(solution)/shard_map/ppermute | solution.py:90
  60.0 1.7 %collective-permute-start.15 = (bf16[512,128]{1,0:T(8,128)(2,1)S(1)}, bf16[512,128]{1,0:T(8,128)(2,1)}, u32[]{:S(2)}, u32[]{:S(2)}) collective-permute-start(bf16[512,128]{1,0:T(8,128)(2,1)S(1)} %add_convert_fusion.2.refs_1_.refs_4_), channel_id=1, source_target_pairs={{0,2},{1,3},{2,0},{3,1},{4,6},{5,7},{6,4},{7,5},{8,10},{9,11},{10,... | collective-permute-start | bytes 393224 | tf_op jit(solution)/shard_map/ppermute | solution.py:90
  61.8 5.2 %cached.3 = (bf16[384,2048]{1,0:T(8,128)(2,1)S(1)}, f32[384,128]{1,0:T(8,128)S(1)}) custom-call(s32[64,128]{1,0:T(8,128)S(1)} %copy.25.refs_2_.len_ref, bf16[512,2048]{1,0:T(8,128)(2,1)S(1)} %copy-done.1, bf16[512,16,512]{2,1,0:T(8,128)(2,1)} %kv_ref.3, f32[128,128]{1,0:T(8,128)S(1)} %get-tuple-element.31.refs_1_.refs_0_, ...), custom_call_target="tpu_custom_call" | custom-call | flops 1 | bytes 1 | tf_op jit(solution)/shard_map/cached/pallas_call | solution.py:388
  67.0 1.1 %collective-permute-done.5.refs_6_ = bf16[2,256,512]{2,1,0:T(8,128)(2,1)} collective-permute-done((bf16[2,256,512]{2,1,0:T(8,128)(2,1)}, bf16[2,256,512]{2,1,0:T(8,128)(2,1)}, u32[]{:S(2)}, u32[]{:S(2)}) %collective-permute-start.5) | collective-permute-done | bytes 524320 | tf_op jit(solution)/shard_map/ppermute | solution.py:90
  68.1 2.8 %gather_up.1 = (f32[512,512]{1,0:T(8,128)S(1)}, bf16[8,256,512]{2,1,0:T(8,128)(2,1)S(1)}) custom-call(s32[3]{0:T(128)S(1)} %broadcast_1_flags_ref.2.flags_ref, bf16[512,512]{1,0:T(8,128)(2,1)S(1)} %copy-done.3, bf16[512,512]{1,0:T(8,128)(2,1)} %collective-permute-done.refs_1_, bf16[512,512]{1,0:T(8,128)(2,1)} %collective-permute-done.2.refs_2_, ...), custom_call_target="tpu_custom_call" | custom-call | flops 1 | bytes 1 | tf_op jit(solution)/shard_map/gather_up/pallas_call | solution.py:423
  70.9 5.9 %finish.1 = (bf16[512,512]{1,0:T(8,128)(2,1)}, bf16[512,2048]{1,0:T(8,128)(2,1)}) custom-call(s32[8]{0:T(128)S(1)} %stack.75.ids_ref, s32[512,1]{1,0:T(8,128)S(1)} %copy.26.variant_ref.refs_1_, bf16[512,2048]{1,0:T(8,128)(2,1)S(1)} %copy-done.1, f32[512,512]{1,0:T(8,128)S(1)} %get-tuple-element.34.base_ref, ...), custom_call_target="tpu_custom_call" | custom-call | flops 1 | bytes 1 | tf_op jit(solution)/shard_map/finish/pallas_call | solution.py:515
  (50 shorter events, 1.5 us)
Async XLA Ops:
  0.6 4.4 %copy-start = (bf16[512,2048]{1,0:T(8,128)(2,1)S(1)}, bf16[512,2048]{1,0:T(8,128)(2,1)}, u32[]{:S(2)}) copy-start(bf16[512,2048]{1,0:T(8,128)(2,1)} %refs_0_.5) | copy-start | bytes 6291460
  0.6 29.9 %collective-permute-start.6 = (bf16[512,2048]{1,0:T(8,128)(2,1)}, bf16[512,2048]{1,0:T(8,128)(2,1)}, u32[]{:S(2)}, u32[]{:S(2)}) collective-permute-start(bf16[512,2048]{1,0:T(8,128)(2,1)} %refs_0_.5), channel_id=1, source_target_pairs={{0,4},{4,0},{8,12},{12,8},{1,5},{5,1},{9,13},{13,9},{2,6},{6,2},{1... | collective-permute-start | bytes 6291464 | tf_op jit(solution)/shard_map/ppermute | solution.py:90
  2.3 17.0 %collective-permute-start.8 = (bf16[1,2048,128]{2,1,0:T(8,128)(2,1)S(1)}, bf16[1,2048,128]{2,1,0:T(8,128)(2,1)S(1)}, u32[]{:S(2)}, u32[]{:S(2)}) collective-permute-start(bf16[1,2048,128]{2,1,0:T(8,128)(2,1)S(1)} %cut.1.refs_1_), channel_id=1, source_target_pairs={{0,8},{4,12},{8,0},{12,4},{1,9},{5,13},{9,1},{13,5},{2,10},{6,14},... | collective-permute-start | bytes 1572872 | tf_op jit(solution)/shard_map/ppermute | solution.py:90
  5.0 6.5 %copy-start.7 = (s32[512,1]{0,1:T(1,128)S(1)}, s32[512,1]{0,1:T(1,128)}, u32[]{:S(2)}) copy-start(s32[512,1]{0,1:T(1,128)} %param.12) | copy-start | bytes 6148
  9.3 30.6 %collective-permute-start.9 = (bf16[2,2048,128]{2,1,0:T(8,128)(2,1)}, bf16[2,2048,128]{2,1,0:T(8,128)(2,1)}, u32[]{:S(2)}, u32[]{:S(2)}) collective-permute-start(bf16[2,2048,128]{2,1,0:T(8,128)(2,1)} %get-tuple-element.27), channel_id=1, source_target_pairs={{0,8},{4,12},{8,0},{12,4},{1,9},{5,13},{9,1},{13,5},{2,10},{6,14},... | collective-permute-start | bytes 3145736 | tf_op jit(solution)/shard_map/ppermute | solution.py:90
  9.7 14.0 %collective-permute-start.1 = (bf16[512,512]{1,0:T(8,128)(2,1)}, bf16[512,512]{1,0:T(8,128)(2,1)}, u32[]{:S(2)}, u32[]{:S(2)}) collective-permute-start(bf16[512,512]{1,0:T(8,128)(2,1)} %get-tuple-element.20.refs_0_), channel_id=1, source_target_pairs={{0,1},{1,0},{2,3},{3,2},{4,5},{5,4},{6,7},{7,6},{8,9},{9,8},{10,11... | collective-permute-start | bytes 1572872 | tf_op jit(solution)/shard_map/ppermute | solution.py:90
  11.7 15.8 %collective-permute-start.7 = (s32[512,1]{1,0:T(8,128)S(1)}, s32[512,1]{1,0:T(8,128)}, u32[]{:S(2)}, u32[]{:S(2)}) collective-permute-start(s32[512,1]{1,0:T(8,128)S(1)} %copy.26.variant_ref.refs_1_), channel_id=1, source_target_pairs={{0,4},{4,0},{8,12},{12,8},{1,5},{5,1},{9,13},{13,9},{2,6},{6,2},{1... | collective-permute-start | bytes 6152 | tf_op jit(solution)/shard_map/ppermute | solution.py:90
  11.7 1.0 %copy-start.6 = (bf16[512,512]{1,0:T(8,128)(2,1)S(1)}, bf16[512,512]{1,0:T(8,128)(2,1)}, u32[]{:S(2)}) copy-start(bf16[512,512]{1,0:T(8,128)(2,1)} %get-tuple-element.20.refs_0_) | copy-start | bytes 1572868
  19.3 10.9 %copy-start.8 = (s32[512]{0:T(512)S(1)}, s32[512]{0:T(512)}, u32[]{:S(2)}) copy-start(s32[512]{0:T(512)} %param.11) | copy-start | bytes 6148
  19.4 1.0 %copy-start.2 = (bf16[512,512]{1,0:T(8,128)(2,1)S(1)}, bf16[512,512]{1,0:T(8,128)(2,1)}, u32[]{:S(2)}) copy-start(bf16[512,512]{1,0:T(8,128)(2,1)} %get-tuple-element.21.refs_1_.refs_0_) | copy-start | bytes 1572868
  20.4 10.1 %copy-start.3 = (bf16[512,512]{1,0:T(8,128)(2,1)S(1)}, bf16[512,512]{1,0:T(8,128)(2,1)}, u32[]{:S(2)}) copy-start(bf16[512,512]{1,0:T(8,128)(2,1)} %get-tuple-element.21.refs_1_.refs_0_) | copy-start | bytes 1572868
  20.4 15.1 %collective-permute-start.10 = (bf16[1,2048,128]{2,1,0:T(8,128)(2,1)S(1)}, bf16[1,2048,128]{2,1,0:T(8,128)(2,1)}, u32[]{:S(2)}, u32[]{:S(2)}) collective-permute-start(bf16[1,2048,128]{2,1,0:T(8,128)(2,1)S(1)} %gate.3.refs_1_.refs_6_), channel_id=1, source_target_pairs={{0,16},{16,0},{1,17},{17,1},{2,18},{18,2},{3,19},{19,3},{4,20},{20... | collective-permute-start | bytes 1572872 | tf_op jit(solution)/shard_map/ppermute | solution.py:90
  23.7 22.1 %collective-permute-start = (bf16[512,512]{1,0:T(8,128)(2,1)}, bf16[512,512]{1,0:T(8,128)(2,1)}, u32[]{:S(2)}, u32[]{:S(2)}) collective-permute-start(bf16[512,512]{1,0:T(8,128)(2,1)} %get-tuple-element.22), channel_id=1, source_target_pairs={{0,1},{1,0},{2,3},{3,2},{4,5},{5,4},{6,7},{7,6},{8,9},{9,8},{10,11... | collective-permute-start | bytes 1572872 | tf_op jit(solution)/shard_map/ppermute | solution.py:90
  27.5 25.1 %collective-permute-start.2 = (bf16[512,512]{1,0:T(8,128)(2,1)}, bf16[512,512]{1,0:T(8,128)(2,1)}, u32[]{:S(2)}, u32[]{:S(2)}) collective-permute-start(bf16[512,512]{1,0:T(8,128)(2,1)} %add_convert_fusion), channel_id=1, source_target_pairs={{0,2},{1,3},{2,0},{3,1},{4,6},{5,7},{6,4},{7,5},{8,10},{9,11},{10,... | collective-permute-start | bytes 1572872 | tf_op jit(solution)/shard_map/ppermute | solution.py:90
  42.6 12.2 %copy-start.1 = (bf16[512,2048]{1,0:T(8,128)(2,1)S(1)}, bf16[512,2048]{1,0:T(8,128)(2,1)}, u32[]{:S(2)}) copy-start(bf16[512,2048]{1,0:T(8,128)(2,1)} %q_ref.5) | copy-start | bytes 6291460
  42.6 2.1 %collective-permute-start.11 = (bf16[512,128]{1,0:T(8,128)(2,1)S(1)}, bf16[512,128]{1,0:T(8,128)(2,1)S(1)}, u32[]{:S(2)}, u32[]{:S(2)}) collective-permute-start(bf16[512,128]{1,0:T(8,128)(2,1)S(1)} %get-tuple-element.30), channel_id=1, source_target_pairs={{0,4},{4,0},{8,12},{12,8},{1,5},{5,1},{9,13},{13,9},{2,6},{6,2},{1... | collective-permute-start | bytes 393224 | tf_op jit(solution)/shard_map/ppermute | solution.py:90
  42.7 24.4 %collective-permute-start.3 = (bf16[2,256,512]{2,1,0:T(8,128)(2,1)}, bf16[2,256,512]{2,1,0:T(8,128)(2,1)}, u32[]{:S(2)}, u32[]{:S(2)}) collective-permute-start(bf16[2,256,512]{2,1,0:T(8,128)(2,1)} %refs_3_.1), channel_id=1, source_target_pairs={{0,8},{4,12},{8,0},{12,4},{1,9},{5,13},{9,1},{13,5},{2,10},{6,14},... | collective-permute-start | bytes 1572872 | tf_op jit(solution)/shard_map/ppermute | solution.py:90
  44.5 22.6 %collective-permute-start.4 = (bf16[2,256,512]{2,1,0:T(8,128)(2,1)}, bf16[2,256,512]{2,1,0:T(8,128)(2,1)}, u32[]{:S(2)}, u32[]{:S(2)}) collective-permute-start(bf16[2,256,512]{2,1,0:T(8,128)(2,1)} %refs_3_.1), channel_id=1, source_target_pairs={{0,4},{4,0},{8,12},{12,8},{1,5},{5,1},{9,13},{13,9},{2,6},{6,2},{1... | collective-permute-start | bytes 1572872 | tf_op jit(solution)/shard_map/ppermute | solution.py:90
  44.6 8.0 %collective-permute-start.12 = (bf16[512,128]{1,0:T(8,128)(2,1)S(1)}, bf16[512,128]{1,0:T(8,128)(2,1)S(1)}, u32[]{:S(2)}, u32[]{:S(2)}) collective-permute-start(bf16[512,128]{1,0:T(8,128)(2,1)S(1)} %get-tuple-element.28.refs_7_), channel_id=1, source_target_pairs={{0,4},{4,0},{8,12},{12,8},{1,5},{5,1},{9,13},{13,9},{2,6},{6,2},{1... | collective-permute-start | bytes 393224 | tf_op jit(solution)/shard_map/ppermute | solution.py:90
  45.8 22.3 %collective-permute-start.5 = (bf16[2,256,512]{2,1,0:T(8,128)(2,1)}, bf16[2,256,512]{2,1,0:T(8,128)(2,1)}, u32[]{:S(2)}, u32[]{:S(2)}) collective-permute-start(bf16[2,256,512]{2,1,0:T(8,128)(2,1)} %refs_3_.1), channel_id=1, source_target_pairs={{0,12},{4,8},{8,4},{12,0},{1,13},{5,9},{9,5},{13,1},{2,14},{6,10},... | collective-permute-start | bytes 1572872 | tf_op jit(solution)/shard_map/ppermute | solution.py:90
  52.6 5.0 %collective-permute-start.14 = (bf16[512,128]{1,0:T(8,128)(2,1)S(1)}, bf16[512,128]{1,0:T(8,128)(2,1)S(1)}, u32[]{:S(2)}, u32[]{:S(2)}) collective-permute-start(bf16[512,128]{1,0:T(8,128)(2,1)S(1)} %gate.4.refs_0_), channel_id=1, source_target_pairs={{0,1},{1,0},{2,3},{3,2},{4,5},{5,4},{6,7},{7,6},{8,9},{9,8},{10,11... | collective-permute-start | bytes 393224 | tf_op jit(solution)/shard_map/ppermute | solution.py:90
  52.7 7.3 %collective-permute-start.13 = (bf16[512,128]{1,0:T(8,128)(2,1)S(1)}, bf16[512,128]{1,0:T(8,128)(2,1)S(1)}, u32[]{:S(2)}, u32[]{:S(2)}) collective-permute-start(bf16[512,128]{1,0:T(8,128)(2,1)S(1)} %add_convert_fusion.3), channel_id=1, source_target_pairs={{0,1},{1,0},{2,3},{3,2},{4,5},{5,4},{6,7},{7,6},{8,9},{9,8},{10,11... | collective-permute-start | bytes 393224 | tf_op jit(solution)/shard_map/ppermute | solution.py:90
  57.3 2.7 %copy-start.4 = (bf16[128,2048]{1,0:T(8,128)(2,1)}, bf16[128,2048]{1,0:T(8,128)(2,1)S(1)}, u32[]{:S(2)}) copy-start(bf16[128,2048]{1,0:T(8,128)(2,1)S(1)} %get-tuple-element.36.refs_0_) | copy-start | bytes 1572868
  57.6 13.2 %collective-permute-start.16 = (bf16[512,128]{1,0:T(8,128)(2,1)S(1)}, bf16[512,128]{1,0:T(8,128)(2,1)S(1)}, u32[]{:S(2)}, u32[]{:S(2)}) collective-permute-start(bf16[512,128]{1,0:T(8,128)(2,1)S(1)} %gate.5.refs_2_.refs_8_.refs_6_), channel_id=1, source_target_pairs={{0,2},{1,3},{2,0},{3,1},{4,6},{5,7},{6,4},{7,5},{8,10},{9,11},{10,... | collective-permute-start | bytes 393224 | tf_op jit(solution)/shard_map/ppermute | solution.py:90
  60.0 10.8 %collective-permute-start.15 = (bf16[512,128]{1,0:T(8,128)(2,1)S(1)}, bf16[512,128]{1,0:T(8,128)(2,1)}, u32[]{:S(2)}, u32[]{:S(2)}) collective-permute-start(bf16[512,128]{1,0:T(8,128)(2,1)S(1)} %add_convert_fusion.2.refs_1_.refs_4_), channel_id=1, source_target_pairs={{0,2},{1,3},{2,0},{3,1},{4,6},{5,7},{6,4},{7,5},{8,10},{9,11},{10,... | collective-permute-start | bytes 393224 | tf_op jit(solution)/shard_map/ppermute | solution.py:90
  67.0 3.9 %copy-start.5 = (bf16[128,2048]{1,0:T(8,128)(2,1)S(1)}, bf16[128,2048]{1,0:T(8,128)(2,1)}, u32[]{:S(2)}) copy-start(bf16[128,2048]{1,0:T(8,128)(2,1)} %copy-done.4) | copy-start | bytes 1572868

commit v4 on v3

--- a/solution.py
+++ b/solution.py
@@ -105,8 +105,10 @@
         down_ref = refs[0] if extra else None
         refs = refs[extra + len(after) :]
         outs, cuts = refs[:count], refs[count : count + len(takes)]
-        held, made, load_sems, store_sems = refs[count + len(takes) :][:4]
-        scratch = refs[count + len(takes) + 4 :]
+        refs = refs[count + len(takes) :]
+        token_ref, held, made, load_sems, store_sems = refs[:5]
+        scratch = refs[5:]
+        token_ref[...] = jnp.zeros_like(token_ref)
         loads = [
             [
                 pltpu.make_async_copy(
@@ -191,11 +193,12 @@
             scratch.append(pltpu.VMEM(piece, BF16))
             scalars.append(first)
         scratch.append(pltpu.SemaphoreType.DMA((len(takes), 2)))
+    shapes.append(jax.ShapeDtypeStruct((8, 128), F32))
     return pl.pallas_call(
         body,
         out_shape=shapes,
         in_specs=[SCALARS, WHOLE] + [ANY] * (1 + extra + len(after)),
-        out_specs=[WHOLE if i in near_adds else ANY for i in range(len(shapes))],
+        out_specs=[WHOLE if i in near_adds else ANY for i in range(len(shapes) - 1)] + [WHOLE],
         scratch_shapes=scratch,
         compiler_params=params(20),
         cost_estimate=brief(),
@@ -461,11 +464,8 @@
             return result
 
         stores = []
-        for at in range(0, rows, chunk):
-            here = slice(at, at + chunk)
-            which = max(n for n in range(len(ranges)) if firsts[n] <= at)
-            out1_ref, lse_ref = done[which]
-            inner = slice(at - firsts[which], at - firsts[which] + chunk)
+        for at in range(0, rows, 2 * chunk):
+            here = slice(at, at + 2 * chunk)
             variant = variant_ref[here]
             code = jnp.concatenate(
                 [total(a_refs, here).astype(BF16), total(b_refs, here).astype(BF16)], axis=1
@@ -481,6 +481,12 @@
             )
             fresh = (base_ref[here] + change.astype(BF16).astype(F32)).astype(BF16)
             fresh_made[here] = fresh
+        for at in range(0, rows, chunk):
+            here = slice(at, at + chunk)
+            which = max(n for n in range(len(ranges)) if firsts[n] <= at)
+            out1_ref, lse_ref = done[which]
+            inner = slice(at - firsts[which], at - firsts[which] + chunk)
+            fresh = fresh_made[here]
             keys, values = [], []
             for g in range(width // (2 * HEAD)):
                 keys.append(fresh[:, 2 * g * HEAD : (2 * g + 1) * HEAD].astype(F32))
@@ -567,15 +573,15 @@
     every = lax.all_gather(delta_down, "adapter", axis=0, tiled=True)
     up = lax.all_gather(delta_up, "adapter", axis=0, tiled=True)
     order = sorted(range(size), key=lambda t: (-(t & 1), -t))
-    parts = project(tokens, base_weight, [me ^ t for t in order], width, [])
+    *parts, token = project(tokens, base_weight, [me ^ t for t in order], width, [])
     base_terms = reduce_parts(dict(zip(order, parts)))
     ids = jnp.arange(owners * variants, dtype=jnp.int32)
     rows_of = [(tokens, variant_ids, None)]
     codes_a, codes_b = [
-        all_reduce(codes(rows_of, [every[:, :, at : at + half]], ids, 0, [BF16], parts[:1])[0])
+        all_reduce(codes(rows_of, [every[:, :, at : at + half]], ids, 0, [BF16], [token])[0])
         for at in (0, half)
     ]
-    ranges = [cached(queries, kv_cache, lengths, 0, tokens.shape[0], parts[:1])]
+    ranges = [cached(queries, kv_cache, lengths, 0, tokens.shape[0], [token])]
     base, up = gather_up(base_terms, [1] * len(base_terms), [up], [])
     return finish(variant_ids, queries, ranges, base, codes_a, codes_b, up, ids)
 
@@ -592,16 +598,16 @@
     near_ids = swap(variant_ids, "adapter", 1)
     (first,) = cut(delta_down, [(group, 1, 0)], [])
     from_y = swap(first, "adapter", 2)
-    part_3, second = project(
+    part_3, second, token = project(
         tokens, base_weight, [me ^ 3], width, [first], delta_down, [(0, 2, 1)]
     )
     got_3 = swap(part_3, "tensor", 1)
     far = swap(second, "adapter", 2)
-    part_1, part_2, own = project(
-        tokens, base_weight, [me ^ 1, me ^ 2, me], width, [part_3]
+    part_1, part_2, own, token = project(
+        tokens, base_weight, [me ^ 1, me ^ 2, me], width, [token]
     )
     got_1 = swap(part_1, "tensor", 1)
-    from_y = gate(from_y, [own])
+    from_y = gate(from_y, [token])
     from_x = swap(from_y, "groups", 1)
     start, start_near, near = near_codes(
         tokens,
@@ -610,7 +616,7 @@
         near_ids,
         delta_down,
         jnp.stack([2 * mine, 2 * mine + 1]),
-        [own, from_y, lengths],
+        [token, from_y, lengths],
     )
     sum_2 = added([part_2, got_3])
     got_2 = swap(sum_2, "tensor", 2)

time: 77.4 us -> 77.3 us (level)
  waiting for transfers between devices: 13.9 us -> 16.7 us
  local copies, waits for them, and re-layouts: 2.56 us -> 0.49 us
    ppermute x17, waiting for transfers between devices: 13.9 us -> 16.7 us  [swap(): lax.ppermute(value, axis, [(i, i ^ bit) for i in range(lax.axis_size(axis...]
    unnamed x19 -> x15, local copies, waits for them, and re-layouts: 2.25 us -> 0.18 us
    pallas_call x1, Pallas kernels: 5.88 us -> 4.99 us  [finish(): pl.pallas_call(body, out_shape=[jax.ShapeDtypeStruct((rows, width), BF16)...]
    pallas_call x1, Pallas kernels: 1.15 us -> 1.94 us  [cut(): pl.pallas_call(body, out_shape=[in_vmem((count, depth, half), value.dtype...]
where the time goes in v4:
time: 77.3 us; the launch traced here: 77 us
  Pallas kernels  37.6 us (49%)
  starting transfers between devices  18.4 us (24%)
  waiting for transfers between devices  16.7 us (22%)
  other arithmetic  2.66 us (3%)
  between operations  1.05 us (1%)
    ppermute x17, starting transfers between devices, swap(): lax.ppermute(value, axis, [(i, i ^ bit) for i in range(lax.axis_size(axis...  18.4 us
    ppermute x17, waiting for transfers between devices, swap(): lax.ppermute(value, axis, [(i, i ^ bit) for i in range(lax.axis_size(axis...  16.7 us
    pallas_call x2, Pallas kernels, project(): pl.pallas_call(body, out_shape=shapes, in_specs=[SCALARS, WHOLE] + [ANY]...  10.8 us
    pallas_call x2, Pallas kernels, cached(): pl.pallas_call(body, out_shape=[in_vmem((rows, features), BF16), in_vmem(...  7.77 us
    pallas_call x1, Pallas kernels, finish(): pl.pallas_call(body, out_shape=[jax.ShapeDtypeStruct((rows, width), BF16)...  4.99 us
    pallas_call x2, Pallas kernels, codes(): pl.pallas_call(body, out_shape=shapes, in_specs=[SCALARS] + specs + [WHOL...  4.82 us
    pallas_call x1, Pallas kernels, near_codes(): pl.pallas_call(body, out_shape=[in_vmem((rows, rank), F32), in_vmem((rows...  4.49 us
    pallas_call x1, Pallas kernels, gather_up(): pl.pallas_call(body, out_shape=[in_vmem(terms[0].shape, F32), in_vmem((su...  2.76 us
  transfers between devices with their start and end apart: 17, of which 7 were waited for; matrix products, arithmetic and copies ran while one was open for 4% of the time, Pallas kernels for 42%

profile of v4, /device:TPU:0, one launch (start us, length us, event | category | flops | bytes accessed | tf_op | source)
XLA Modules:
  0.0 77.0 jit_solution(16681507461121131481)
XLA Ops:
  0.6 0.5 collective-permute-start.6
  1.2 1.9 %cut.1.refs_1_ = bf16[1,2048,128]{2,1,0:T(8,128)(2,1)} custom-call(s32[1]{0:T(128)} %bitcast.12.first_ref, bf16[2,2048,256]{2,1,0:T(8,128)(2,1)} %down_ref.1), custom_call_target="tpu_custom_call" | custom-call | flops 1 | bytes 1 | tf_op jit(solution)/shard_map/cut/pallas_call | solution.py:75
  3.1 2.6 %collective-permute-start.8 = (bf16[1,2048,128]{2,1,0:T(8,128)(2,1)}, bf16[1,2048,128]{2,1,0:T(8,128)(2,1)S(1)}, u32[]{:S(2)}, u32[]{:S(2)}) collective-permute-start(bf16[1,2048,128]{2,1,0:T(8,128)(2,1)} %cut.1.refs_1_), channel_id=1, source_target_pairs={{0,8},{4,12},{8,0},{12,4},{1,9},{5,13},{9,1},{13,5},{2,10},{6,14},... | collective-permute-start | bytes 1572872 | tf_op jit(solution)/shard_map/ppermute | solution.py:90
  5.8 4.3 %project.2 = (bf16[512,512]{1,0:T(8,128)(2,1)}, bf16[2,2048,128]{2,1,0:T(8,128)(2,1)}, f32[8,128]{1,0:T(8,128)S(1)}) custom-call(s32[2]{0:T(128)S(1)} %pad_add_fusion.1.scalars_ref, bf16[512,2048]{1,0:T(8,128)(2,1)S(1)} %copy-done, bf16[2048,2048]{1,0:T(8,128)(2,1)} %w_ref.3, bf16[2,2048,256]{2,1,0:T(8,128)(2,1)} %down_ref.1, bf16[1,2048,128]{2,1,0:T(8,128)(2,1)} %cut.1.refs_1_), custom_call_target="tpu_custom_call" | custom-call | flops 1 | bytes 1 | tf_op jit(solution)/shard_map/project/pallas_call | solution.py:197
  10.1 0.1 collective-permute-start.9
  10.2 2.1 %collective-permute-start.1 = (bf16[512,512]{1,0:T(8,128)(2,1)}, bf16[512,512]{1,0:T(8,128)(2,1)}, u32[]{:S(2)}, u32[]{:S(2)}) collective-permute-start(bf16[512,512]{1,0:T(8,128)(2,1)} %get-tuple-element.26), channel_id=1, source_target_pairs={{0,1},{1,0},{2,3},{3,2},{4,5},{5,4},{6,7},{7,6},{8,9},{9,8},{10,11... | collective-permute-start | bytes 1572872 | tf_op jit(solution)/shard_map/ppermute | solution.py:90
  12.3 0.1 copy.26.variant_ref.refs_1_
  12.6 6.5 %project.3 = (bf16[512,512]{1,0:T(8,128)(2,1)}, bf16[512,512]{1,0:T(8,128)(2,1)}, bf16[512,512]{1,0:T(8,128)(2,1)}, f32[8,128]{1,0:T(8,128)S(1)}) custom-call(s32[3]{0:T(128)S(1)} %pad_add_fusion.scalars_ref, bf16[512,2048]{1,0:T(8,128)(2,1)S(1)} %copy-done, bf16[2048,2048]{1,0:T(8,128)(2,1)} %w_ref.3, f32[8,128]{1,0:T(8,128)S(1)} %get-tuple-element.22.refs_0_), custom_call_target="tpu_custom_call" | custom-call | flops 1 | bytes 1 | tf_op jit(solution)/shard_map/project/pallas_call | solution.py:197
  19.2 1.6 %collective-permute-start.10 = (bf16[1,2048,128]{2,1,0:T(8,128)(2,1)S(1)}, bf16[1,2048,128]{2,1,0:T(8,128)(2,1)}, u32[]{:S(2)}, u32[]{:S(2)}) collective-permute-start(bf16[1,2048,128]{2,1,0:T(8,128)(2,1)S(1)} %gate.3.refs_1_.refs_6_), channel_id=1, source_target_pairs={{0,16},{16,0},{1,17},{17,1},{2,18},{18,2},{3,19},{19,3},{4,20},{20... | collective-permute-start | bytes 1572872 | tf_op jit(solution)/shard_map/ppermute | solution.py:90
  20.8 3.7 %collective-permute-done.1 = bf16[512,512]{1,0:T(8,128)(2,1)} collective-permute-done((bf16[512,512]{1,0:T(8,128)(2,1)}, bf16[512,512]{1,0:T(8,128)(2,1)}, u32[]{:S(2)}, u32[]{:S(2)}) %collective-permute-start.1) | collective-permute-done | bytes 524320 | tf_op jit(solution)/shard_map/ppermute | solution.py:90
  24.5 1.7 %collective-permute-start = (bf16[512,512]{1,0:T(8,128)(2,1)}, bf16[512,512]{1,0:T(8,128)(2,1)}, u32[]{:S(2)}, u32[]{:S(2)}) collective-permute-start(bf16[512,512]{1,0:T(8,128)(2,1)} %get-tuple-element.24), channel_id=1, source_target_pairs={{0,1},{1,0},{2,3},{3,2},{4,5},{5,4},{6,7},{7,6},{8,9},{9,8},{10,11... | collective-permute-start | bytes 1572872 | tf_op jit(solution)/shard_map/ppermute | solution.py:90
  26.2 2.1 %add_convert_fusion = bf16[512,512]{1,0:T(8,128)(2,1)} fusion(bf16[512,512]{1,0:T(8,128)(2,1)} %collective-permute-done.1, bf16[512,512]{1,0:T(8,128)(2,1)} %get-tuple-element.25), kind=kLoop, calls=%fused_computation | loop fusion | flops 1048576 | bytes 1572864 | tf_op jit(solution)/shard_map/convert_element_type | solution.py:94
  28.3 2.6 %collective-permute-start.2 = (bf16[512,512]{1,0:T(8,128)(2,1)}, bf16[512,512]{1,0:T(8,128)(2,1)}, u32[]{:S(2)}, u32[]{:S(2)}) collective-permute-start(bf16[512,512]{1,0:T(8,128)(2,1)} %add_convert_fusion), channel_id=1, source_target_pairs={{0,2},{1,3},{2,0},{3,1},{4,6},{5,7},{6,4},{7,5},{8,10},{9,11},{10,... | collective-permute-start | bytes 1572872 | tf_op jit(solution)/shard_map/ppermute | solution.py:90
  31.3 4.5 %near_codes.1 = (f32[512,256]{1,0:T(8,128)S(1)}, f32[512,256]{1,0:T(8,128)S(1)}, bf16[512,2048]{1,0:T(8,128)(2,1)S(1)}) custom-call(s32[2]{0:T(128)S(1)} %pad_add_fusion.3.ids_ref, bf16[512,2048]{1,0:T(8,128)(2,1)S(1)} %copy-done, s32[512,1]{1,0:T(8,128)S(1)} %copy.26.variant_ref.refs_1_, bf16[512,2048]{1,0:T(8,128)(2,1)} %collective-permute-done.6.near_ref, ...), custom_call_target="tpu_custom_call" | custom-call | flops 1 | bytes 1 | tf_op jit(solution)/shard_map/near_codes/pallas_call | solution.py:238
  35.9 2.3 %codes.2 = (f32[512,128]{1,0:T(8,128)S(1)}, bf16[512,128]{1,0:T(8,128)(2,1)S(1)}) custom-call(s32[2]{0:T(128)S(1)} %pad_add_fusion.4.ids_ref, bf16[512,2048]{1,0:T(8,128)(2,1)S(1)} %copy-done, s32[512,1]{1,0:T(8,128)S(1)} %copy.26.variant_ref.refs_1_, f32[512,256]{1,0:T(8,128)S(1)} %get-tuple-element.28.refs_2_.refs_8_, ...), custom_call_target="tpu_custom_call" | custom-call | flops 1 | bytes 1 | tf_op jit(solution)/shard_map/codes/pallas_call | solution.py:309
  38.2 2.8 %collective-permute-done.9.refs_6_ = bf16[2,2048,128]{2,1,0:T(8,128)(2,1)} collective-permute-done((bf16[2,2048,128]{2,1,0:T(8,128)(2,1)}, bf16[2,2048,128]{2,1,0:T(8,128)(2,1)}, u32[]{:S(2)}, u32[]{:S(2)}) %collective-permute-start.9) | collective-permute-done | bytes 1048608 | tf_op jit(solution)/shard_map/ppermute | solution.py:90
  41.0 2.5 %codes.3 = (f32[512,128]{1,0:T(8,128)S(1)}, bf16[512,128]{1,0:T(8,128)(2,1)S(1)}) custom-call(s32[2]{0:T(128)S(1)} %pad_add_fusion.2.ids_ref, bf16[512,2048]{1,0:T(8,128)(2,1)S(1)} %copy-done, s32[512,1]{1,0:T(8,128)S(1)} %copy.26.variant_ref.refs_1_, f32[512,256]{1,0:T(8,128)S(1)} %get-tuple-element.28.refs_2_.refs_8_, ...), custom_call_target="tpu_custom_call" | custom-call | flops 1 | bytes 1 | tf_op jit(solution)/shard_map/codes/pallas_call | solution.py:309
  43.6 1.8 %collective-permute-start.3 = (bf16[2,256,512]{2,1,0:T(8,128)(2,1)}, bf16[2,256,512]{2,1,0:T(8,128)(2,1)}, u32[]{:S(2)}, u32[]{:S(2)}) collective-permute-start(bf16[2,256,512]{2,1,0:T(8,128)(2,1)} %refs_3_.1), channel_id=1, source_target_pairs={{0,8},{4,12},{8,0},{12,4},{1,9},{5,13},{9,1},{13,5},{2,10},{6,14},... | collective-permute-start | bytes 1572872 | tf_op jit(solution)/shard_map/ppermute | solution.py:90
  45.4 0.2 collective-permute-start.4
  45.5 0.3 collective-permute-start.12
  45.9 0.9 %collective-permute-done.refs_1_ = bf16[512,512]{1,0:T(8,128)(2,1)} collective-permute-done((bf16[512,512]{1,0:T(8,128)(2,1)}, bf16[512,512]{1,0:T(8,128)(2,1)}, u32[]{:S(2)}, u32[]{:S(2)}) %collective-permute-start) | collective-permute-done | bytes 524320 | tf_op jit(solution)/shard_map/ppermute | solution.py:90
  46.9 6.5 %collective-permute-done.2.refs_2_ = bf16[512,512]{1,0:T(8,128)(2,1)} collective-permute-done((bf16[512,512]{1,0:T(8,128)(2,1)}, bf16[512,512]{1,0:T(8,128)(2,1)}, u32[]{:S(2)}, u32[]{:S(2)}) %collective-permute-start.2) | collective-permute-done | bytes 524320 | tf_op jit(solution)/shard_map/ppermute | solution.py:90
  53.4 2.1 %collective-permute-start.13 = (bf16[512,128]{1,0:T(8,128)(2,1)S(1)}, bf16[512,128]{1,0:T(8,128)(2,1)S(1)}, u32[]{:S(2)}, u32[]{:S(2)}) collective-permute-start(bf16[512,128]{1,0:T(8,128)(2,1)S(1)} %add_convert_fusion.3), channel_id=1, source_target_pairs={{0,1},{1,0},{2,3},{3,2},{4,5},{5,4},{6,7},{7,6},{8,9},{9,8},{10,11... | collective-permute-start | bytes 393224 | tf_op jit(solution)/shard_map/ppermute | solution.py:90
  55.5 2.5 %cached.2 = (bf16[128,2048]{1,0:T(8,128)(2,1)S(1)}, f32[128,128]{1,0:T(8,128)S(1)}) custom-call(s32[64,128]{1,0:T(8,128)S(1)} %copy.25.refs_2_.len_ref, bf16[512,2048]{1,0:T(8,128)(2,1)S(1)} %copy-done.1, bf16[512,16,512]{2,1,0:T(8,128)(2,1)} %kv_ref.3, bf16[512,128]{1,0:T(8,128)(2,1)S(1)} %gate.4.refs_0_), custom_call_target="tpu_custom_call" | custom-call | flops 1 | bytes 1 | tf_op jit(solution)/shard_map/cached/pallas_call | solution.py:391
  58.1 0.3 collective-permute-done.14
  58.4 1.0 %collective-permute-start.16 = (bf16[512,128]{1,0:T(8,128)(2,1)S(1)}, bf16[512,128]{1,0:T(8,128)(2,1)S(1)}, u32[]{:S(2)}, u32[]{:S(2)}) collective-permute-start(bf16[512,128]{1,0:T(8,128)(2,1)S(1)} %gate.5.refs_2_.refs_8_.refs_6_), channel_id=1, source_target_pairs={{0,2},{1,3},{2,0},{3,1},{4,6},{5,7},{6,4},{7,5},{8,10},{9,11},{10,... | collective-permute-start | bytes 393224 | tf_op jit(solution)/shard_map/ppermute | solution.py:90
  59.4 1.4 %collective-permute-done.13 = bf16[512,128]{1,0:T(8,128)(2,1)S(1)} collective-permute-done((bf16[512,128]{1,0:T(8,128)(2,1)S(1)}, bf16[512,128]{1,0:T(8,128)(2,1)S(1)}, u32[]{:S(2)}, u32[]{:S(2)}) %collective-permute-start.13) | collective-permute-done | bytes 131104 | tf_op jit(solution)/shard_map/ppermute | solution.py:90
  60.8 1.7 %collective-permute-start.15 = (bf16[512,128]{1,0:T(8,128)(2,1)S(1)}, bf16[512,128]{1,0:T(8,128)(2,1)S(1)}, u32[]{:S(2)}, u32[]{:S(2)}) collective-permute-start(bf16[512,128]{1,0:T(8,128)(2,1)S(1)} %add_convert_fusion.2.refs_1_.refs_4_), channel_id=1, source_target_pairs={{0,2},{1,3},{2,0},{3,1},{4,6},{5,7},{6,4},{7,5},{8,10},{9,11},{10,... | collective-permute-start | bytes 393224 | tf_op jit(solution)/shard_map/ppermute | solution.py:90
  62.6 5.2 %cached.3 = (bf16[384,2048]{1,0:T(8,128)(2,1)S(1)}, f32[384,128]{1,0:T(8,128)S(1)}) custom-call(s32[64,128]{1,0:T(8,128)S(1)} %copy.25.refs_2_.len_ref, bf16[512,2048]{1,0:T(8,128)(2,1)S(1)} %copy-done.1, bf16[512,16,512]{2,1,0:T(8,128)(2,1)} %kv_ref.3, f32[128,128]{1,0:T(8,128)S(1)} %get-tuple-element.35.refs_1_.refs_0_, ...), custom_call_target="tpu_custom_call" | custom-call | flops 1 | bytes 1 | tf_op jit(solution)/shard_map/cached/pallas_call | solution.py:391
  67.9 1.1 %collective-permute-done.5.refs_6_ = bf16[2,256,512]{2,1,0:T(8,128)(2,1)} collective-permute-done((bf16[2,256,512]{2,1,0:T(8,128)(2,1)}, bf16[2,256,512]{2,1,0:T(8,128)(2,1)}, u32[]{:S(2)}, u32[]{:S(2)}) %collective-permute-start.5) | collective-permute-done | bytes 524320 | tf_op jit(solution)/shard_map/ppermute | solution.py:90
  69.0 2.8 %gather_up.1 = (f32[512,512]{1,0:T(8,128)S(1)}, bf16[8,256,512]{2,1,0:T(8,128)(2,1)S(1)}) custom-call(s32[3]{0:T(128)S(1)} %broadcast_1_flags_ref.2.flags_ref, bf16[512,512]{1,0:T(8,128)(2,1)S(1)} %copy-done.2, bf16[512,512]{1,0:T(8,128)(2,1)} %collective-permute-done.refs_1_, bf16[512,512]{1,0:T(8,128)(2,1)} %collective-permute-done.2.refs_2_, ...), custom_call_target="tpu_custom_call" | custom-call | flops 1 | bytes 1 | tf_op jit(solution)/shard_map/gather_up/pallas_call | solution.py:426
  71.8 5.0 %finish.1 = (bf16[512,512]{1,0:T(8,128)(2,1)}, bf16[512,2048]{1,0:T(8,128)(2,1)}) custom-call(s32[8]{0:T(128)S(1)} %stack.75.ids_ref, s32[512,1]{1,0:T(8,128)S(1)} %copy.26.variant_ref.refs_1_, bf16[512,2048]{1,0:T(8,128)(2,1)S(1)} %copy-done.1, f32[512,512]{1,0:T(8,128)S(1)} %get-tuple-element.38.base_ref, ...), custom_call_target="tpu_custom_call" | custom-call | flops 1 | bytes 1 | tf_op jit(solution)/shard_map/finish/pallas_call | solution.py:521
  (46 shorter events, 1.1 us)
Async XLA Ops:
  0.6 5.2 %copy-start = (bf16[512,2048]{1,0:T(8,128)(2,1)S(1)}, bf16[512,2048]{1,0:T(8,128)(2,1)}, u32[]{:S(2)}) copy-start(bf16[512,2048]{1,0:T(8,128)(2,1)} %refs_0_.5) | copy-start | bytes 6291460
  0.6 30.7 %collective-permute-start.6 = (bf16[512,2048]{1,0:T(8,128)(2,1)}, bf16[512,2048]{1,0:T(8,128)(2,1)}, u32[]{:S(2)}, u32[]{:S(2)}) collective-permute-start(bf16[512,2048]{1,0:T(8,128)(2,1)} %refs_0_.5), channel_id=1, source_target_pairs={{0,4},{4,0},{8,12},{12,8},{1,5},{5,1},{9,13},{13,9},{2,6},{6,2},{1... | collective-permute-start | bytes 6291464 | tf_op jit(solution)/shard_map/ppermute | solution.py:90
  3.1 16.1 %collective-permute-start.8 = (bf16[1,2048,128]{2,1,0:T(8,128)(2,1)}, bf16[1,2048,128]{2,1,0:T(8,128)(2,1)S(1)}, u32[]{:S(2)}, u32[]{:S(2)}) collective-permute-start(bf16[1,2048,128]{2,1,0:T(8,128)(2,1)} %cut.1.refs_1_), channel_id=1, source_target_pairs={{0,8},{4,12},{8,0},{12,4},{1,9},{5,13},{9,1},{13,5},{2,10},{6,14},... | collective-permute-start | bytes 1572872 | tf_op jit(solution)/shard_map/ppermute | solution.py:90
  5.8 6.5 %copy-start.5 = (s32[512,1]{0,1:T(1,128)S(1)}, s32[512,1]{0,1:T(1,128)}, u32[]{:S(2)}) copy-start(s32[512,1]{0,1:T(1,128)} %param.12) | copy-start | bytes 6148
  10.1 30.8 %collective-permute-start.9 = (bf16[2,2048,128]{2,1,0:T(8,128)(2,1)}, bf16[2,2048,128]{2,1,0:T(8,128)(2,1)}, u32[]{:S(2)}, u32[]{:S(2)}) collective-permute-start(bf16[2,2048,128]{2,1,0:T(8,128)(2,1)} %get-tuple-element.31), channel_id=1, source_target_pairs={{0,8},{4,12},{8,0},{12,4},{1,9},{5,13},{9,1},{13,5},{2,10},{6,14},... | collective-permute-start | bytes 3145736 | tf_op jit(solution)/shard_map/ppermute | solution.py:90
  10.2 14.3 %collective-permute-start.1 = (bf16[512,512]{1,0:T(8,128)(2,1)}, bf16[512,512]{1,0:T(8,128)(2,1)}, u32[]{:S(2)}, u32[]{:S(2)}) collective-permute-start(bf16[512,512]{1,0:T(8,128)(2,1)} %get-tuple-element.26), channel_id=1, source_target_pairs={{0,1},{1,0},{2,3},{3,2},{4,5},{5,4},{6,7},{7,6},{8,9},{9,8},{10,11... | collective-permute-start | bytes 1572872 | tf_op jit(solution)/shard_map/ppermute | solution.py:90
  12.4 15.9 %collective-permute-start.7 = (s32[512,1]{1,0:T(8,128)S(1)}, s32[512,1]{1,0:T(8,128)S(1)}, u32[]{:S(2)}, u32[]{:S(2)}) collective-permute-start(s32[512,1]{1,0:T(8,128)S(1)} %copy.26.variant_ref.refs_1_), channel_id=1, source_target_pairs={{0,4},{4,0},{8,12},{12,8},{1,5},{5,1},{9,13},{13,9},{2,6},{6,2},{1... | collective-permute-start | bytes 6152 | tf_op jit(solution)/shard_map/ppermute | solution.py:90
  19.1 11.9 %copy-start.6 = (s32[512]{0:T(512)S(1)}, s32[512]{0:T(512)}, u32[]{:S(2)}) copy-start(s32[512]{0:T(512)} %param.11) | copy-start | bytes 6148
  19.2 16.7 %collective-permute-start.10 = (bf16[1,2048,128]{2,1,0:T(8,128)(2,1)S(1)}, bf16[1,2048,128]{2,1,0:T(8,128)(2,1)}, u32[]{:S(2)}, u32[]{:S(2)}) collective-permute-start(bf16[1,2048,128]{2,1,0:T(8,128)(2,1)S(1)} %gate.3.refs_1_.refs_6_), channel_id=1, source_target_pairs={{0,16},{16,0},{1,17},{17,1},{2,18},{18,2},{3,19},{19,3},{4,20},{20... | collective-permute-start | bytes 1572872 | tf_op jit(solution)/shard_map/ppermute | solution.py:90
  24.5 22.4 %collective-permute-start = (bf16[512,512]{1,0:T(8,128)(2,1)}, bf16[512,512]{1,0:T(8,128)(2,1)}, u32[]{:S(2)}, u32[]{:S(2)}) collective-permute-start(bf16[512,512]{1,0:T(8,128)(2,1)} %get-tuple-element.24), channel_id=1, source_target_pairs={{0,1},{1,0},{2,3},{3,2},{4,5},{5,4},{6,7},{7,6},{8,9},{9,8},{10,11... | collective-permute-start | bytes 1572872 | tf_op jit(solution)/shard_map/ppermute | solution.py:90
  28.3 25.1 %collective-permute-start.2 = (bf16[512,512]{1,0:T(8,128)(2,1)}, bf16[512,512]{1,0:T(8,128)(2,1)}, u32[]{:S(2)}, u32[]{:S(2)}) collective-permute-start(bf16[512,512]{1,0:T(8,128)(2,1)} %add_convert_fusion), channel_id=1, source_target_pairs={{0,2},{1,3},{2,0},{3,1},{4,6},{5,7},{6,4},{7,5},{8,10},{9,11},{10,... | collective-permute-start | bytes 1572872 | tf_op jit(solution)/shard_map/ppermute | solution.py:90
  43.5 12.1 %copy-start.1 = (bf16[512,2048]{1,0:T(8,128)(2,1)S(1)}, bf16[512,2048]{1,0:T(8,128)(2,1)}, u32[]{:S(2)}) copy-start(bf16[512,2048]{1,0:T(8,128)(2,1)} %q_ref.5) | copy-start | bytes 6291460
  43.5 2.1 %collective-permute-start.11 = (bf16[512,128]{1,0:T(8,128)(2,1)S(1)}, bf16[512,128]{1,0:T(8,128)(2,1)S(1)}, u32[]{:S(2)}, u32[]{:S(2)}) collective-permute-start(bf16[512,128]{1,0:T(8,128)(2,1)S(1)} %get-tuple-element.34), channel_id=1, source_target_pairs={{0,4},{4,0},{8,12},{12,8},{1,5},{5,1},{9,13},{13,9},{2,6},{6,2},{1... | collective-permute-start | bytes 393224 | tf_op jit(solution)/shard_map/ppermute | solution.py:90
  43.6 24.3 %collective-permute-start.3 = (bf16[2,256,512]{2,1,0:T(8,128)(2,1)}, bf16[2,256,512]{2,1,0:T(8,128)(2,1)}, u32[]{:S(2)}, u32[]{:S(2)}) collective-permute-start(bf16[2,256,512]{2,1,0:T(8,128)(2,1)} %refs_3_.1), channel_id=1, source_target_pairs={{0,8},{4,12},{8,0},{12,4},{1,9},{5,13},{9,1},{13,5},{2,10},{6,14},... | collective-permute-start | bytes 1572872 | tf_op jit(solution)/shard_map/ppermute | solution.py:90
  45.4 22.5 %collective-permute-start.4 = (bf16[2,256,512]{2,1,0:T(8,128)(2,1)}, bf16[2,256,512]{2,1,0:T(8,128)(2,1)}, u32[]{:S(2)}, u32[]{:S(2)}) collective-permute-start(bf16[2,256,512]{2,1,0:T(8,128)(2,1)} %refs_3_.1), channel_id=1, source_target_pairs={{0,4},{4,0},{8,12},{12,8},{1,5},{5,1},{9,13},{13,9},{2,6},{6,2},{1... | collective-permute-start | bytes 1572872 | tf_op jit(solution)/shard_map/ppermute | solution.py:90
  45.5 7.9 %collective-permute-start.12 = (bf16[512,128]{1,0:T(8,128)(2,1)S(1)}, bf16[512,128]{1,0:T(8,128)(2,1)S(1)}, u32[]{:S(2)}, u32[]{:S(2)}) collective-permute-start(bf16[512,128]{1,0:T(8,128)(2,1)S(1)} %get-tuple-element.32.refs_7_), channel_id=1, source_target_pairs={{0,4},{4,0},{8,12},{12,8},{1,5},{5,1},{9,13},{13,9},{2,6},{6,2},{1... | collective-permute-start | bytes 393224 | tf_op jit(solution)/shard_map/ppermute | solution.py:90
  46.8 22.2 %collective-permute-start.5 = (bf16[2,256,512]{2,1,0:T(8,128)(2,1)}, bf16[2,256,512]{2,1,0:T(8,128)(2,1)}, u32[]{:S(2)}, u32[]{:S(2)}) collective-permute-start(bf16[2,256,512]{2,1,0:T(8,128)(2,1)} %refs_3_.1), channel_id=1, source_target_pairs={{0,12},{4,8},{8,4},{12,0},{1,13},{5,9},{9,5},{13,1},{2,14},{6,10},... | collective-permute-start | bytes 1572872 | tf_op jit(solution)/shard_map/ppermute | solution.py:90
  53.4 5.0 %collective-permute-start.14 = (bf16[512,128]{1,0:T(8,128)(2,1)S(1)}, bf16[512,128]{1,0:T(8,128)(2,1)S(1)}, u32[]{:S(2)}, u32[]{:S(2)}) collective-permute-start(bf16[512,128]{1,0:T(8,128)(2,1)S(1)} %gate.4.refs_0_), channel_id=1, source_target_pairs={{0,1},{1,0},{2,3},{3,2},{4,5},{5,4},{6,7},{7,6},{8,9},{9,8},{10,11... | collective-permute-start | bytes 393224 | tf_op jit(solution)/shard_map/ppermute | solution.py:90
  53.4 7.3 %collective-permute-start.13 = (bf16[512,128]{1,0:T(8,128)(2,1)S(1)}, bf16[512,128]{1,0:T(8,128)(2,1)S(1)}, u32[]{:S(2)}, u32[]{:S(2)}) collective-permute-start(bf16[512,128]{1,0:T(8,128)(2,1)S(1)} %add_convert_fusion.3), channel_id=1, source_target_pairs={{0,1},{1,0},{2,3},{3,2},{4,5},{5,4},{6,7},{7,6},{8,9},{9,8},{10,11... | collective-permute-start | bytes 393224 | tf_op jit(solution)/shard_map/ppermute | solution.py:90
  58.1 2.7 %copy-start.3 = (bf16[128,2048]{1,0:T(8,128)(2,1)}, bf16[128,2048]{1,0:T(8,128)(2,1)S(1)}, u32[]{:S(2)}) copy-start(bf16[128,2048]{1,0:T(8,128)(2,1)S(1)} %get-tuple-element.40.refs_0_) | copy-start | bytes 1572868
  58.4 13.3 %collective-permute-start.16 = (bf16[512,128]{1,0:T(8,128)(2,1)S(1)}, bf16[512,128]{1,0:T(8,128)(2,1)S(1)}, u32[]{:S(2)}, u32[]{:S(2)}) collective-permute-start(bf16[512,128]{1,0:T(8,128)(2,1)S(1)} %gate.5.refs_2_.refs_8_.refs_6_), channel_id=1, source_target_pairs={{0,2},{1,3},{2,0},{3,1},{4,6},{5,7},{6,4},{7,5},{8,10},{9,11},{10,... | collective-permute-start | bytes 393224 | tf_op jit(solution)/shard_map/ppermute | solution.py:90
  60.8 11.0 %collective-permute-start.15 = (bf16[512,128]{1,0:T(8,128)(2,1)S(1)}, bf16[512,128]{1,0:T(8,128)(2,1)S(1)}, u32[]{:S(2)}, u32[]{:S(2)}) collective-permute-start(bf16[512,128]{1,0:T(8,128)(2,1)S(1)} %add_convert_fusion.2.refs_1_.refs_4_), channel_id=1, source_target_pairs={{0,2},{1,3},{2,0},{3,1},{4,6},{5,7},{6,4},{7,5},{8,10},{9,11},{10,... | collective-permute-start | bytes 393224 | tf_op jit(solution)/shard_map/ppermute | solution.py:90
  62.6 6.4 %copy-start.2 = (bf16[512,512]{1,0:T(8,128)(2,1)S(1)}, bf16[512,512]{1,0:T(8,128)(2,1)}, u32[]{:S(2)}) copy-start(bf16[512,512]{1,0:T(8,128)(2,1)} %get-tuple-element.23.refs_0_) | copy-start | bytes 1572868
  67.8 3.9 %copy-start.4 = (bf16[128,2048]{1,0:T(8,128)(2,1)S(1)}, bf16[128,2048]{1,0:T(8,128)(2,1)}, u32[]{:S(2)}) copy-start(bf16[128,2048]{1,0:T(8,128)(2,1)} %copy-done.3) | copy-start | bytes 1572868

commit v5 on v4

--- a/solution.py
+++ b/solution.py
@@ -604,7 +604,7 @@
     got_3 = swap(part_3, "tensor", 1)
     far = swap(second, "adapter", 2)
     part_1, part_2, own, token = project(
-        tokens, base_weight, [me ^ 1, me ^ 2, me], width, [token]
+        tokens, base_weight, [me ^ 1, me ^ 2, me], width, [token], near_adds=[1]
     )
     got_1 = swap(part_1, "tensor", 1)
     from_y = gate(from_y, [token])

time: 77.3 us -> 77.3 us (level)
  local copies, waits for them, and re-layouts: 0.49 us -> 1.28 us
    unnamed x15 -> x17, local copies, waits for them, and re-layouts: 0.18 us -> 0.97 us
where the time goes in v5:
time: 77.3 us; the launch traced here: 77 us
  Pallas kernels  37.6 us (49%)
  starting transfers between devices  18.4 us (24%)
  waiting for transfers between devices  16 us (21%)
  other arithmetic  2.66 us (3%)
  local copies, waits for them, and re-layouts  1.28 us (2%)
  between operations  1.03 us (1%)
    ppermute x17, starting transfers between devices, swap(): lax.ppermute(value, axis, [(i, i ^ bit) for i in range(lax.axis_size(axis...  18.4 us
    ppermute x17, waiting for transfers between devices, swap(): lax.ppermute(value, axis, [(i, i ^ bit) for i in range(lax.axis_size(axis...  16 us
    pallas_call x2, Pallas kernels, project(): pl.pallas_call(body, out_shape=shapes, in_specs=[SCALARS, WHOLE] + [ANY]...  10.8 us
    pallas_call x2, Pallas kernels, cached(): pl.pallas_call(body, out_shape=[in_vmem((rows, features), BF16), in_vmem(...  7.77 us
    pallas_call x1, Pallas kernels, finish(): pl.pallas_call(body, out_shape=[jax.ShapeDtypeStruct((rows, width), BF16)...  4.99 us
    pallas_call x2, Pallas kernels, codes(): pl.pallas_call(body, out_shape=shapes, in_specs=[SCALARS] + specs + [WHOL...  4.82 us
    pallas_call x1, Pallas kernels, near_codes(): pl.pallas_call(body, out_shape=[in_vmem((rows, rank), F32), in_vmem((rows...  4.49 us
    pallas_call x1, Pallas kernels, gather_up(): pl.pallas_call(body, out_shape=[in_vmem(terms[0].shape, F32), in_vmem((su...  2.76 us
  transfers between devices with their start and end apart: 17, of which 7 were waited for; matrix products, arithmetic and copies ran while one was open for 4% of the time, Pallas kernels for 42%

profile of v5, /device:TPU:0, one launch (start us, length us, event | category | flops | bytes accessed | tf_op | source)
XLA Modules:
  0.0 77.0 jit_solution(15236335792587971924)
XLA Ops:
  0.6 0.5 collective-permute-start.6
  1.2 1.9 %cut.1.refs_1_ = bf16[1,2048,128]{2,1,0:T(8,128)(2,1)} custom-call(s32[1]{0:T(128)} %bitcast.12.first_ref, bf16[2,2048,256]{2,1,0:T(8,128)(2,1)} %down_ref.1), custom_call_target="tpu_custom_call" | custom-call | flops 1 | bytes 1 | tf_op jit(solution)/shard_map/cut/pallas_call | solution.py:75
  3.1 2.6 %collective-permute-start.8 = (bf16[1,2048,128]{2,1,0:T(8,128)(2,1)}, bf16[1,2048,128]{2,1,0:T(8,128)(2,1)S(1)}, u32[]{:S(2)}, u32[]{:S(2)}) collective-permute-start(bf16[1,2048,128]{2,1,0:T(8,128)(2,1)} %cut.1.refs_1_), channel_id=1, source_target_pairs={{0,8},{4,12},{8,0},{12,4},{1,9},{5,13},{9,1},{13,5},{2,10},{6,14},... | collective-permute-start | bytes 1572872 | tf_op jit(solution)/shard_map/ppermute | solution.py:90
  5.8 4.3 %project.2 = (bf16[512,512]{1,0:T(8,128)(2,1)}, bf16[2,2048,128]{2,1,0:T(8,128)(2,1)}, f32[8,128]{1,0:T(8,128)S(1)}) custom-call(s32[2]{0:T(128)S(1)} %pad_add_fusion.1.scalars_ref, bf16[512,2048]{1,0:T(8,128)(2,1)S(1)} %copy-done, bf16[2048,2048]{1,0:T(8,128)(2,1)} %w_ref.3, bf16[2,2048,256]{2,1,0:T(8,128)(2,1)} %down_ref.1, bf16[1,2048,128]{2,1,0:T(8,128)(2,1)} %cut.1.refs_1_), custom_call_target="tpu_custom_call" | custom-call | flops 1 | bytes 1 | tf_op jit(solution)/shard_map/project/pallas_call | solution.py:197
  10.2 2.1 %collective-permute-start.1 = (bf16[512,512]{1,0:T(8,128)(2,1)}, bf16[512,512]{1,0:T(8,128)(2,1)}, u32[]{:S(2)}, u32[]{:S(2)}) collective-permute-start(bf16[512,512]{1,0:T(8,128)(2,1)} %get-tuple-element.26), channel_id=1, source_target_pairs={{0,1},{1,0},{2,3},{3,2},{4,5},{5,4},{6,7},{7,6},{8,9},{9,8},{10,11... | collective-permute-start | bytes 1572872 | tf_op jit(solution)/shard_map/ppermute | solution.py:90
  12.3 0.1 copy.26.variant_ref.refs_1_
  12.6 6.5 %project.3 = (bf16[512,512]{1,0:T(8,128)(2,1)}, bf16[512,512]{1,0:T(8,128)(2,1)S(1)}, bf16[512,512]{1,0:T(8,128)(2,1)}, f32[8,128]{1,0:T(8,128)S(1)}) custom-call(s32[3]{0:T(128)S(1)} %pad_add_fusion.scalars_ref, bf16[512,2048]{1,0:T(8,128)(2,1)S(1)} %copy-done, bf16[2048,2048]{1,0:T(8,128)(2,1)} %w_ref.3, f32[8,128]{1,0:T(8,128)S(1)} %get-tuple-element.22.refs_0_), custom_call_target="tpu_custom_call" | custom-call | flops 1 | bytes 1 | tf_op jit(solution)/shard_map/project/pallas_call | solution.py:197
  19.1 0.8 %copy-done.5 = bf16[512,512]{1,0:T(8,128)(2,1)} copy-done((bf16[512,512]{1,0:T(8,128)(2,1)}, bf16[512,512]{1,0:T(8,128)(2,1)S(1)}, u32[]{:S(2)}) %copy-start.5) | copy-done | bytes 524312
  19.9 1.5 %collective-permute-start.10 = (bf16[1,2048,128]{2,1,0:T(8,128)(2,1)S(1)}, bf16[1,2048,128]{2,1,0:T(8,128)(2,1)}, u32[]{:S(2)}, u32[]{:S(2)}) collective-permute-start(bf16[1,2048,128]{2,1,0:T(8,128)(2,1)S(1)} %gate.3.refs_1_.refs_6_), channel_id=1, source_target_pairs={{0,16},{16,0},{1,17},{17,1},{2,18},{18,2},{3,19},{19,3},{4,20},{20... | collective-permute-start | bytes 1572872 | tf_op jit(solution)/shard_map/ppermute | solution.py:90
  21.5 3.0 %collective-permute-done.1 = bf16[512,512]{1,0:T(8,128)(2,1)} collective-permute-done((bf16[512,512]{1,0:T(8,128)(2,1)}, bf16[512,512]{1,0:T(8,128)(2,1)}, u32[]{:S(2)}, u32[]{:S(2)}) %collective-permute-start.1) | collective-permute-done | bytes 524320 | tf_op jit(solution)/shard_map/ppermute | solution.py:90
  24.5 1.7 %collective-permute-start = (bf16[512,512]{1,0:T(8,128)(2,1)}, bf16[512,512]{1,0:T(8,128)(2,1)}, u32[]{:S(2)}, u32[]{:S(2)}) collective-permute-start(bf16[512,512]{1,0:T(8,128)(2,1)} %get-tuple-element.24), channel_id=1, source_target_pairs={{0,1},{1,0},{2,3},{3,2},{4,5},{5,4},{6,7},{7,6},{8,9},{9,8},{10,11... | collective-permute-start | bytes 1572872 | tf_op jit(solution)/shard_map/ppermute | solution.py:90
  26.2 2.1 %add_convert_fusion = bf16[512,512]{1,0:T(8,128)(2,1)} fusion(bf16[512,512]{1,0:T(8,128)(2,1)} %collective-permute-done.1, bf16[512,512]{1,0:T(8,128)(2,1)} %copy-done.5), kind=kLoop, calls=%fused_computation | loop fusion | flops 1048576 | bytes 1572864 | tf_op jit(solution)/shard_map/convert_element_type | solution.py:94
  28.3 2.6 %collective-permute-start.2 = (bf16[512,512]{1,0:T(8,128)(2,1)}, bf16[512,512]{1,0:T(8,128)(2,1)}, u32[]{:S(2)}, u32[]{:S(2)}) collective-permute-start(bf16[512,512]{1,0:T(8,128)(2,1)} %add_convert_fusion), channel_id=1, source_target_pairs={{0,2},{1,3},{2,0},{3,1},{4,6},{5,7},{6,4},{7,5},{8,10},{9,11},{10,... | collective-permute-start | bytes 1572872 | tf_op jit(solution)/shard_map/ppermute | solution.py:90
  31.3 4.5 %near_codes.1 = (f32[512,256]{1,0:T(8,128)S(1)}, f32[512,256]{1,0:T(8,128)S(1)}, bf16[512,2048]{1,0:T(8,128)(2,1)S(1)}) custom-call(s32[2]{0:T(128)S(1)} %pad_add_fusion.3.ids_ref, bf16[512,2048]{1,0:T(8,128)(2,1)S(1)} %copy-done, s32[512,1]{1,0:T(8,128)S(1)} %copy.26.variant_ref.refs_1_, bf16[512,2048]{1,0:T(8,128)(2,1)} %collective-permute-done.6.near_ref, ...), custom_call_target="tpu_custom_call" | custom-call | flops 1 | bytes 1 | tf_op jit(solution)/shard_map/near_codes/pallas_call | solution.py:238
  35.9 2.3 %codes.2 = (f32[512,128]{1,0:T(8,128)S(1)}, bf16[512,128]{1,0:T(8,128)(2,1)S(1)}) custom-call(s32[2]{0:T(128)S(1)} %pad_add_fusion.4.ids_ref, bf16[512,2048]{1,0:T(8,128)(2,1)S(1)} %copy-done, s32[512,1]{1,0:T(8,128)S(1)} %copy.26.variant_ref.refs_1_, f32[512,256]{1,0:T(8,128)S(1)} %get-tuple-element.28.refs_2_.refs_8_, ...), custom_call_target="tpu_custom_call" | custom-call | flops 1 | bytes 1 | tf_op jit(solution)/shard_map/codes/pallas_call | solution.py:309
  38.2 2.8 %collective-permute-done.9.refs_6_ = bf16[2,2048,128]{2,1,0:T(8,128)(2,1)} collective-permute-done((bf16[2,2048,128]{2,1,0:T(8,128)(2,1)}, bf16[2,2048,128]{2,1,0:T(8,128)(2,1)}, u32[]{:S(2)}, u32[]{:S(2)}) %collective-permute-start.9) | collective-permute-done | bytes 1048608 | tf_op jit(solution)/shard_map/ppermute | solution.py:90
  41.0 2.5 %codes.3 = (f32[512,128]{1,0:T(8,128)S(1)}, bf16[512,128]{1,0:T(8,128)(2,1)S(1)}) custom-call(s32[2]{0:T(128)S(1)} %pad_add_fusion.2.ids_ref, bf16[512,2048]{1,0:T(8,128)(2,1)S(1)} %copy-done, s32[512,1]{1,0:T(8,128)S(1)} %copy.26.variant_ref.refs_1_, f32[512,256]{1,0:T(8,128)S(1)} %get-tuple-element.28.refs_2_.refs_8_, ...), custom_call_target="tpu_custom_call" | custom-call | flops 1 | bytes 1 | tf_op jit(solution)/shard_map/codes/pallas_call | solution.py:309
  43.6 1.8 %collective-permute-start.3 = (bf16[2,256,512]{2,1,0:T(8,128)(2,1)}, bf16[2,256,512]{2,1,0:T(8,128)(2,1)}, u32[]{:S(2)}, u32[]{:S(2)}) collective-permute-start(bf16[2,256,512]{2,1,0:T(8,128)(2,1)} %refs_3_.1), channel_id=1, source_target_pairs={{0,8},{4,12},{8,0},{12,4},{1,9},{5,13},{9,1},{13,5},{2,10},{6,14},... | collective-permute-start | bytes 1572872 | tf_op jit(solution)/shard_map/ppermute | solution.py:90
  45.4 0.2 collective-permute-start.4
  45.5 0.3 collective-permute-start.12
  45.9 0.9 %collective-permute-done.refs_1_ = bf16[512,512]{1,0:T(8,128)(2,1)} collective-permute-done((bf16[512,512]{1,0:T(8,128)(2,1)}, bf16[512,512]{1,0:T(8,128)(2,1)}, u32[]{:S(2)}, u32[]{:S(2)}) %collective-permute-start) | collective-permute-done | bytes 524320 | tf_op jit(solution)/shard_map/ppermute | solution.py:90
  46.9 6.5 %collective-permute-done.2.refs_2_ = bf16[512,512]{1,0:T(8,128)(2,1)} collective-permute-done((bf16[512,512]{1,0:T(8,128)(2,1)}, bf16[512,512]{1,0:T(8,128)(2,1)}, u32[]{:S(2)}, u32[]{:S(2)}) %collective-permute-start.2) | collective-permute-done | bytes 524320 | tf_op jit(solution)/shard_map/ppermute | solution.py:90
  53.4 2.1 %collective-permute-start.13 = (bf16[512,128]{1,0:T(8,128)(2,1)S(1)}, bf16[512,128]{1,0:T(8,128)(2,1)S(1)}, u32[]{:S(2)}, u32[]{:S(2)}) collective-permute-start(bf16[512,128]{1,0:T(8,128)(2,1)S(1)} %add_convert_fusion.3), channel_id=1, source_target_pairs={{0,1},{1,0},{2,3},{3,2},{4,5},{5,4},{6,7},{7,6},{8,9},{9,8},{10,11... | collective-permute-start | bytes 393224 | tf_op jit(solution)/shard_map/ppermute | solution.py:90
  55.5 2.5 %cached.2 = (bf16[128,2048]{1,0:T(8,128)(2,1)S(1)}, f32[128,128]{1,0:T(8,128)S(1)}) custom-call(s32[64,128]{1,0:T(8,128)S(1)} %copy.25.refs_2_.len_ref, bf16[512,2048]{1,0:T(8,128)(2,1)S(1)} %copy-done.1, bf16[512,16,512]{2,1,0:T(8,128)(2,1)} %kv_ref.3, bf16[512,128]{1,0:T(8,128)(2,1)S(1)} %gate.4.refs_0_), custom_call_target="tpu_custom_call" | custom-call | flops 1 | bytes 1 | tf_op jit(solution)/shard_map/cached/pallas_call | solution.py:391
  58.1 0.3 collective-permute-done.14
  58.4 1.0 %collective-permute-start.16 = (bf16[512,128]{1,0:T(8,128)(2,1)S(1)}, bf16[512,128]{1,0:T(8,128)(2,1)S(1)}, u32[]{:S(2)}, u32[]{:S(2)}) collective-permute-start(bf16[512,128]{1,0:T(8,128)(2,1)S(1)} %gate.5.refs_2_.refs_8_.refs_6_), channel_id=1, source_target_pairs={{0,2},{1,3},{2,0},{3,1},{4,6},{5,7},{6,4},{7,5},{8,10},{9,11},{10,... | collective-permute-start | bytes 393224 | tf_op jit(solution)/shard_map/ppermute | solution.py:90
  59.4 1.4 %collective-permute-done.13 = bf16[512,128]{1,0:T(8,128)(2,1)S(1)} collective-permute-done((bf16[512,128]{1,0:T(8,128)(2,1)S(1)}, bf16[512,128]{1,0:T(8,128)(2,1)S(1)}, u32[]{:S(2)}, u32[]{:S(2)}) %collective-permute-start.13) | collective-permute-done | bytes 131104 | tf_op jit(solution)/shard_map/ppermute | solution.py:90
  60.8 1.7 %collective-permute-start.15 = (bf16[512,128]{1,0:T(8,128)(2,1)S(1)}, bf16[512,128]{1,0:T(8,128)(2,1)S(1)}, u32[]{:S(2)}, u32[]{:S(2)}) collective-permute-start(bf16[512,128]{1,0:T(8,128)(2,1)S(1)} %add_convert_fusion.2.refs_1_.refs_4_), channel_id=1, source_target_pairs={{0,2},{1,3},{2,0},{3,1},{4,6},{5,7},{6,4},{7,5},{8,10},{9,11},{10,... | collective-permute-start | bytes 393224 | tf_op jit(solution)/shard_map/ppermute | solution.py:90
  62.6 5.2 %cached.3 = (bf16[384,2048]{1,0:T(8,128)(2,1)S(1)}, f32[384,128]{1,0:T(8,128)S(1)}) custom-call(s32[64,128]{1,0:T(8,128)S(1)} %copy.25.refs_2_.len_ref, bf16[512,2048]{1,0:T(8,128)(2,1)S(1)} %copy-done.1, bf16[512,16,512]{2,1,0:T(8,128)(2,1)} %kv_ref.3, f32[128,128]{1,0:T(8,128)S(1)} %get-tuple-element.35.refs_1_.refs_0_, ...), custom_call_target="tpu_custom_call" | custom-call | flops 1 | bytes 1 | tf_op jit(solution)/shard_map/cached/pallas_call | solution.py:391
  67.9 1.1 %collective-permute-done.5.refs_6_ = bf16[2,256,512]{2,1,0:T(8,128)(2,1)} collective-permute-done((bf16[2,256,512]{2,1,0:T(8,128)(2,1)}, bf16[2,256,512]{2,1,0:T(8,128)(2,1)}, u32[]{:S(2)}, u32[]{:S(2)}) %collective-permute-start.5) | collective-permute-done | bytes 524320 | tf_op jit(solution)/shard_map/ppermute | solution.py:90
  69.0 2.8 %gather_up.1 = (f32[512,512]{1,0:T(8,128)S(1)}, bf16[8,256,512]{2,1,0:T(8,128)(2,1)S(1)}) custom-call(s32[3]{0:T(128)S(1)} %broadcast_1_flags_ref.2.flags_ref, bf16[512,512]{1,0:T(8,128)(2,1)S(1)} %copy-done.2, bf16[512,512]{1,0:T(8,128)(2,1)} %collective-permute-done.refs_1_, bf16[512,512]{1,0:T(8,128)(2,1)} %collective-permute-done.2.refs_2_, ...), custom_call_target="tpu_custom_call" | custom-call | flops 1 | bytes 1 | tf_op jit(solution)/shard_map/gather_up/pallas_call | solution.py:426
  71.8 5.0 %finish.1 = (bf16[512,512]{1,0:T(8,128)(2,1)}, bf16[512,2048]{1,0:T(8,128)(2,1)}) custom-call(s32[8]{0:T(128)S(1)} %stack.75.ids_ref, s32[512,1]{1,0:T(8,128)S(1)} %copy.26.variant_ref.refs_1_, bf16[512,2048]{1,0:T(8,128)(2,1)S(1)} %copy-done.1, f32[512,512]{1,0:T(8,128)S(1)} %get-tuple-element.38.base_ref, ...), custom_call_target="tpu_custom_call" | custom-call | flops 1 | bytes 1 | tf_op jit(solution)/shard_map/finish/pallas_call | solution.py:521
  (48 shorter events, 1.2 us)
Async XLA Ops:
  0.6 5.2 %copy-start = (bf16[512,2048]{1,0:T(8,128)(2,1)S(1)}, bf16[512,2048]{1,0:T(8,128)(2,1)}, u32[]{:S(2)}) copy-start(bf16[512,2048]{1,0:T(8,128)(2,1)} %refs_0_.5) | copy-start | bytes 6291460
  0.6 30.7 %collective-permute-start.6 = (bf16[512,2048]{1,0:T(8,128)(2,1)}, bf16[512,2048]{1,0:T(8,128)(2,1)}, u32[]{:S(2)}, u32[]{:S(2)}) collective-permute-start(bf16[512,2048]{1,0:T(8,128)(2,1)} %refs_0_.5), channel_id=1, source_target_pairs={{0,4},{4,0},{8,12},{12,8},{1,5},{5,1},{9,13},{13,9},{2,6},{6,2},{1... | collective-permute-start | bytes 6291464 | tf_op jit(solution)/shard_map/ppermute | solution.py:90
  3.1 16.8 %collective-permute-start.8 = (bf16[1,2048,128]{2,1,0:T(8,128)(2,1)}, bf16[1,2048,128]{2,1,0:T(8,128)(2,1)S(1)}, u32[]{:S(2)}, u32[]{:S(2)}) collective-permute-start(bf16[1,2048,128]{2,1,0:T(8,128)(2,1)} %cut.1.refs_1_), channel_id=1, source_target_pairs={{0,8},{4,12},{8,0},{12,4},{1,9},{5,13},{9,1},{13,5},{2,10},{6,14},... | collective-permute-start | bytes 1572872 | tf_op jit(solution)/shard_map/ppermute | solution.py:90
  5.8 6.5 %copy-start.6 = (s32[512,1]{0,1:T(1,128)S(1)}, s32[512,1]{0,1:T(1,128)}, u32[]{:S(2)}) copy-start(s32[512,1]{0,1:T(1,128)} %param.12) | copy-start | bytes 6148
  10.1 30.8 %collective-permute-start.9 = (bf16[2,2048,128]{2,1,0:T(8,128)(2,1)}, bf16[2,2048,128]{2,1,0:T(8,128)(2,1)}, u32[]{:S(2)}, u32[]{:S(2)}) collective-permute-start(bf16[2,2048,128]{2,1,0:T(8,128)(2,1)} %get-tuple-element.31), channel_id=1, source_target_pairs={{0,8},{4,12},{8,0},{12,4},{1,9},{5,13},{9,1},{13,5},{2,10},{6,14},... | collective-permute-start | bytes 3145736 | tf_op jit(solution)/shard_map/ppermute | solution.py:90
  10.2 14.3 %collective-permute-start.1 = (bf16[512,512]{1,0:T(8,128)(2,1)}, bf16[512,512]{1,0:T(8,128)(2,1)}, u32[]{:S(2)}, u32[]{:S(2)}) collective-permute-start(bf16[512,512]{1,0:T(8,128)(2,1)} %get-tuple-element.26), channel_id=1, source_target_pairs={{0,1},{1,0},{2,3},{3,2},{4,5},{5,4},{6,7},{7,6},{8,9},{9,8},{10,11... | collective-permute-start | bytes 1572872 | tf_op jit(solution)/shard_map/ppermute | solution.py:90
  12.4 15.9 %collective-permute-start.7 = (s32[512,1]{1,0:T(8,128)S(1)}, s32[512,1]{1,0:T(8,128)S(1)}, u32[]{:S(2)}, u32[]{:S(2)}) collective-permute-start(s32[512,1]{1,0:T(8,128)S(1)} %copy.26.variant_ref.refs_1_), channel_id=1, source_target_pairs={{0,4},{4,0},{8,12},{12,8},{1,5},{5,1},{9,13},{13,9},{2,6},{6,2},{1... | collective-permute-start | bytes 6152 | tf_op jit(solution)/shard_map/ppermute | solution.py:90
  19.1 0.8 %copy-start.5 = (bf16[512,512]{1,0:T(8,128)(2,1)}, bf16[512,512]{1,0:T(8,128)(2,1)S(1)}, u32[]{:S(2)}) copy-start(bf16[512,512]{1,0:T(8,128)(2,1)S(1)} %get-tuple-element.25) | copy-start | bytes 1572868
  19.9 11.1 %copy-start.7 = (s32[512]{0:T(512)S(1)}, s32[512]{0:T(512)}, u32[]{:S(2)}) copy-start(s32[512]{0:T(512)} %param.11) | copy-start | bytes 6148
  19.9 15.9 %collective-permute-start.10 = (bf16[1,2048,128]{2,1,0:T(8,128)(2,1)S(1)}, bf16[1,2048,128]{2,1,0:T(8,128)(2,1)}, u32[]{:S(2)}, u32[]{:S(2)}) collective-permute-start(bf16[1,2048,128]{2,1,0:T(8,128)(2,1)S(1)} %gate.3.refs_1_.refs_6_), channel_id=1, source_target_pairs={{0,16},{16,0},{1,17},{17,1},{2,18},{18,2},{3,19},{19,3},{4,20},{20... | collective-permute-start | bytes 1572872 | tf_op jit(solution)/shard_map/ppermute | solution.py:90
  24.5 22.4 %collective-permute-start = (bf16[512,512]{1,0:T(8,128)(2,1)}, bf16[512,512]{1,0:T(8,128)(2,1)}, u32[]{:S(2)}, u32[]{:S(2)}) collective-permute-start(bf16[512,512]{1,0:T(8,128)(2,1)} %get-tuple-element.24), channel_id=1, source_target_pairs={{0,1},{1,0},{2,3},{3,2},{4,5},{5,4},{6,7},{7,6},{8,9},{9,8},{10,11... | collective-permute-start | bytes 1572872 | tf_op jit(solution)/shard_map/ppermute | solution.py:90
  28.3 25.1 %collective-permute-start.2 = (bf16[512,512]{1,0:T(8,128)(2,1)}, bf16[512,512]{1,0:T(8,128)(2,1)}, u32[]{:S(2)}, u32[]{:S(2)}) collective-permute-start(bf16[512,512]{1,0:T(8,128)(2,1)} %add_convert_fusion), channel_id=1, source_target_pairs={{0,2},{1,3},{2,0},{3,1},{4,6},{5,7},{6,4},{7,5},{8,10},{9,11},{10,... | collective-permute-start | bytes 1572872 | tf_op jit(solution)/shard_map/ppermute | solution.py:90
  43.5 12.1 %copy-start.1 = (bf16[512,2048]{1,0:T(8,128)(2,1)S(1)}, bf16[512,2048]{1,0:T(8,128)(2,1)}, u32[]{:S(2)}) copy-start(bf16[512,2048]{1,0:T(8,128)(2,1)} %q_ref.5) | copy-start | bytes 6291460
  43.5 2.1 %collective-permute-start.11 = (bf16[512,128]{1,0:T(8,128)(2,1)S(1)}, bf16[512,128]{1,0:T(8,128)(2,1)S(1)}, u32[]{:S(2)}, u32[]{:S(2)}) collective-permute-start(bf16[512,128]{1,0:T(8,128)(2,1)S(1)} %get-tuple-element.34), channel_id=1, source_target_pairs={{0,4},{4,0},{8,12},{12,8},{1,5},{5,1},{9,13},{13,9},{2,6},{6,2},{1... | collective-permute-start | bytes 393224 | tf_op jit(solution)/shard_map/ppermute | solution.py:90
  43.6 24.3 %collective-permute-start.3 = (bf16[2,256,512]{2,1,0:T(8,128)(2,1)}, bf16[2,256,512]{2,1,0:T(8,128)(2,1)}, u32[]{:S(2)}, u32[]{:S(2)}) collective-permute-start(bf16[2,256,512]{2,1,0:T(8,128)(2,1)} %refs_3_.1), channel_id=1, source_target_pairs={{0,8},{4,12},{8,0},{12,4},{1,9},{5,13},{9,1},{13,5},{2,10},{6,14},... | collective-permute-start | bytes 1572872 | tf_op jit(solution)/shard_map/ppermute | solution.py:90
  45.4 22.5 %collective-permute-start.4 = (bf16[2,256,512]{2,1,0:T(8,128)(2,1)}, bf16[2,256,512]{2,1,0:T(8,128)(2,1)}, u32[]{:S(2)}, u32[]{:S(2)}) collective-permute-start(bf16[2,256,512]{2,1,0:T(8,128)(2,1)} %refs_3_.1), channel_id=1, source_target_pairs={{0,4},{4,0},{8,12},{12,8},{1,5},{5,1},{9,13},{13,9},{2,6},{6,2},{1... | collective-permute-start | bytes 1572872 | tf_op jit(solution)/shard_map/ppermute | solution.py:90
  45.5 7.9 %collective-permute-start.12 = (bf16[512,128]{1,0:T(8,128)(2,1)S(1)}, bf16[512,128]{1,0:T(8,128)(2,1)S(1)}, u32[]{:S(2)}, u32[]{:S(2)}) collective-permute-start(bf16[512,128]{1,0:T(8,128)(2,1)S(1)} %get-tuple-element.32.refs_7_), channel_id=1, source_target_pairs={{0,4},{4,0},{8,12},{12,8},{1,5},{5,1},{9,13},{13,9},{2,6},{6,2},{1... | collective-permute-start | bytes 393224 | tf_op jit(solution)/shard_map/ppermute | solution.py:90
  46.8 22.2 %collective-permute-start.5 = (bf16[2,256,512]{2,1,0:T(8,128)(2,1)}, bf16[2,256,512]{2,1,0:T(8,128)(2,1)}, u32[]{:S(2)}, u32[]{:S(2)}) collective-permute-start(bf16[2,256,512]{2,1,0:T(8,128)(2,1)} %refs_3_.1), channel_id=1, source_target_pairs={{0,12},{4,8},{8,4},{12,0},{1,13},{5,9},{9,5},{13,1},{2,14},{6,10},... | collective-permute-start | bytes 1572872 | tf_op jit(solution)/shard_map/ppermute | solution.py:90
  53.4 5.0 %collective-permute-start.14 = (bf16[512,128]{1,0:T(8,128)(2,1)S(1)}, bf16[512,128]{1,0:T(8,128)(2,1)S(1)}, u32[]{:S(2)}, u32[]{:S(2)}) collective-permute-start(bf16[512,128]{1,0:T(8,128)(2,1)S(1)} %gate.4.refs_0_), channel_id=1, source_target_pairs={{0,1},{1,0},{2,3},{3,2},{4,5},{5,4},{6,7},{7,6},{8,9},{9,8},{10,11... | collective-permute-start | bytes 393224 | tf_op jit(solution)/shard_map/ppermute | solution.py:90
  53.4 7.3 %collective-permute-start.13 = (bf16[512,128]{1,0:T(8,128)(2,1)S(1)}, bf16[512,128]{1,0:T(8,128)(2,1)S(1)}, u32[]{:S(2)}, u32[]{:S(2)}) collective-permute-start(bf16[512,128]{1,0:T(8,128)(2,1)S(1)} %add_convert_fusion.3), channel_id=1, source_target_pairs={{0,1},{1,0},{2,3},{3,2},{4,5},{5,4},{6,7},{7,6},{8,9},{9,8},{10,11... | collective-permute-start | bytes 393224 | tf_op jit(solution)/shard_map/ppermute | solution.py:90
  58.1 2.7 %copy-start.3 = (bf16[128,2048]{1,0:T(8,128)(2,1)}, bf16[128,2048]{1,0:T(8,128)(2,1)S(1)}, u32[]{:S(2)}) copy-start(bf16[128,2048]{1,0:T(8,128)(2,1)S(1)} %get-tuple-element.40.refs_0_) | copy-start | bytes 1572868
  58.4 13.3 %collective-permute-start.16 = (bf16[512,128]{1,0:T(8,128)(2,1)S(1)}, bf16[512,128]{1,0:T(8,128)(2,1)S(1)}, u32[]{:S(2)}, u32[]{:S(2)}) collective-permute-start(bf16[512,128]{1,0:T(8,128)(2,1)S(1)} %gate.5.refs_2_.refs_8_.refs_6_), channel_id=1, source_target_pairs={{0,2},{1,3},{2,0},{3,1},{4,6},{5,7},{6,4},{7,5},{8,10},{9,11},{10,... | collective-permute-start | bytes 393224 | tf_op jit(solution)/shard_map/ppermute | solution.py:90
  60.8 11.0 %collective-permute-start.15 = (bf16[512,128]{1,0:T(8,128)(2,1)S(1)}, bf16[512,128]{1,0:T(8,128)(2,1)S(1)}, u32[]{:S(2)}, u32[]{:S(2)}) collective-permute-start(bf16[512,128]{1,0:T(8,128)(2,1)S(1)} %add_convert_fusion.2.refs_1_.refs_4_), channel_id=1, source_target_pairs={{0,2},{1,3},{2,0},{3,1},{4,6},{5,7},{6,4},{7,5},{8,10},{9,11},{10,... | collective-permute-start | bytes 393224 | tf_op jit(solution)/shard_map/ppermute | solution.py:90
  62.6 6.4 %copy-start.2 = (bf16[512,512]{1,0:T(8,128)(2,1)S(1)}, bf16[512,512]{1,0:T(8,128)(2,1)}, u32[]{:S(2)}) copy-start(bf16[512,512]{1,0:T(8,128)(2,1)} %get-tuple-element.23.refs_0_) | copy-start | bytes 1572868
  67.8 3.9 %copy-start.4 = (bf16[128,2048]{1,0:T(8,128)(2,1)S(1)}, bf16[128,2048]{1,0:T(8,128)(2,1)}, u32[]{:S(2)}) copy-start(bf16[128,2048]{1,0:T(8,128)(2,1)} %copy-done.3) | copy-start | bytes 1572868
